TPU v7x, 32 devices: a whole 2x2x4 slice. The times are simulated.
32 devices in a mesh: ship: 8 (over z, y), boot: 4 (over x, core).
Axes of the slice: x: 2, y: 2, z: 4, core: 2. Of those that a mesh axis runs over, the one named last changes fastest.
Arguments:
- fitted: float32 [131072], P('ship'), may hold values from -6 to 6
- resid: float32 [131072], P('ship'), may hold values from -32 to 32
- row_weight: float32 [131072], P('ship'), may hold values from 0.5 to 2
- lane_block: int32 [131072, 1], P('ship'), may hold values from 0 to 7; in each aligned block of 16384 rows (0 to 16383, 16384 to 32767, ...) at most 4096 rows name the same one
- lane_within: int32 [131072], P('ship'), may hold values from 0 to 2047
- week_id: int32 [131072], P('ship'), may hold values from 0 to 259
- supplier_runs: int32 [8, 128], P('ship'), may hold values from 1 to 512, 16384 in all within a row
- signs: int32 [128, 1024], P('boot', 'ship'), may hold values from 0 to 1
- supplier_scale: float32 [1024], P('ship'), may hold values from 0.17677669 to 0.70710677
- lane_scale: float32 [16384], P('ship'), may hold values from 0.70710677 to 2.828427
- week_scale: float32 [260], replicated, may hold values from 0.089076206 to 0.35630482
Outputs:
- v_supplier: float32 [128, 1024], P('boot', 'ship')
- v_lane: float32 [128, 16384], P('boot', 'ship')
- v_week: float32 [128, 260], P('boot')
- u_next: float32 [128, 131072], P('boot', 'ship')
- step_size: float32 [128], P('boot')
- spread_supplier: float32 [1024], P('ship')
- spread_lane: float32 [16384], P('ship')
Inputs may be any that keep to these rules, and one draw needn't show every extreme that they name: `lane_block`: among the 16384 shipments of one device at most 4096 have the same lane block, and in every draw some device has exactly 4096 in some block. `supplier_runs`: each row sums to 16384; in every row one supplier has exactly the largest count.
All inputs are finite; a program needn't handle non-finite values.
Results may differ from a plain program's by a relative error of at most 0.00011.
Values sent between devices are 32-bit elements; how exact they have to be, the bound alone decides.
No kernel may reach another device: no remote copies, remote signals or barrier semaphores. Data moves between devices by JAX's collectives and lax.ppermute only.
A program may use at most 64 MiB of HBM per device.

v0:
```python
import jax
import jax.numpy as jnp
from jax import lax
from jax.sharding import PartitionSpec as P

EPS = 1e-06


def product(left, right):
    return jnp.dot(left, right, precision=lax.Precision.HIGHEST, preferred_element_type=jnp.float32)


def product_rows(left, hot):
    return lax.dot_general(
        left,
        hot,
        (((1,), (1,)), ((), ())),
        precision=lax.Precision.HIGHEST,
        preferred_element_type=jnp.float32,
    )


def on_device(
    fitted,
    resid,
    row_weight,
    lane_block,
    lane_within,
    week_id,
    supplier_runs,
    signs,
    supplier_scale,
    lane_scale,
    week_scale,
):
    rows = fitted.shape[0]
    columns = signs.shape[0]
    n_ship = lax.axis_size("ship")
    lane_own = lane_scale.shape[0]
    weeks = week_scale.shape[0]
    supplier_own = supplier_scale.shape[0]
    shipments_all = rows * n_ship
    effects_all = supplier_own * n_ship + lane_own * n_ship + weeks
    ratio = effects_all / shipments_all
    position = jnp.arange(rows, dtype=jnp.int32)
    run_end = jnp.cumsum(supplier_runs[0])
    run_start = run_end - supplier_runs[0]
    supplier_hot = (
        (position[:, None] >= run_start[None, :]) & (position[:, None] < run_end[None, :])
    ).astype(jnp.float32)
    week_hot = (week_id[:, None] == jnp.arange(weeks, dtype=jnp.int32)[None, :]).astype(jnp.float32)
    sign_value = (2 * signs - 1).astype(jnp.float32)
    rhs = fitted[None, :] + product_rows(sign_value, supplier_hot) * resid[None, :]
    square_sum = jnp.sum(rhs * rhs, axis=1)
    owner = lane_block[:, 0]
    lane_index = owner * lane_own + lane_within
    total_square = lax.psum(square_sum, "ship")
    beta_first = jnp.sqrt(total_square / shipments_all + EPS)
    basis = rhs / beta_first[:, None]
    weighted = basis * row_weight[None, :]
    week_part = lax.psum(product(weighted, week_hot), "ship")
    supplier_part = product(weighted, supplier_hot)
    dense = jax.ops.segment_sum(weighted.T, lane_index, lane_own * n_ship).T
    lane_part = lax.psum_scatter(dense, "ship", scatter_dimension=1, tiled=True)
    p_supplier = ratio * supplier_scale[None, :] * supplier_part
    p_lane = ratio * lane_scale[None, :] * lane_part
    p_week = ratio * week_scale[None, :] * week_part
    own_square = jnp.sum(p_supplier * p_supplier, axis=1) + jnp.sum(p_lane * p_lane, axis=1)
    week_square = jnp.sum(p_week * p_week, axis=1)
    effect_square = lax.psum(own_square, "ship")
    alpha = jnp.sqrt((effect_square + week_square) / effects_all + EPS)
    v_supplier = p_supplier / alpha[:, None]
    v_lane = p_lane / alpha[:, None]
    v_week = p_week / alpha[:, None]
    forward = product(v_supplier * supplier_scale[None, :], supplier_hot.T)
    table = lax.all_gather(v_lane * lane_scale[None, :], "ship", axis=1, tiled=True)
    forward = forward + table[:, lane_index]
    forward = forward + product(v_week * week_scale[None, :], week_hot.T)
    residual = row_weight[None, :] * forward - alpha[:, None] * basis
    residual_square = lax.psum(jnp.sum(residual * residual, axis=1), "ship")
    beta_next = jnp.sqrt(residual_square / shipments_all + EPS)
    u_next = residual / beta_next[:, None]
    step_size = alpha * beta_first / (alpha * alpha + beta_next * beta_next)
    x_supplier = step_size[:, None] * v_supplier
    x_lane = step_size[:, None] * v_lane
    supplier_total, lane_total = lax.psum(
        (jnp.sum(x_supplier * x_supplier, axis=0), jnp.sum(x_lane * x_lane, axis=0)), "boot"
    )
    columns_all = columns * lax.axis_size("boot")
    spread_supplier = jnp.sqrt(supplier_total / columns_all + EPS)
    spread_lane = jnp.sqrt(lane_total / columns_all + EPS)
    return (v_supplier, v_lane, v_week, u_next, step_size, spread_supplier, spread_lane)


def solution(mesh):
    return jax.shard_map(
        on_device,
        mesh=mesh,
        in_specs=(
            P("ship"),
            P("ship"),
            P("ship"),
            P("ship", None),
            P("ship"),
            P("ship"),
            P("ship", None),
            P("boot", "ship"),
            P("ship"),
            P("ship"),
            P(),
        ),
        out_specs=(
            P("boot", "ship"),
            P("boot", "ship"),
            P("boot", None),
            P("boot", "ship"),
            P("boot"),
            P("ship"),
            P("ship"),
        ),
        check_vma=False,
    )
```

profile of v0, /device:TPU:0, one launch (start us, length us, event | category | flops | bytes accessed | tf_op | source)
XLA Modules:
  0.0 555.4 jit_solution(1613656349951330191)
XLA Ops:
  7.2 0.8 copy.26
  8.3 0.7 fusion.38
  8.9 7.4 %multiply_reduce_fusion.1 = (f32[32]{0:T(128)S(1)}, f32[32,16384]{1,0:T(8,128)}) fusion(f32[16384]{0:T(1024)} %param.12, s32[128]{0:T(128)S(1)} %reduce, s32[128]{0:T(128)S(1)} %fusion.38, s32[32,128]{1,0:T(8,128)} %param.18, f32[16384]{0:T(1024)} %param.11), kind=kOutput, calls=%fused_computation.25 | convolution fusion | flops 813707264 | bytes 2245760 | tf_op jit(solution)/shard_map/dot_general | solution.py:14
  16.3 23.1 %psum.42 = f32[32]{0:T(128)S(1)} all-reduce(f32[32]{0:T(128)S(1)} %get-tuple-element.38), channel_id=1, replica_groups=mesh['ship'=8,'boot'=4] {'ship'}, use_global_device_ids=true, to_apply=%region_2.3 | all-reduce | flops 32 | bytes 256 | tf_op jit(solution)/shard_map/psum | solution.py:57
  39.5 1.8 multiply_bitcast_fusion
  41.3 4.7 copy.27
  46.1 91.3 %scatter_custom_fusion = f32[16384,32]{1,0:T(8,128)} fusion(s32[16384]{0:T(1024)S(1)} %get-tuple-element.33, f32[16384,32]{1,0:T(8,128)} %copy.27, f32[]{:T(128)} %constant.15.clone.1), kind=kCustom, calls=%fused_computation.16 | custom fusion | flops 524288 | bytes 2097664 | tf_op jit(solution)/shard_map/scatter-add | solution.py:63
  138.2 0.9 copy-done
  139.1 8.7 %fusion.3 = f32[32,260]{1,0:T(8,128)S(1)} fusion(s32[16384]{0:T(1024)S(1)} %copy-done.10, f32[16384]{0:T(1024)S(1)} %copy-done.2, f32[32,16384]{1,0:T(8,128)S(1)} %copy-done, f32[32]{0:T(128)S(1)} %add_sqrt_fusion.4), kind=kOutput, calls=%fused_computation.9 | convolution fusion | flops 1641086976 | bytes 2261632 | tf_op jit(solution)/shard_map/dot_general | solution.py:10
  147.9 3.9 multiply_reduce_fusion.6
  151.7 131.9 %reduce-scatter.2.cloned.1.call-done = f32[32,2048]{0,1:T(8,128)} async-done(((f32[32,16384]{0,1:T(8,128)}), f32[32,2048]{0,1:T(8,128)}) %reduce-scatter.2.cloned.1.call-update) | async-done | bytes 262160 | tf_op jit(solution)/shard_map/reduce_scatter | solution.py:64
  283.7 1.6 multiply_reduce_fusion.3
  285.3 35.7 %all-reduce = (f32[32]{0:T(128)S(1)}, f32[32,260]{1,0:T(8,128)S(1)}) all-reduce(f32[32]{0:T(128)S(1)} %add.76, f32[32,260]{1,0:T(8,128)S(1)} %fusion.3), channel_id=1, replica_groups=mesh['ship'=8,'boot'=4] {'ship'}, use_global_device_ids=true, to_apply=%region_7.8 | all-reduce | flops 8352 | bytes 66816 | tf_op jit(solution)/shard_map/psum | solution.py:70
  321.1 2.5 broadcast_multiply_fusion
  323.6 1.0 copy.29
  324.8 121.1 %all-gather.2.cloned.1.call-done = f32[32,16384]{0,1:T(8,128)} async-done(((f32[32,2048]{0,1:T(8,128)}), f32[32,16384]{0,1:T(8,128)}) %all-gather.2.cloned.1.call-update) | async-done | bytes 2097168 | tf_op jit(solution)/shard_map/all_gather | solution.py:76
  445.9 57.8 %gather_fusion = f32[16384,32]{1,0:T(8,128)} fusion(f32[32,16384]{0,1:T(8,128)} %all-gather.2.cloned.1.call-done, s32[16384]{0:T(1024)S(1)} %get-tuple-element.32), kind=kCustom, calls=%fused_computation | custom fusion | bytes 4259840 | tf_op jit(solution)/shard_map/gather | solution.py:77
  503.7 5.1 copy.28
  508.8 5.0 convolution_add_fusion.1
  513.9 7.1 %multiply_reduce_fusion = (f32[32]{0:T(128)S(1)}, f32[32,16384]{1,0:T(8,128)S(1)}) fusion(f32[32,16384]{1,0:T(8,128)S(1)} %copy-done.1, f32[32]{0:T(128)S(1)} %add_sqrt_fusion.4, f32[32]{0:T(128)S(1)} %add_sqrt_fusion.3, f32[32,16384]{1,0:T(8,128)S(1)} %convolution_add_fusion.1, s32[16384]{0:T(1024)S(1)} %copy-done.10, ...), kind=kOutput, calls=%fused_computation.24 | convolution fusion | flops 1643716736 | bytes 6457232 | tf_op jit(solution)/shard_map/dot_general | solution.py:10
  521.1 18.4 %psum.45 = f32[32]{0:T(128)S(1)} all-reduce(f32[32]{0:T(128)S(1)} %get-tuple-element.42), channel_id=1, replica_groups=mesh['ship'=8,'boot'=4] {'ship'}, use_global_device_ids=true, to_apply=%region_11.12 | all-reduce | flops 32 | bytes 256 | tf_op jit(solution)/shard_map/psum | solution.py:80
  540.0 5.9 %all-reduce.1 = (f32[128]{0:T(128)S(1)}, f32[2048]{0:T(1024)S(1)}) all-reduce(f32[128]{0:T(128)S(1)} %multiply_reduce_fusion.5, f32[2048]{0:T(1024)S(1)} %multiply_reduce_fusion.2), channel_id=1, replica_groups=mesh['ship'=8,'boot'=4] {'boot'}, use_global_device_ids=true, to_apply=%region_13.14 | all-reduce | flops 2176 | bytes 17408 | tf_op jit(solution)/shard_map/psum | solution.py:86
  545.9 0.6 add_sqrt_fusion
  547.0 1.5 broadcast_divide_fusion
  (44 shorter events, 2.4 us)
Async XLA Ops:
  7.2 276.5 %reduce-scatter.2.cloned.1.call-start = ((), (), s32[]{:S(2)}) async-start(), calls=%async_computation.1 | async-start | bytes 9437184 | tf_op jit(solution)/shard_map/reduce_scatter | solution.py:64
  8.9 30.5 %copy-start.2 = (f32[16384]{0:T(1024)S(1)}, f32[16384]{0:T(1024)}, u32[]{:S(2)}) copy-start(f32[16384]{0:T(1024)} %param.13) | copy-start | bytes 196612
  41.3 4.7 copy-start.3
  41.3 4.8 copy-start.4
  137.5 0.7 copy-start.11
  137.5 0.7 copy-start.9
  137.5 0.7 copy-start.6
  137.5 1.6 copy-start
  137.5 1.6 copy-start.10
  137.5 308.4 %all-gather.2.cloned.1.call-start = ((), (), s32[]{:S(2)}) async-start(), calls=%async_computation.2 | async-start | bytes 9437184 | tf_op jit(solution)/shard_map/all_gather | solution.py:76
  324.7 184.1 %copy-start.7 = (f32[32,128]{1,0:T(8,128)}, f32[32,128]{1,0:T(8,128)S(1)}, u32[]{:S(2)}) copy-start(f32[32,128]{1,0:T(8,128)S(1)} %broadcast_divide_fusion.2) | copy-start | bytes 49156
  324.8 189.1 %copy-start.5 = (f32[32,260]{1,0:T(8,128)}, f32[32,260]{1,0:T(8,128)S(1)}, u32[]{:S(2)}) copy-start(f32[32,260]{1,0:T(8,128)S(1)} %multiply_divide_fusion.1) | copy-start | bytes 99844
  508.8 5.1 copy-start.1
  539.5 9.0 %copy-start.8 = (f32[32]{0:T(128)}, f32[32]{0:T(128)S(1)}, u32[]{:S(2)}) copy-start(f32[32]{0:T(128)S(1)} %get-tuple-element.36) | copy-start | bytes 388
Sparse Core Ops, SparseCore 0:
  137.6 146.0 reduce-scatter.1
  323.7 122.1 all-gather.1
where the time goes:
time: 556 us; the launch traced here: 555 us
  waiting for transfers between devices  253 us (46%)
  other arithmetic  102 us (18%)
  blocking collectives  83.1 us (15%)
  local copies, waits for them, and re-layouts  70.7 us (13%)
  matrix products  32.2 us (6%)
  between operations  14.2 us (3%)
    reduce_scatter x1, waiting for transfers between devices, on_device(): lane_part = lax.psum_scatter(dense, 'ship', scatter_dimension=1, tiled=True)  132 us
    all_gather x1, waiting for transfers between devices, on_device(): lax.all_gather(v_lane * lane_scale[None, :], 'ship', axis=1, tiled=True)  121 us
    scatter-add x1, other arithmetic, on_device(): dense = jax.ops.segment_sum(weighted.T, lane_index, lane_own * n_ship).T  91.3 us
    gather x2, local copies, waits for them, and re-layouts, on_device(): forward = forward + table[:, lane_index]  62.9 us
    psum x1, blocking collectives, on_device(): effect_square = lax.psum(own_square, 'ship')  35.7 us
    dot_general x4, matrix products, product(): jnp.dot(left, right, precision=lax.Precision.HIGHEST, preferred_element_t...  24.8 us
    psum x1, blocking collectives, on_device(): total_square = lax.psum(square_sum, 'ship')  23.1 us
    psum x1, blocking collectives, on_device(): residual_square = lax.psum(jnp.sum(residual * residual, axis=1), 'ship')  18.4 us
  transfers between devices with their start and end apart: 2, of which 2 were waited for; matrix products, arithmetic and copies ran while one was open for 2% of the time, Pallas kernels for 0%

commit v1 on v0

v1 whole, which is shorter than its diff:
```python
import functools

import jax
import jax.numpy as jnp
from jax import lax
from jax.experimental import pallas as pl
from jax.experimental.pallas import tpu as pltpu
from jax.sharding import PartitionSpec as P

EPS = 1e-06
BLOCK = 256
SLOTS = 7
LANES_WIDE = 128
VMEM = pl.BlockSpec(memory_space=pltpu.VMEM)
SMEM = pl.BlockSpec(memory_space=pltpu.SMEM)
PARAMS = pltpu.CompilerParams(vmem_limit_bytes=40 << 20)


def split(value):
    high = value.astype(jnp.bfloat16)
    low = (value - high.astype(jnp.float32)).astype(jnp.bfloat16)
    return high, low


def product(left, right):
    return jnp.dot(left, right, precision=lax.Precision.HIGHEST, preferred_element_type=jnp.float32)


def product_rows(left, hot):
    return lax.dot_general(
        left,
        hot,
        (((1,), (1,)), ((), ())),
        precision=lax.Precision.HIGHEST,
        preferred_element_type=jnp.float32,
    )


def swap(value, axis, step):
    size = lax.axis_size(axis)
    return lax.ppermute(value, axis, [(i, i ^ step) for i in range(size)])


def sum_over(value, axis):
    step = 1
    while step < lax.axis_size(axis):
        value = value + swap(value, axis, step)
        step *= 2
    return value


def lane_sums_kernel(low_n, turn_n, with_prev, meta, planes, signs, *refs):
    if with_prev:
        prev, outs, acc, acc_fit = refs[:turn_n], refs[turn_n : 2 * turn_n], refs[-2], refs[-1]
    else:
        prev, outs, acc, acc_fit = None, refs[:turn_n], refs[-2], refs[-1]
    suppliers = signs.shape[1]
    columns = outs[0].shape[0]
    own = outs[0].shape[1]
    rows = (planes.shape[0] - 8) // 3
    blocks = rows * 128 // BLOCK
    offset, turn = meta[2, 0], meta[2, 1]
    shift = low_n.bit_length() - 1
    acc[...] = jnp.zeros_like(acc)
    acc_fit[...] = jnp.zeros_like(acc_fit)
    high_at = lax.broadcasted_iota(jnp.int32, (8, BLOCK), 0)
    place = lax.broadcasted_iota(jnp.int32, (8, BLOCK), 1)
    low_at = lax.broadcasted_iota(jnp.int32, (low_n, BLOCK), 0)

    def two_rows(start):
        pair = [planes[pl.ds(start + u, 1), :] for u in range(BLOCK // 128)]
        return jnp.concatenate(pair, axis=1)

    def prepare(block):
        row = block * (BLOCK // 128)
        local = two_rows(row).astype(jnp.int32) - offset
        high, low = local >> shift, local & (low_n - 1)
        match = jnp.broadcast_to(high, (8, BLOCK)) == high_at
        fit = jnp.where(match, jnp.broadcast_to(two_rows(rows + row), (8, BLOCK)), 0.0)
        res = jnp.where(match, jnp.broadcast_to(two_rows(2 * rows + row), (8, BLOCK)), 0.0)
        hot = jnp.where(jnp.broadcast_to(low, (low_n, BLOCK)) == low_at, 1.0, 0.0).astype(jnp.bfloat16)
        return fit, res, hot

    def group(first, block, fit, res, hot):
        at = place + block * BLOCK
        parts = []
        for u in range(SLOTS):
            inside = (at >= meta[0, first + u]) & (at < meta[0, first + u + 1])
            parts.append(jnp.where(inside, res, 0.0))
        left = jnp.concatenate(parts + [fit], axis=0)
        both = lax.dot_general(
            jnp.concatenate(split(left), axis=0),
            hot,
            (((1,), (1,)), ((), ())),
            preferred_element_type=jnp.float32,
        )
        return both[: 8 * SLOTS + 8] + both[8 * SLOTS + 8 :]

    def add(first, sums):
        at = pl.ds(pl.multiple_of(first * 8, 8), 8 * SLOTS)
        for u in range(low_n // 128):
            acc[u, at, :] = acc[u, at, :] + sums[: 8 * SLOTS, u * 128 : (u + 1) * 128]

    unroll = 4

    @pl.loop(0, blocks // unroll)
    def _(step):
        ready = [prepare(step * unroll + u) for u in range(unroll)]
        firsts = [meta[1, step * unroll + u] for u in range(unroll)]
        sums = [group(firsts[u], step * unroll + u, *ready[u]) for u in range(unroll)]
        for u in range(unroll):
            add(firsts[u], sums[u])
        acc_fit[...] = acc_fit[...] + sum(one[8 * SLOTS :] for one in sums)
        for u in range(unroll):
            block = step * unroll + u
            more = (meta[1, block + 1] - firsts[u]) // SLOTS

            @pl.loop(0, more)
            def _(turn_at):
                first = firsts[u] + (turn_at + 1) * SLOTS
                fit, res, hot = prepare(block)
                add(first, group(first, block, fit, res, hot))

    for part in range(turn_n):
        here = pl.multiple_of((turn ^ part) * columns, columns)
        sign = (2 * signs[pl.ds(here, columns), :] - 1).astype(jnp.float32).astype(jnp.bfloat16)
        left = jnp.concatenate([sign, sign], axis=1)
        for high in range(-(-own // low_n)):
            rows_at = pl.ds(high, suppliers, stride=8)
            wide = jnp.concatenate([acc[u, rows_at, :] for u in range(low_n // 128)], axis=1)
            right = jnp.concatenate(split(wide), axis=0)
            total = jnp.dot(left, right, preferred_element_type=jnp.float32)
            total = total + jnp.broadcast_to(acc_fit[high : high + 1, :], total.shape)
            at = slice(high * low_n, (high + 1) * low_n)
            if with_prev:
                total = total + prev[part][:, at]
            outs[part][:, at] = total


def lane_sums(meta, planes, signs, prev, columns, own, turn_n):
    low_n = max(own // 8, 128)
    suppliers = signs.shape[1]
    shape = jax.ShapeDtypeStruct((columns, own), jnp.float32)
    return pl.pallas_call(
        functools.partial(lane_sums_kernel, low_n, turn_n, bool(prev)),
        out_shape=[shape] * turn_n,
        in_specs=[SMEM, VMEM, VMEM] + [VMEM] * len(prev),
        out_specs=[VMEM] * turn_n,
        scratch_shapes=[
            pltpu.VMEM((low_n // 128, (suppliers + SLOTS + 1) * 8, 128), jnp.float32),
            pltpu.VMEM((8, low_n), jnp.float32),
        ],
        compiler_params=PARAMS,
        name="lane_sums",
    )(meta, planes, signs, *prev)


def table_kernel(ratio, scale, *refs):
    parts, entries, table, squares = refs[:-3], refs[-3], refs[-2], refs[-1]
    total = parts[0][...]
    for part in parts[1:]:
        total = total + part[...]
    by = jnp.broadcast_to(scale[...], total.shape)
    entry = ratio * by * total
    entries[...] = entry
    squares[...] = jnp.sum(entry * entry, axis=1, keepdims=True)
    scaled = by * entry
    quarter = table.shape[0]
    count = total.shape[1] // quarter
    stacked = jnp.concatenate([scaled[:, u * quarter : (u + 1) * quarter] for u in range(count)], axis=0)
    table[...] = stacked.T


def lane_table(ratio, scale, parts):
    columns, own = parts[0].shape
    quarter = own * columns // LANES_WIDE
    return pl.pallas_call(
        functools.partial(table_kernel, ratio),
        out_shape=[
            jax.ShapeDtypeStruct((columns, own), jnp.float32),
            jax.ShapeDtypeStruct((quarter, LANES_WIDE), jnp.float32),
            jax.ShapeDtypeStruct((columns, 1), jnp.float32),
        ],
        in_specs=[VMEM] * (1 + len(parts)),
        out_specs=[VMEM] * 3,
        compiler_params=PARAMS,
        name="lane_table",
    )(scale, *parts)


def forward_kernel(index, lane_part, weight, inverse, base, *refs):
    tables, out, squares, table, first, second, total = refs[:-6], *refs[-6:]
    at = 0
    for piece in tables:
        table[at : at + piece.shape[0], :] = piece[...]
        at += piece.shape[0]
    groups = weight.shape[0]
    columns = out.shape[0]
    scale = jnp.broadcast_to(inverse[...], (columns, 128))
    total[...] = jnp.zeros_like(total)

    def gather(group, store):
        for u in range(128):
            store[u : u + 1, :] = table[pl.ds(index[group * 128 + u], 1), :]

    def finish(group, store):
        turned = store[...].T
        part = jnp.broadcast_to(lane_part[pl.ds(group, 1), :], (columns, 128))
        picked = turned[0:columns]
        for u in range(1, 128 // columns):
            picked = jnp.where(part == u, turned[u * columns : (u + 1) * columns], picked)
        at = pl.ds(pl.multiple_of(group * 128, 128), 128)
        by = jnp.broadcast_to(weight[pl.ds(group, 1), :], (columns, 128))
        value = base[:, at] + picked * by * scale
        out[:, at] = value
        total[...] = total[...] + value * value

    gather(0, first)

    @pl.loop(0, groups // 2)
    def _(step):
        gather(2 * step + 1, second)
        finish(2 * step, first)
        gather(jnp.minimum(2 * step + 2, groups - 1), first)
        finish(2 * step + 1, second)

    squares[...] = jnp.sum(total[...], axis=1, keepdims=True)


def forward_lanes(index, lane_part, weight, inverse, base, tables):
    columns, rows = base.shape
    lines = sum(piece.shape[0] for piece in tables)
    return pl.pallas_call(
        forward_kernel,
        out_shape=[
            jax.ShapeDtypeStruct((columns, rows), jnp.float32),
            jax.ShapeDtypeStruct((columns, 1), jnp.float32),
        ],
        in_specs=[SMEM] + [VMEM] * (4 + len(tables)),
        out_specs=[VMEM] * 2,
        scratch_shapes=[
            pltpu.VMEM((lines, LANES_WIDE), jnp.float32),
            pltpu.VMEM((128, LANES_WIDE), jnp.float32),
            pltpu.VMEM((128, LANES_WIDE), jnp.float32),
            pltpu.VMEM((columns, 128), jnp.float32),
        ],
        compiler_params=PARAMS,
        name="forward_lanes",
    )(index, lane_part, weight, inverse, base, *tables)


def gather_tables(table, n_ship):
    if n_ship > 16:
        return [lax.all_gather(table, "ship", axis=0, tiled=True)], False
    held = {0: table}
    for step in range(2, n_ship, 2):
        held[step] = swap(table, "ship", step)
    for step in range(0, n_ship, 2):
        held[step + 1] = swap(held[step], "ship", 1)
    return [held[step] for step in range(n_ship)], True


def on_device(
    fitted,
    resid,
    row_weight,
    lane_block,
    lane_within,
    week_id,
    supplier_runs,
    signs,
    supplier_scale,
    lane_scale,
    week_scale,
):
    rows = fitted.shape[0]
    columns = signs.shape[0]
    n_ship = lax.axis_size("ship")
    n_boot = lax.axis_size("boot")
    me_ship = lax.axis_index("ship")
    me_boot = lax.axis_index("boot")
    lane_own = lane_scale.shape[0]
    weeks = week_scale.shape[0]
    supplier_own = supplier_scale.shape[0]
    shipments_all = rows * n_ship
    effects_all = supplier_own * n_ship + lane_own * n_ship + weeks
    ratio = effects_all / shipments_all
    share = n_ship // n_boot

    owner = lane_block[:, 0]
    lane = owner * lane_own + lane_within
    runs = supplier_runs[0]
    before = jnp.arange(supplier_own)
    run_end = jnp.sum(jnp.where(before[None, :] <= before[:, None], runs[None, :], 0), axis=1)
    first_of = jnp.sum(
        (run_end[None, :] <= (jnp.arange(128, dtype=jnp.int32) * BLOCK)[:, None]).astype(jnp.int32), axis=1
    )
    square = (rows // 128, 128)
    planes = jnp.concatenate(
        [
            lane.astype(jnp.float32).reshape(square),
            (row_weight * fitted).reshape(square),
            (row_weight * resid).reshape(square),
            run_end.astype(jnp.float32)[None, :],
            first_of.astype(jnp.float32)[None, :],
            jnp.zeros((6, 128), jnp.float32),
        ],
        axis=0,
    )
    all_signs = lax.all_to_all(jnp.broadcast_to(signs[None], (n_boot,) + signs.shape), "boot", 0, 0)
    all_signs = all_signs.reshape(n_boot * columns, supplier_own)
    sums = []
    for turn in range(share):
        pairs = []
        for a in range(n_boot):
            for r in range(share):
                for b in range(n_boot):
                    pairs.append(((a * share + r) * n_boot + b, (b * share + (r + turn) % share) * n_boot + a))
        got = lax.ppermute(planes, ("ship", "boot"), pairs)
        got_signs = lax.ppermute(all_signs, ("ship", "boot"), pairs)
        start = got[3 * square[0]].astype(jnp.int32)
        firsts = got[3 * square[0] + 1].astype(jnp.int32)
        pad = supplier_own + 128
        start = jnp.concatenate([jnp.zeros((1,), jnp.int32), start, jnp.full((127,), rows, jnp.int32)])
        firsts = jnp.concatenate([firsts, jnp.zeros((pad - 128,), jnp.int32)])
        place = jnp.concatenate(
            [(me_ship * lane_own)[None], me_boot[None], jnp.zeros((pad - 2,), jnp.int32)]
        ).astype(jnp.int32)
        sums = lane_sums(jnp.stack([start, firsts, place]), got, got_signs, sums, columns, lane_own, n_boot)
    parts = [sums[0]] + [swap(sums[step], "boot", step) for step in range(1, n_boot)]
    entry, table, entry_square = lane_table(ratio, lane_scale[None, :], parts)
    tables, by_step = gather_tables(table, n_ship)

    position = jnp.arange(rows, dtype=jnp.int32)
    run_start = run_end - runs
    supplier_hot = (
        (position[:, None] >= run_start[None, :]) & (position[:, None] < run_end[None, :])
    ).astype(jnp.float32)
    week_hot = (week_id[:, None] == jnp.arange(weeks, dtype=jnp.int32)[None, :]).astype(jnp.float32)
    sign_value = (2 * signs - 1).astype(jnp.float32)
    rhs = fitted[None, :] + product_rows(sign_value, supplier_hot) * resid[None, :]
    square_sum = jnp.sum(rhs * rhs, axis=1)
    weighted = rhs * row_weight[None, :]
    week_part = product(weighted, week_hot)
    supplier_part = product(weighted, supplier_hot)
    early = sum_over(jnp.concatenate([week_part, square_sum[:, None]], axis=1), "ship")
    beta_first = jnp.sqrt(early[:, weeks] / shipments_all + EPS)
    by_beta = (1.0 / beta_first)[:, None]
    p_supplier = ratio * supplier_scale[None, :] * supplier_part * by_beta
    p_week = ratio * week_scale[None, :] * early[:, :weeks] * by_beta
    p_lane = entry * by_beta
    own_square = jnp.sum(p_supplier * p_supplier, axis=1) + entry_square[:, 0] * by_beta[:, 0] * by_beta[:, 0]
    week_square = jnp.sum(p_week * p_week, axis=1)
    effect_square = sum_over(own_square, "ship")
    alpha = jnp.sqrt((effect_square + week_square) / effects_all + EPS)
    by_alpha = (1.0 / alpha)[:, None]
    v_supplier = p_supplier * by_alpha
    v_lane = p_lane * by_alpha
    v_week = p_week * by_alpha
    forward = product(v_supplier * supplier_scale[None, :], supplier_hot.T)
    forward = forward + product(v_week * week_scale[None, :], week_hot.T)
    base = row_weight[None, :] * forward - (alpha[:, None] * by_beta) * rhs

    quarter = lane_own * columns // LANES_WIDE
    slot = (owner ^ me_ship) if by_step else owner
    index = slot * quarter + lane_within % quarter
    lane_part = (lane_within // quarter).reshape(square)
    residual, residual_sum = forward_lanes(
        index, lane_part, row_weight.reshape(square), by_beta * by_alpha, base, tables
    )
    residual_square = sum_over(residual_sum[:, 0], "ship")
    beta_next = jnp.sqrt(residual_square / shipments_all + EPS)
    u_next = residual / beta_next[:, None]
    step_size = alpha * beta_first / (alpha * alpha + beta_next * beta_next)
    x_supplier = step_size[:, None] * v_supplier
    x_lane = step_size[:, None] * v_lane
    effects = jnp.concatenate([jnp.sum(x_supplier * x_supplier, axis=0), jnp.sum(x_lane * x_lane, axis=0)])
    effects = effects + sum(swap(effects, "boot", step) for step in range(1, n_boot))
    spread = jnp.sqrt(effects / (columns * n_boot) + EPS)
    return (v_supplier, v_lane, v_week, u_next, step_size, spread[:supplier_own], spread[supplier_own:])


def solution(mesh):
    return jax.shard_map(
        on_device,
        mesh=mesh,
        in_specs=(
            P("ship"),
            P("ship"),
            P("ship"),
            P("ship", None),
            P("ship"),
            P("ship"),
            P("ship", None),
            P("boot", "ship"),
            P("ship"),
            P("ship"),
            P(),
        ),
        out_specs=(
            P("boot", "ship"),
            P("boot", "ship"),
            P("boot", None),
            P("boot", "ship"),
            P("boot"),
            P("ship"),
            P("ship"),
        ),
        check_vma=False,
    )
```

time: 556 us -> 176 us (0.32)
  waiting for transfers between devices: 253 us -> 58 us
  other arithmetic: 102 us -> 8.91 us
  blocking collectives: 83.1 us -> 0 us
  local copies, waits for them, and re-layouts: 70.7 us -> 5.1 us
  starting transfers between devices: 0.26 us -> 36.6 us
  Pallas kernels: 0 us -> 34.8 us
  between operations: 14.2 us -> 0.96 us
    reduce_scatter x1 -> x0, waiting for transfers between devices: 132 us -> none  [on_device(): lane_part = lax.psum_scatter(dense, 'ship', scatter_dimension=1, tiled=True)]
    all_gather x1 -> x0, waiting for transfers between devices: 121 us -> none  [on_device(): lax.all_gather(v_lane * lane_scale[None, :], 'ship', axis=1, tiled=True)]
    scatter-add x1 -> x0, other arithmetic: 91.3 us -> none  [on_device(): dense = jax.ops.segment_sum(weighted.T, lane_index, lane_own * n_ship).T]
    psum x4 -> x0, blocking collectives: 83.1 us -> none  [the longest x1 35.7 us: on_device(): effect_square = lax.psum(own_square, 'ship')]
    gather x2 -> x0, local copies, waits for them, and re-layouts: 62.9 us -> none  [on_device(): forward = forward + table[:, lane_index]]
    ppermute x0 -> x26, waiting for transfers between devices: none -> 58 us  [the longest x22 58 us: swap(): return lax.ppermute(value, axis, [(i, i ^ step) for i in range(size)])]
    pallas_call x0 -> x4, Pallas kernels: none -> 34.8 us  [the longest x1 17.4 us: forward_lanes(): pl.pallas_call(forward_kernel, out_shape=[jax.ShapeDtypeStruct((columns,...]
    ppermute x0 -> x26, starting transfers between devices: none -> 29.3 us  [the longest x22 24.2 us: swap(): return lax.ppermute(value, axis, [(i, i ^ step) for i in range(size)])]
  transfers between devices with their start and end apart: 2 -> 27, of which waited for: 2 -> 14; matrix products, arithmetic and copies ran while one was open for 2% -> 20% of each run, Pallas kernels for 0% -> 5%
where the time goes in v1:
time: 176 us; the launch traced here: 175 us
  waiting for transfers between devices  58 us (33%)
  starting transfers between devices  36.6 us (21%)
  Pallas kernels  34.8 us (20%)
  matrix products  31 us (18%)
  other arithmetic  8.91 us (5%)
  local copies, waits for them, and re-layouts  5.1 us (3%)
    ppermute x22, waiting for transfers between devices, swap(): return lax.ppermute(value, axis, [(i, i ^ step) for i in range(size)])  58 us
    dot_general x4, matrix products, product(): jnp.dot(left, right, precision=lax.Precision.HIGHEST, preferred_element_t...  24.9 us
    ppermute x22, starting transfers between devices, swap(): return lax.ppermute(value, axis, [(i, i ^ step) for i in range(size)])  24.2 us
    pallas_call x1, Pallas kernels, forward_lanes(): pl.pallas_call(forward_kernel, out_shape=[jax.ShapeDtypeStruct((columns,...  17.4 us
    pallas_call x2, Pallas kernels, lane_sums(): pl.pallas_call(functools.partial(lane_sums_kernel, low_n, turn_n, bool(pr...  17.2 us
    all_to_all x1, starting transfers between devices, on_device(): lax.all_to_all(jnp.broadcast_to(signs[None], (n_boot,) + signs.shape), 'b...  7.31 us
    dot_general x1, matrix products, product_rows(): lax.dot_general(left, hot, (((1,), (1,)), ((), ())), precision=lax.Precis...  6.08 us
    ppermute x2, starting transfers between devices, on_device(): got = lax.ppermute(planes, ('ship', 'boot'), pairs)  3.7 us
  transfers between devices with their start and end apart: 27, of which 14 were waited for; matrix products, arithmetic and copies ran while one was open for 20% of the time, Pallas kernels for 5%

profile of v1, /device:TPU:0, one launch (start us, length us, event | category | flops | bytes accessed | tf_op | source)
XLA Modules:
  0.0 175.5 jit_solution(12293709108126246988)
XLA Ops:
  5.1 3.0 %collective-permute-start.3 = (f32[392,128]{1,0:T(8,128)S(1)}, f32[392,128]{1,0:T(8,128)S(1)}, u32[]{:S(2)}, u32[]{:S(2)}) collective-permute-start(f32[392,128]{1,0:T(8,128)S(1)} %concatenate.26), channel_id=1, source_target_pairs={{0,4},{1,12},{2,20},{3,28},{4,0},{5,8},{6,16},{7,24},{8,5},{9,13},... | collective-permute-start | bytes 602120 | tf_op jit(solution)/shard_map/ppermute | solution.py:319
  9.5 7.3 %all-to-all-start = ((s32[4,32,128]{2,1,0:T(8,128)}), s32[4,32,128]{2,1,0:T(8,128)S(1)}, u32[]{:S(2)}, u32[]{:S(2)}) async-start(s32[4,32,128]{2,1,0:T(8,128)} %broadcast_in_dim.34), calls=%async_computation | async-start | bytes 131072 | tf_op jit(solution)/shard_map/all_to_all | solution.py:310
  17.5 6.1 %multiply_reduce_fusion = (f32[32]{0:T(128)S(1)}, f32[32,16384]{1,0:T(8,128)S(1)}) fusion(f32[16384]{0:T(1024)} %param.12, s32[128]{0:T(128)S(1)} %select_reduce_fusion, s32[128]{0:T(128)S(1)} %fusion.53, s32[32,128]{1,0:T(8,128)} %param.18, f32[16384]{0:T(1024)} %param.11), kind=kOutput, calls=%fused_computation.20 | convolution fusion | flops 813707264 | bytes 2245760 | tf_op jit(solution)/shard_map/dot_general | solution.py:30
  23.7 8.7 %fusion.3 = f32[32,260]{1,0:T(8,128)S(1)} fusion(s32[16384]{0:T(1024)S(1)} %copy-done.9, f32[32,16384]{1,0:T(8,128)S(1)} %get-tuple-element.61, f32[16384]{0:T(1024)S(1)} %copy-done), kind=kOutput, calls=%fused_computation.6 | convolution fusion | flops 1640562688 | bytes 2261504 | tf_op jit(solution)/shard_map/dot_general | solution.py:26
  33.0 3.6 %collective-permute-done = f32[32,261]{1,0:T(8,128)S(1)} collective-permute-done((f32[32,261]{1,0:T(8,128)S(1)}, f32[32,261]{1,0:T(8,128)S(1)}, u32[]{:S(2)}, u32[]{:S(2)}) %collective-permute-start) | collective-permute-done | bytes 33440 | tf_op jit(solution)/shard_map/ppermute | solution.py:41
  37.1 3.7 %collective-permute-done.1 = f32[32,261]{1,0:T(8,128)S(1)} collective-permute-done((f32[32,261]{1,0:T(8,128)S(1)}, f32[32,261]{1,0:T(8,128)S(1)}, u32[]{:S(2)}, u32[]{:S(2)}) %collective-permute-start.1) | collective-permute-done | bytes 33440 | tf_op jit(solution)/shard_map/ppermute | solution.py:41
  40.8 3.3 %collective-permute-start.2 = (f32[32,261]{1,0:T(8,128)S(1)}, f32[32,261]{1,0:T(8,128)S(1)}, u32[]{:S(2)}, u32[]{:S(2)}) collective-permute-start(f32[32,261]{1,0:T(8,128)S(1)} %add.94), channel_id=1, source_target_pairs={{0,16},{4,20},{8,24},{12,28},{16,0},{20,4},{24,8},{28,12},{1,17},{... | collective-permute-start | bytes 100232 | tf_op jit(solution)/shard_map/ppermute | solution.py:41
  46.5 8.6 %lane_sums.2 = (f32[32,2048]{1,0:T(8,128)S(1)}, f32[32,2048]{1,0:T(8,128)S(1)}, f32[32,2048]{1,0:T(8,128)S(1)}, f32[32,2048]{1,0:T(8,128)S(1)}) custom-call(s32[3,256]{1,0:T(4,128)S(1)} %get-tuple-element.56.meta, f32[392,128]{1,0:T(8,128)S(1)} %collective-permute-done.5.planes, s32[128,128]{1,0:T(8,128)S(1)} %collective-permute-done.6.signs), custom_call_target="tpu_custom_call" | custom-call | tf_op jit(solution)/shard_map/lane_sums/pallas_call | solution.py:144
  55.1 8.6 %lane_sums.3 = (f32[32,2048]{1,0:T(8,128)S(1)}, f32[32,2048]{1,0:T(8,128)S(1)}, f32[32,2048]{1,0:T(8,128)S(1)}, f32[32,2048]{1,0:T(8,128)S(1)}) custom-call(s32[3,256]{1,0:T(4,128)S(1)} %get-tuple-element.57.meta, f32[392,128]{1,0:T(8,128)S(1)} %collective-permute-done.3.planes, s32[128,128]{1,0:T(8,128)S(1)} %collective-permute-done.4.signs, ...), custom_call_target="tpu_custom_call" | custom-call | tf_op jit(solution)/shard_map/lane_sums/pallas_call | solution.py:144
  63.8 4.1 %collective-permute-start.7 = (f32[32,2048]{1,0:T(8,128)S(1)}, f32[32,2048]{1,0:T(8,128)S(1)}, u32[]{:S(2)}, u32[]{:S(2)}) collective-permute-start(f32[32,2048]{1,0:T(8,128)S(1)} %get-tuple-element.25), channel_id=1, source_target_pairs={{0,1},{1,0},{2,3},{3,2},{4,5},{5,4},{6,7},{7,6},{8,9},{9,8},{10,11... | collective-permute-start | bytes 786440 | tf_op jit(solution)/shard_map/ppermute | solution.py:41
  67.9 4.6 %collective-permute-start.8 = (f32[32,2048]{1,0:T(8,128)S(1)}, f32[32,2048]{1,0:T(8,128)S(1)}, u32[]{:S(2)}, u32[]{:S(2)}) collective-permute-start(f32[32,2048]{1,0:T(8,128)S(1)} %get-tuple-element.26), channel_id=1, source_target_pairs={{0,2},{1,3},{2,0},{3,1},{4,6},{5,7},{6,4},{7,5},{8,10},{9,11},{10,... | collective-permute-start | bytes 786440 | tf_op jit(solution)/shard_map/ppermute | solution.py:41
  72.6 3.8 %multiply_reduce_fusion.4 = (f32[32]{0:T(128)S(1)}, f32[32,128]{1,0:T(8,128)S(1)}) fusion(f32[32]{0:T(128)S(1)} %get-tuple-element.34, s32[128]{0:T(128)S(1)} %select_reduce_fusion, s32[128]{0:T(128)S(1)} %fusion.53, f32[32,16384]{1,0:T(8,128)S(1)} %get-tuple-element.61, f32[16384]{0:T(1024)S(1)} %copy-done, f32[128]{0:T(128)S(1)} %broadcast_multiply_fusion.3), kind=kOutput, calls=%fused_computation.60 | convolution fusion | flops 812138496 | bytes 2180864 | tf_op jit(solution)/shard_map/dot_general | solution.py:26
  76.4 3.3 %collective-permute-done.8.refs_2_ = f32[32,2048]{1,0:T(8,128)S(1)} collective-permute-done((f32[32,2048]{1,0:T(8,128)S(1)}, f32[32,2048]{1,0:T(8,128)S(1)}, u32[]{:S(2)}, u32[]{:S(2)}) %collective-permute-start.8) | collective-permute-done | bytes 262176 | tf_op jit(solution)/shard_map/ppermute | solution.py:41
  79.7 5.1 %collective-permute-done.9.refs_3_ = f32[32,2048]{1,0:T(8,128)S(1)} collective-permute-done((f32[32,2048]{1,0:T(8,128)S(1)}, f32[32,2048]{1,0:T(8,128)S(1)}, u32[]{:S(2)}, u32[]{:S(2)}) %collective-permute-start.9) | collective-permute-done | bytes 262176 | tf_op jit(solution)/shard_map/ppermute | solution.py:41
  86.6 2.8 %collective-permute-done.10 = f32[32]{0:T(128)S(1)} collective-permute-done((f32[32]{0:T(128)S(1)}, f32[32]{0:T(128)S(1)}, u32[]{:S(2)}, u32[]{:S(2)}) %collective-permute-start.10) | collective-permute-done | bytes 160 | tf_op jit(solution)/shard_map/ppermute | solution.py:41
  95.0 19.7 %collective-permute-done.12 = f32[32]{0:T(128)S(1)} collective-permute-done((f32[32]{0:T(128)S(1)}, f32[32]{0:T(128)S(1)}, u32[]{:S(2)}, u32[]{:S(2)}) %collective-permute-start.12) | collective-permute-done | bytes 160 | tf_op jit(solution)/shard_map/ppermute | solution.py:41
  115.0 5.1 %fusion.7 = f32[32,16384]{1,0:T(8,128)S(1)} fusion(s32[128]{0:T(128)S(1)} %select_reduce_fusion, s32[128]{0:T(128)S(1)} %fusion.53, f32[32,128]{1,0:T(8,128)S(1)} %broadcast_multiply_fusion.1, f32[128]{0:T(128)S(1)} %copy-done.10), kind=kOutput, calls=%fused_computation.12 | convolution fusion | flops 811601920 | bytes 2115072 | tf_op jit(solution)/shard_map/dot_general | solution.py:26
  122.8 7.3 %fusion.2.base = f32[32,16384]{1,0:T(8,128)S(1)} fusion(f32[32,16384]{1,0:T(8,128)S(1)} %fusion.7, s32[16384]{0:T(1024)S(1)} %copy-done.9, f32[32,16384]{1,0:T(8,128)S(1)} %copy-done.12, f32[32]{0:T(128)S(1)} %get-tuple-element.39, f32[16384]{0:T(1024)S(1)} %copy-done, f32[32,260]{1,0:T(8,128)S(1)} %fusion.38, f32[260]{0:T(512)S(1)} %copy-done.8), kind=kOutput, calls=%fused_computation.4 | convolution fusion | flops 1642143872 | bytes 6456976 | tf_op jit(solution)/shard_map/dot_general | solution.py:26
  130.8 4.3 %collective-permute-done.17.refs_5_ = f32[512,128]{1,0:T(8,128)S(1)} collective-permute-done((f32[512,128]{1,0:T(8,128)S(1)}, f32[512,128]{1,0:T(8,128)S(1)}, u32[]{:S(2)}, u32[]{:S(2)}) %collective-permute-start.17) | collective-permute-done | bytes 262176 | tf_op jit(solution)/shard_map/ppermute | solution.py:41
  135.1 3.5 %collective-permute-done.15.refs_3_ = f32[512,128]{1,0:T(8,128)S(1)} collective-permute-done((f32[512,128]{1,0:T(8,128)S(1)}, f32[512,128]{1,0:T(8,128)S(1)}, u32[]{:S(2)}, u32[]{:S(2)}) %collective-permute-start.15) | collective-permute-done | bytes 262176 | tf_op jit(solution)/shard_map/ppermute | solution.py:41
  139.6 17.4 %forward_lanes.1 = (f32[32,16384]{1,0:T(8,128)S(1)}, f32[32,1]{1,0:T(8,128)S(1)}) custom-call(s32[16384]{0:T(1024)S(1)} %get-tuple-element.51.index, s32[128,128]{1,0:T(8,128)S(1)} %get-tuple-element.49.lane_part, f32[128,128]{1,0:T(8,128)S(1)} %bitcast.41, f32[32,1]{1,0:T(8,128)S(1)} %copy.23.inverse, f32[32,16384]{1,0:T(8,128)S(1)} %fusion.2.base, ...), custom_call_target="tpu_custom_call" | custom-call | tf_op jit(solution)/shard_map/forward_lanes/pallas_call | solution.py:233
  157.7 3.0 %collective-permute-done.20 = f32[32]{0:T(128)S(1)} collective-permute-done((f32[32]{0:T(128)S(1)}, f32[32]{0:T(128)S(1)}, u32[]{:S(2)}, u32[]{:S(2)}) %collective-permute-start.20) | collective-permute-done | bytes 160 | tf_op jit(solution)/shard_map/ppermute | solution.py:41
  160.7 3.5 %collective-permute-done.21 = f32[32]{0:T(128)S(1)} collective-permute-done((f32[32]{0:T(128)S(1)}, f32[32]{0:T(128)S(1)}, u32[]{:S(2)}, u32[]{:S(2)}) %collective-permute-start.21) | collective-permute-done | bytes 160 | tf_op jit(solution)/shard_map/ppermute | solution.py:41
  164.2 4.4 %collective-permute-done.22 = f32[32]{0:T(128)S(1)} collective-permute-done((f32[32]{0:T(128)S(1)}, f32[32]{0:T(128)S(1)}, u32[]{:S(2)}, u32[]{:S(2)}) %collective-permute-start.22) | collective-permute-done | bytes 160 | tf_op jit(solution)/shard_map/ppermute | solution.py:41
  (114 shorter events, 29.5 us)
Async XLA Ops:
  4.4 41.9 %collective-permute-start.5 = (f32[392,128]{1,0:T(8,128)S(1)}, f32[392,128]{1,0:T(8,128)S(1)}, u32[]{:S(2)}, u32[]{:S(2)}) collective-permute-start(f32[392,128]{1,0:T(8,128)S(1)} %concatenate.26), channel_id=1, source_target_pairs={{0,0},{1,8},{2,16},{3,24},{4,4},{5,12},{6,20},{7,28},{8,1},{9,9},{... | collective-permute-start | bytes 602120 | tf_op jit(solution)/shard_map/ppermute | solution.py:319
  5.1 41.3 %collective-permute-start.3 = (f32[392,128]{1,0:T(8,128)S(1)}, f32[392,128]{1,0:T(8,128)S(1)}, u32[]{:S(2)}, u32[]{:S(2)}) collective-permute-start(f32[392,128]{1,0:T(8,128)S(1)} %concatenate.26), channel_id=1, source_target_pairs={{0,4},{1,12},{2,20},{3,28},{4,0},{5,8},{6,16},{7,24},{8,5},{9,13},... | collective-permute-start | bytes 602120 | tf_op jit(solution)/shard_map/ppermute | solution.py:319
  9.5 34.7 %all-to-all-start = ((s32[4,32,128]{2,1,0:T(8,128)}), s32[4,32,128]{2,1,0:T(8,128)S(1)}, u32[]{:S(2)}, u32[]{:S(2)}) async-start(s32[4,32,128]{2,1,0:T(8,128)} %broadcast_in_dim.34), calls=%async_computation | async-start | bytes 131072 | tf_op jit(solution)/shard_map/all_to_all | solution.py:310
  32.5 4.2 %collective-permute-start = (f32[32,261]{1,0:T(8,128)S(1)}, f32[32,261]{1,0:T(8,128)S(1)}, u32[]{:S(2)}, u32[]{:S(2)}) collective-permute-start(f32[32,261]{1,0:T(8,128)S(1)} %pad_maximum_fusion), channel_id=1, source_target_pairs={{0,4},{4,0},{8,12},{12,8},{16,20},{20,16},{24,28},{28,24},{1,5},{5... | collective-permute-start | bytes 100232 | tf_op jit(solution)/shard_map/ppermute | solution.py:41
  36.7 4.1 %collective-permute-start.1 = (f32[32,261]{1,0:T(8,128)S(1)}, f32[32,261]{1,0:T(8,128)S(1)}, u32[]{:S(2)}, u32[]{:S(2)}) collective-permute-start(f32[32,261]{1,0:T(8,128)S(1)} %fusion.57), channel_id=1, source_target_pairs={{0,8},{4,12},{8,0},{12,4},{16,24},{20,28},{24,16},{28,20},{1,9},{5... | collective-permute-start | bytes 100232 | tf_op jit(solution)/shard_map/ppermute | solution.py:41
  40.8 5.3 %collective-permute-start.2 = (f32[32,261]{1,0:T(8,128)S(1)}, f32[32,261]{1,0:T(8,128)S(1)}, u32[]{:S(2)}, u32[]{:S(2)}) collective-permute-start(f32[32,261]{1,0:T(8,128)S(1)} %add.94), channel_id=1, source_target_pairs={{0,16},{4,20},{8,24},{12,28},{16,0},{20,4},{24,8},{28,12},{1,17},{... | collective-permute-start | bytes 100232 | tf_op jit(solution)/shard_map/ppermute | solution.py:41
  45.0 10.1 %collective-permute-start.4 = (s32[128,128]{1,0:T(8,128)S(1)}, s32[128,128]{1,0:T(8,128)S(1)}, u32[]{:S(2)}, u32[]{:S(2)}) collective-permute-start(s32[128,128]{1,0:T(8,128)S(1)} %bitcast.46), channel_id=1, source_target_pairs={{0,4},{1,12},{2,20},{3,28},{4,0},{5,8},{6,16},{7,24},{8,5},{9,13},... | collective-permute-start | bytes 196616 | tf_op jit(solution)/shard_map/ppermute | solution.py:320
  63.8 12.6 %collective-permute-start.7 = (f32[32,2048]{1,0:T(8,128)S(1)}, f32[32,2048]{1,0:T(8,128)S(1)}, u32[]{:S(2)}, u32[]{:S(2)}) collective-permute-start(f32[32,2048]{1,0:T(8,128)S(1)} %get-tuple-element.25), channel_id=1, source_target_pairs={{0,1},{1,0},{2,3},{3,2},{4,5},{5,4},{6,7},{7,6},{8,9},{9,8},{10,11... | collective-permute-start | bytes 786440 | tf_op jit(solution)/shard_map/ppermute | solution.py:41
  67.9 11.8 %collective-permute-start.8 = (f32[32,2048]{1,0:T(8,128)S(1)}, f32[32,2048]{1,0:T(8,128)S(1)}, u32[]{:S(2)}, u32[]{:S(2)}) collective-permute-start(f32[32,2048]{1,0:T(8,128)S(1)} %get-tuple-element.26), channel_id=1, source_target_pairs={{0,2},{1,3},{2,0},{3,1},{4,6},{5,7},{6,4},{7,5},{8,10},{9,11},{10,... | collective-permute-start | bytes 786440 | tf_op jit(solution)/shard_map/ppermute | solution.py:41
  72.5 12.3 %collective-permute-start.9 = (f32[32,2048]{1,0:T(8,128)S(1)}, f32[32,2048]{1,0:T(8,128)S(1)}, u32[]{:S(2)}, u32[]{:S(2)}) collective-permute-start(f32[32,2048]{1,0:T(8,128)S(1)} %get-tuple-element.27), channel_id=1, source_target_pairs={{0,3},{1,2},{2,1},{3,0},{4,7},{5,6},{6,5},{7,4},{8,11},{9,10},{10,... | collective-permute-start | bytes 786440 | tf_op jit(solution)/shard_map/ppermute | solution.py:41
  85.8 3.6 %collective-permute-start.10 = (f32[32]{0:T(128)S(1)}, f32[32]{0:T(128)S(1)}, u32[]{:S(2)}, u32[]{:S(2)}) collective-permute-start(f32[32]{0:T(128)S(1)} %get-tuple-element.43), channel_id=1, source_target_pairs={{0,4},{4,0},{8,12},{12,8},{16,20},{20,16},{24,28},{28,24},{1,5},{5... | collective-permute-start | bytes 392 | tf_op jit(solution)/shard_map/ppermute | solution.py:41
  89.5 3.5 %collective-permute-start.11 = (f32[32]{0:T(128)S(1)}, f32[32]{0:T(128)S(1)}, u32[]{:S(2)}, u32[]{:S(2)}) collective-permute-start(f32[32]{0:T(128)S(1)} %add.99), channel_id=1, source_target_pairs={{0,8},{4,12},{8,0},{12,4},{16,24},{20,28},{24,16},{28,20},{1,9},{5... | collective-permute-start | bytes 392 | tf_op jit(solution)/shard_map/ppermute | solution.py:41
  90.0 30.1 %collective-permute-start.18 = (f32[512,128]{1,0:T(8,128)S(1)}, f32[512,128]{1,0:T(8,128)S(1)}, u32[]{:S(2)}, u32[]{:S(2)}) collective-permute-start(f32[512,128]{1,0:T(8,128)S(1)} %get-tuple-element.30.refs_0_), channel_id=1, source_target_pairs={{0,24},{4,28},{8,16},{12,20},{16,8},{20,12},{24,0},{28,4},{1,25},{... | collective-permute-start | bytes 786440 | tf_op jit(solution)/shard_map/ppermute | solution.py:41
  92.1 28.7 %collective-permute-start.16 = (f32[512,128]{1,0:T(8,128)S(1)}, f32[512,128]{1,0:T(8,128)S(1)}, u32[]{:S(2)}, u32[]{:S(2)}) collective-permute-start(f32[512,128]{1,0:T(8,128)S(1)} %get-tuple-element.30.refs_0_), channel_id=1, source_target_pairs={{0,16},{4,20},{8,24},{12,28},{16,0},{20,4},{24,8},{28,12},{1,17},{... | collective-permute-start | bytes 786440 | tf_op jit(solution)/shard_map/ppermute | solution.py:41
  93.0 21.7 %collective-permute-start.12 = (f32[32]{0:T(128)S(1)}, f32[32]{0:T(128)S(1)}, u32[]{:S(2)}, u32[]{:S(2)}) collective-permute-start(f32[32]{0:T(128)S(1)} %add.100), channel_id=1, source_target_pairs={{0,16},{4,20},{8,24},{12,28},{16,0},{20,4},{24,8},{28,12},{1,17},{... | collective-permute-start | bytes 392 | tf_op jit(solution)/shard_map/ppermute | solution.py:41
  95.0 27.2 %collective-permute-start.14 = (f32[512,128]{1,0:T(8,128)S(1)}, f32[512,128]{1,0:T(8,128)S(1)}, u32[]{:S(2)}, u32[]{:S(2)}) collective-permute-start(f32[512,128]{1,0:T(8,128)S(1)} %get-tuple-element.30.refs_0_), channel_id=1, source_target_pairs={{0,8},{4,12},{8,0},{12,4},{16,24},{20,28},{24,16},{28,20},{1,9},{5... | collective-permute-start | bytes 786440 | tf_op jit(solution)/shard_map/ppermute | solution.py:41
  95.0 35.1 %collective-permute-start.13 = (f32[512,128]{1,0:T(8,128)S(1)}, f32[512,128]{1,0:T(8,128)S(1)}, u32[]{:S(2)}, u32[]{:S(2)}) collective-permute-start(f32[512,128]{1,0:T(8,128)S(1)} %get-tuple-element.30.refs_0_), channel_id=1, source_target_pairs={{0,4},{4,0},{8,12},{12,8},{16,20},{20,16},{24,28},{28,24},{1,5},{5... | collective-permute-start | bytes 786440 | tf_op jit(solution)/shard_map/ppermute | solution.py:41
  120.2 10.7 %collective-permute-start.19 = (f32[512,128]{1,0:T(8,128)S(1)}, f32[512,128]{1,0:T(8,128)S(1)}, u32[]{:S(2)}, u32[]{:S(2)}) collective-permute-start(f32[512,128]{1,0:T(8,128)S(1)} %collective-permute-done.18.refs_6_), channel_id=1, source_target_pairs={{0,4},{4,0},{8,12},{12,8},{16,20},{20,16},{24,28},{28,24},{1,5},{5... | collective-permute-start | bytes 786440 | tf_op jit(solution)/shard_map/ppermute | solution.py:41
  120.8 14.3 %collective-permute-start.17 = (f32[512,128]{1,0:T(8,128)S(1)}, f32[512,128]{1,0:T(8,128)S(1)}, u32[]{:S(2)}, u32[]{:S(2)}) collective-permute-start(f32[512,128]{1,0:T(8,128)S(1)} %collective-permute-done.16.refs_4_), channel_id=1, source_target_pairs={{0,4},{4,0},{8,12},{12,8},{16,20},{20,16},{24,28},{28,24},{1,5},{5... | collective-permute-start | bytes 786440 | tf_op jit(solution)/shard_map/ppermute | solution.py:41
  122.3 16.4 %collective-permute-start.15 = (f32[512,128]{1,0:T(8,128)S(1)}, f32[512,128]{1,0:T(8,128)S(1)}, u32[]{:S(2)}, u32[]{:S(2)}) collective-permute-start(f32[512,128]{1,0:T(8,128)S(1)} %collective-permute-done.14.refs_2_), channel_id=1, source_target_pairs={{0,4},{4,0},{8,12},{12,8},{16,20},{20,16},{24,28},{28,24},{1,5},{5... | collective-permute-start | bytes 786440 | tf_op jit(solution)/shard_map/ppermute | solution.py:41
  157.1 3.6 %collective-permute-start.20 = (f32[32]{0:T(128)S(1)}, f32[32]{0:T(128)S(1)}, u32[]{:S(2)}, u32[]{:S(2)}) collective-permute-start(f32[32]{0:T(128)S(1)} %reduce.3), channel_id=1, source_target_pairs={{0,4},{4,0},{8,12},{12,8},{16,20},{20,16},{24,28},{28,24},{1,5},{5... | collective-permute-start | bytes 392 | tf_op jit(solution)/shard_map/ppermute | solution.py:41
  160.7 3.5 %collective-permute-start.21 = (f32[32]{0:T(128)S(1)}, f32[32]{0:T(128)S(1)}, u32[]{:S(2)}, u32[]{:S(2)}) collective-permute-start(f32[32]{0:T(128)S(1)} %add.107), channel_id=1, source_target_pairs={{0,8},{4,12},{8,0},{12,4},{16,24},{20,28},{24,16},{28,20},{1,9},{5... | collective-permute-start | bytes 392 | tf_op jit(solution)/shard_map/ppermute | solution.py:41
  164.2 4.4 %collective-permute-start.22 = (f32[32]{0:T(128)S(1)}, f32[32]{0:T(128)S(1)}, u32[]{:S(2)}, u32[]{:S(2)}) collective-permute-start(f32[32]{0:T(128)S(1)} %add.108), channel_id=1, source_target_pairs={{0,16},{4,20},{8,24},{12,28},{16,0},{20,4},{24,8},{28,12},{1,17},{... | collective-permute-start | bytes 392 | tf_op jit(solution)/shard_map/ppermute | solution.py:41
  170.6 3.8 %collective-permute-start.24 = (f32[2176]{0:T(1024)S(1)}, f32[2176]{0:T(1024)S(1)}, u32[]{:S(2)}, u32[]{:S(2)}) collective-permute-start(f32[2176]{0:T(1024)S(1)} %pad_maximum_fusion.1), channel_id=1, source_target_pairs={{0,2},{1,3},{2,0},{3,1},{4,6},{5,7},{6,4},{7,5},{8,10},{9,11},{10,... | collective-permute-start | bytes 26120 | tf_op jit(solution)/shard_map/ppermute | solution.py:41
  (16 other events, 132.6 us)

commit v2 on v0

v2 whole, which is shorter than its diff:
```python
import functools

import jax
import jax.numpy as jnp
from jax import lax
from jax.experimental import pallas as pl
from jax.experimental.pallas import tpu as pltpu
from jax.sharding import PartitionSpec as P

EPS = 1e-06
BLOCK = 256
FIRSTS = 256
SLOTS = 7
LANES_WIDE = 128
VMEM = pl.BlockSpec(memory_space=pltpu.VMEM)
SMEM = pl.BlockSpec(memory_space=pltpu.SMEM)
ANY = pl.BlockSpec(memory_space=pl.ANY)
PARAMS = pltpu.CompilerParams(vmem_limit_bytes=40 << 20)


SMALL = pltpu.CompilerParams(vmem_limit_bytes=8 << 20)
WHOLE = pltpu.CompilerParams(vmem_limit_bytes=60 << 20)


def takes(microseconds):
    return pl.CostEstimate(flops=0, bytes_accessed=int(microseconds * 3.6e6), transcendentals=0)


def split(value):
    high = value.astype(jnp.bfloat16)
    low = (value - high.astype(jnp.float32)).astype(jnp.bfloat16)
    return high, low


def fetch(sources, held, arrived):
    copies = [pltpu.make_async_copy(source, here, arrived.at[at]) for at, (source, here) in enumerate(zip(sources, held))]
    for copy in copies:
        copy.start()
    for copy in copies:
        copy.wait()
    return held


def held_for(sources):
    return [pltpu.VMEM(one.shape, one.dtype) for one in sources] + [pltpu.SemaphoreType.DMA((len(sources),))]


def swap(value, axis, step):
    size = lax.axis_size(axis)
    return lax.ppermute(value, axis, [(i, i ^ step) for i in range(size)])


def turned(place, size):
    bits = size.bit_length() - 1
    return sum(((place >> bit) & 1) << (bits - 1 - bit) for bit in range(bits))


def sum_over(value, axis, step=1):
    while step < lax.axis_size(axis):
        value = value + swap(value, axis, step)
        step *= 2
    return value


def lane_blocks_kernel(low_n, rows, where, meta, planes, acc, acc_fit):
    blocks = rows * 128 // BLOCK
    offset = where[0]
    shift = low_n.bit_length() - 1
    acc[...] = jnp.zeros_like(acc)
    acc_fit[...] = jnp.zeros_like(acc_fit)
    high_at = lax.broadcasted_iota(jnp.int32, (8, BLOCK), 0)
    place = lax.broadcasted_iota(jnp.int32, (8, BLOCK), 1)
    low_at = lax.broadcasted_iota(jnp.int32, (low_n, BLOCK), 0)

    def two_rows(start):
        pair = [planes[pl.ds(start + u, 1), :] for u in range(BLOCK // 128)]
        return jnp.concatenate(pair, axis=1)

    def prepare(block):
        row = block * (BLOCK // 128)
        local = two_rows(row).astype(jnp.int32) - offset
        high, low = local >> shift, local & (low_n - 1)
        match = jnp.broadcast_to(high, (8, BLOCK)) == high_at
        fit = jnp.where(match, jnp.broadcast_to(two_rows(rows + row), (8, BLOCK)), 0.0)
        res = jnp.where(match, jnp.broadcast_to(two_rows(2 * rows + row), (8, BLOCK)), 0.0)
        hot = jnp.where(jnp.broadcast_to(low, (low_n, BLOCK)) == low_at, 1.0, 0.0).astype(jnp.bfloat16)
        return fit, res, hot

    def group(first, block, fit, res, hot):
        at = place + block * BLOCK
        parts = []
        for u in range(SLOTS):
            inside = (at >= meta[first + u]) & (at < meta[first + u + 1])
            parts.append(jnp.where(inside, res, 0.0))
        left = jnp.concatenate(parts + [fit], axis=0)
        both = lax.dot_general(
            jnp.concatenate(split(left), axis=0),
            hot,
            (((1,), (1,)), ((), ())),
            preferred_element_type=jnp.float32,
        )
        return both[: 8 * SLOTS + 8] + both[8 * SLOTS + 8 :]

    def add(first, sums):
        at = pl.ds(pl.multiple_of(first * 8, 8), 8 * SLOTS)
        for u in range(low_n // 128):
            acc[u, at, :] = acc[u, at, :] + sums[: 8 * SLOTS, u * 128 : (u + 1) * 128]

    unroll = 4

    @pl.loop(0, blocks // unroll)
    def _(step):
        ready = [prepare(step * unroll + u) for u in range(unroll)]
        firsts = [meta[FIRSTS + step * unroll + u] for u in range(unroll)]
        sums = [group(firsts[u], step * unroll + u, *ready[u]) for u in range(unroll)]
        for u in range(unroll):
            add(firsts[u], sums[u])
        acc_fit[...] = acc_fit[...] + sum(one[8 * SLOTS :] for one in sums)
        for u in range(unroll):
            block = step * unroll + u
            more = (meta[FIRSTS + block + 1] - firsts[u]) // SLOTS

            @pl.loop(0, more)
            def _(turn_at):
                first = firsts[u] + (turn_at + 1) * SLOTS
                fit, res, hot = prepare(block)
                add(first, group(first, block, fit, res, hot))


def lane_blocks(where, meta, planes, rows, suppliers, own):
    low_n = max(own // 8, 128)
    return pl.pallas_call(
        functools.partial(lane_blocks_kernel, low_n, rows),
        out_shape=[
            jax.ShapeDtypeStruct((low_n // 128, (suppliers + SLOTS + 1) * 8, 128), jnp.float32),
            jax.ShapeDtypeStruct((8, low_n), jnp.float32),
        ],
        in_specs=[SMEM, SMEM, VMEM],
        out_specs=[VMEM] * 2,
        compiler_params=PARAMS,
        cost_estimate=takes(8),
        name="lane_blocks",
    )(where, meta, planes)


def lane_parts_kernel(turn_n, suppliers, share, where, *refs):
    inputs, outs, signs = refs[:-4], refs[-4:-1], refs[-1]
    accs, fits, got = inputs[:share], inputs[share : 2 * share], inputs[2 * share :]
    columns, own = outs[0].shape
    low_n = fits[0].shape[1]
    at = 0
    for piece in got:
        signs[at : at + piece.shape[0], :] = (2.0 * piece[...] - 1.0).astype(jnp.bfloat16)
        at += piece.shape[0]
    turn = where[1]
    total_fit = fits[0][...]
    for fit in fits[1:]:
        total_fit = total_fit + fit[...]
    height = share * columns
    groups = []
    for part in range(turn_n):
        here = pl.multiple_of((turn ^ turned(part, turn_n)) * height, height)
        groups.append(signs[pl.ds(here, height), :])
    lefts = []
    for step in range(share):
        left = jnp.concatenate([group[step * columns : (step + 1) * columns] for group in groups], axis=0)
        lefts.append(jnp.concatenate([left, left], axis=1))
    for high in range(-(-own // low_n)):
        total = jnp.broadcast_to(total_fit[high : high + 1, :], (turn_n * columns, low_n))
        for step in range(share):
            rows_at = pl.ds(high, suppliers, stride=8)
            wide = jnp.concatenate([accs[step][u, rows_at, :] for u in range(low_n // 128)], axis=1)
            right = jnp.concatenate(split(wide), axis=0)
            total = total + jnp.dot(lefts[step], right, preferred_element_type=jnp.float32)
        for part in range(turn_n):
            if part % 2:
                target, line = 2, (part // 2) * columns
            else:
                target, line = min(part // 2, 1), max(part // 2 - 1, 0) * columns
            value = total[part * columns : (part + 1) * columns]
            outs[target][line : line + columns, high * low_n : (high + 1) * low_n] = value


def lane_parts(where, blocks, got, columns, own, suppliers, turn_n):
    share = len(blocks)
    heights = [n * columns for n in (1, turn_n // 2 - 1, turn_n // 2)]
    return pl.pallas_call(
        functools.partial(lane_parts_kernel, turn_n, suppliers, share),
        out_shape=[jax.ShapeDtypeStruct((height, own), jnp.float32) for height in heights],
        in_specs=[SMEM] + [VMEM] * (2 * share + len(got)),
        out_specs=[VMEM] * 3,
        scratch_shapes=[pltpu.VMEM((turn_n * share * columns, suppliers), jnp.bfloat16)],
        compiler_params=PARAMS,
        cost_estimate=takes(1),
        name="lane_parts",
    )(where, *[acc for acc, _ in blocks], *[fit for _, fit in blocks], *got)


def table_kernel(ratio, scale, own, *refs):
    parts, entries, table = refs[:-2], refs[-2], refs[-1]
    total = parts[0][...]
    for part in parts[1:]:
        total = total + part[...]
    by = jnp.broadcast_to(scale[...], total.shape)
    entry = ratio * by * total
    entries[...] = entry
    columns = total.shape[0]
    square = jnp.sum(entry * entry, axis=1, keepdims=True) + own[...]
    wide = jnp.broadcast_to(square, (columns, 128))
    scaled = by * entry
    quarter = table.shape[0] - 8
    count = total.shape[1] // quarter
    stacked = jnp.concatenate([scaled[:, u * quarter : (u + 1) * quarter] for u in range(count)], axis=0)
    table[0:quarter, :] = stacked.T
    table[quarter:, :] = jnp.concatenate([wide] * (128 // columns), axis=0).T[0:8]


def lane_table(ratio, scale, own, parts):
    columns, lanes = parts[0].shape
    quarter = lanes * columns // LANES_WIDE
    return pl.pallas_call(
        functools.partial(table_kernel, ratio),
        out_shape=[
            jax.ShapeDtypeStruct((columns, lanes), jnp.float32),
            jax.ShapeDtypeStruct((quarter + 8, LANES_WIDE), jnp.float32),
        ],
        in_specs=[VMEM] * (2 + len(parts)),
        out_specs=[VMEM] * 2,
        compiler_params=SMALL,
        cost_estimate=takes(1),
        name="lane_table",
    )(scale, own, *parts)


def forward_kernel(effects_all, lines, index, before, by_beta, week_square, lane_part, weight, *refs):
    sources, tables = refs[:2], refs[2:-12]
    out, squares, alpha_out, table, first, second, total, forward, rhs, value_out, landed, moved = refs[-12:]
    columns = total.shape[0]
    groups = weight.shape[0]
    copies, at = [], 0
    for place, piece in enumerate(tables):
        here = table.at[pl.ds(at, piece.shape[0])]
        copies.append(pltpu.make_async_copy(piece, here, landed.at[place]))
        at += piece.shape[0]
    parts = 4
    wide = groups * 128 // parts
    loads = []
    for part in range(parts):
        here = (slice(None), pl.ds(part * wide, wide))
        for place, (source, held) in enumerate(zip(sources, (forward, rhs))):
            loads.append(pltpu.make_async_copy(source.at[here], held.at[here], moved.at[place, part]))
    for copy in [*copies, *loads]:
        copy.start()
    for copy in copies:
        copy.wait()
    effect_square = jnp.zeros((1, 128), jnp.float32)
    for start in range(0, at, lines + 8):
        effect_square = effect_square + table[start + lines : start + lines + 1, :]
    effect_square = jnp.broadcast_to(effect_square, (128, 128)).T[0:columns]
    by = by_beta[...]
    alpha = jnp.sqrt((effect_square[:, 0:1] * by * by + week_square[...]) / effects_all + EPS)
    alpha_out[...] = alpha
    scale = jnp.broadcast_to(by / alpha, (columns, 128))
    share = jnp.broadcast_to(by * alpha, (columns, 128))
    total[...] = jnp.zeros_like(total)

    def gather(group, store):
        for u in range(128):
            store[u : u + 1, :] = table[pl.ds(index[group * 128 + u], 1), :]

    def finish(group, store):
        turned_over = store[...].T
        part = jnp.broadcast_to(lane_part[pl.ds(group, 1), :], (columns, 128))
        picked = turned_over[0:columns]
        for u in range(1, 128 // columns):
            picked = jnp.where(part == u, turned_over[u * columns : (u + 1) * columns], picked)
        at = pl.ds(pl.multiple_of(group * 128, 128), 128)
        line = jnp.broadcast_to(weight[pl.ds(group, 1), :], (columns, 128))
        value = (forward[:, at] + picked * line) * scale - share * rhs[:, at]
        value_out[:, at] = value
        total[...] = total[...] + value * value

    gather(0, first)
    stores = []
    for part in range(parts):
        for copy in loads[2 * part : 2 * part + 2]:
            copy.wait()

        @pl.loop(part * groups // 2 // parts, (part + 1) * groups // 2 // parts)
        def _(step):
            gather(2 * step + 1, second)
            finish(2 * step, first)
            gather(jnp.minimum(2 * step + 2, groups - 1), first)
            finish(2 * step + 1, second)

        here = (slice(None), pl.ds(part * wide, wide))
        stores.append(pltpu.make_async_copy(value_out.at[here], out.at[here], moved.at[2, part]))
        stores[-1].start()
    across = jnp.broadcast_to(jnp.sum(total[...], axis=1, keepdims=True), (columns, 128))
    squares[...] = jnp.concatenate([across] * (128 // columns), axis=0).T[0:8]
    for copy in stores:
        copy.wait()


def forward_lanes(effects_all, lines, index, before, by_beta, week_square, lane_part, weight, forward, rhs, tables):
    columns, rows = rhs.shape
    height = sum(piece.shape[0] for piece in tables)
    return pl.pallas_call(
        functools.partial(forward_kernel, effects_all, lines),
        out_shape=[
            jax.ShapeDtypeStruct((columns, rows), jnp.float32),
            jax.ShapeDtypeStruct((8, 128), jnp.float32),
            jax.ShapeDtypeStruct((columns, 1), jnp.float32),
        ],
        in_specs=[SMEM] + [VMEM] * 5 + [ANY] * (2 + len(tables)),
        out_specs=[ANY] + [VMEM] * 2,
        scratch_shapes=[
            pltpu.VMEM((height, LANES_WIDE), jnp.float32),
            pltpu.VMEM((128, LANES_WIDE), jnp.float32),
            pltpu.VMEM((128, LANES_WIDE), jnp.float32),
            pltpu.VMEM((columns, 128), jnp.float32),
            *[pltpu.VMEM((columns, rows), jnp.float32)] * 3,
            pltpu.SemaphoreType.DMA((len(tables),)),
            pltpu.SemaphoreType.DMA((3, 4)),
        ],
        compiler_params=WHOLE,
        cost_estimate=takes(18),
        name="forward_lanes",
    )(index, before, by_beta, week_square, lane_part, weight, forward, rhs, *tables)


def message_kernel(lane_own, *refs):
    sources, (planes, bounds, firsts), held, arrived = refs[:7], refs[7:10], refs[10:17], refs[17]
    fitted, resid, weight, block, within, runs, signs = fetch(sources, held, arrived)
    rows = fitted.shape[0]
    planes[0:rows, :] = (block[...] * lane_own + within[...]).astype(jnp.float32)
    planes[rows : 2 * rows, :] = weight[...] * fitted[...]
    planes[2 * rows : 3 * rows, :] = weight[...] * resid[...]
    suppliers = runs.shape[1]
    across = jnp.broadcast_to(runs[...].astype(jnp.float32), (suppliers, suppliers))
    down = across.T
    at_row = lax.broadcasted_iota(jnp.int32, (suppliers, suppliers), 0)
    at_lane = lax.broadcasted_iota(jnp.int32, (suppliers, suppliers), 1)
    end_column = jnp.sum(jnp.where(at_lane <= at_row, across, 0.0), axis=1, keepdims=True)
    start_column = jnp.sum(jnp.where(at_lane < at_row, across, 0.0), axis=1, keepdims=True)
    start_row = jnp.sum(jnp.where(at_row < at_lane, down, 0.0), axis=0, keepdims=True)
    whole = (at_lane * BLOCK).astype(jnp.float32)
    first_row = jnp.sum(jnp.where(end_column <= whole, 1.0, 0.0), axis=0, keepdims=True)
    full = jnp.full((1, suppliers), rows * 128.0, jnp.float32)
    planes[3 * rows + 8 :, :] = signs[...].astype(jnp.float32)
    planes[3 * rows : 3 * rows + 8, :] = jnp.concatenate(
        [start_row, full, first_row, jnp.zeros((5, suppliers), jnp.float32)], axis=0
    )
    firsts[...] = first_row.astype(jnp.int32)
    columns = [start_column, end_column, jnp.zeros((suppliers, 6), jnp.float32)]
    bounds[0:suppliers, :] = jnp.concatenate(columns, axis=1).astype(jnp.int32)
    bounds[suppliers:, :] = jnp.full((16, 8), rows * 128, jnp.int32)


def message(lane_own, *sources):
    fitted, runs, signs = sources[0], sources[5], sources[6]
    rows = fitted.shape[0]
    suppliers = runs.shape[1]
    return pl.pallas_call(
        functools.partial(message_kernel, lane_own),
        out_shape=[
            jax.ShapeDtypeStruct((3 * rows + 8 + signs.shape[0], 128), jnp.float32),
            jax.ShapeDtypeStruct((suppliers + 16, 8), jnp.int32),
            jax.ShapeDtypeStruct((1, suppliers), jnp.int32),
        ],
        in_specs=[ANY] * 7,
        out_specs=[VMEM] * 3,
        scratch_shapes=held_for(sources),
        compiler_params=WHOLE,
        cost_estimate=takes(2),
        name="message",
    )(*sources)


def row_of(ref, start):
    pair = [ref[pl.ds(start + u, 1), :] for u in range(BLOCK // 128)]
    return jnp.concatenate(pair, axis=1)


def hot_supplier(block, bounds):
    suppliers = bounds.shape[0] - 16
    place = lax.broadcasted_iota(jnp.int32, (suppliers, BLOCK), 1) + block * BLOCK
    inside = (place >= bounds[0:suppliers, 0:1]) & (place < bounds[0:suppliers, 1:2])
    return jnp.where(inside, 1.0, 0.0).astype(jnp.bfloat16)


def hot_week(block, week, weeks):
    at = lax.broadcasted_iota(jnp.int32, (weeks, BLOCK), 0)
    same = jnp.broadcast_to(row_of(week, block * (BLOCK // 128)), (weeks, BLOCK)) == at
    return jnp.where(same, 1.0, 0.0).astype(jnp.bfloat16)


def own_sums_kernel(weeks, firsts, *refs):
    supplier, stats, by_week, fit_week, by_sign = refs[6], refs[7], *refs[-3:]
    fitted, resid, weight, week, bounds, signs = fetch(refs[:6], refs[8:14], refs[14])
    columns, suppliers = signs.shape
    blocks = fitted.shape[0] * 128 // BLOCK
    by_week[...] = jnp.zeros_like(by_week)
    fit_week[...] = jnp.zeros_like(fit_week)
    by_sign[...] = jnp.zeros_like(by_sign)
    shape = (8, BLOCK)
    place = lax.broadcasted_iota(jnp.int32, shape, 1)
    line = lax.broadcasted_iota(jnp.int32, shape, 0)

    def prepare(block):
        row = block * (BLOCK // 128)
        fit, res, by = [jnp.broadcast_to(row_of(one, row), shape) for one in (fitted, resid, weight)]
        more, less = fit + res, fit - res
        both = jnp.where(line == 0, more * more, jnp.where(line == 1, less * less, 0.0))
        both = jnp.where(line == 2, by * more, jnp.where(line == 3, by * less, both))
        return jnp.where(line == 0, by * fit, 0.0), by * res, both, hot_week(block, week, weeks)

    def group(first, block, fit, res, both, hot):
        at = place + block * BLOCK
        here = bounds[pl.ds(first, 8), :]
        inside = (at >= here[:, 0:1]) & (at < here[:, 1:2])
        left = jnp.concatenate([jnp.where(inside, res, 0.0), fit], axis=0)
        left = jnp.concatenate(split(left), axis=0)
        sums = lax.dot_general(left, hot, (((1,), (1,)), ((), ())), preferred_element_type=jnp.float32)
        mask = jnp.where(jnp.concatenate([inside, inside], axis=0), 1.0, 0.0).astype(jnp.bfloat16)
        pair = jnp.concatenate(split(both), axis=0)
        signed = lax.dot_general(mask, pair, (((1,), (1,)), ((), ())), preferred_element_type=jnp.float32)
        return sums[:16] + sums[16:], signed[:8]

    def add(first, got):
        at = pl.ds(first, 8)
        for u in range(by_week.shape[0]):
            part = got[0][:8, u * 128 : (u + 1) * 128]
            wide = slice(0, part.shape[1])
            by_week[u, at, wide] = by_week[u, at, wide] + part
        by_sign[at, 0:16] = by_sign[at, 0:16] + got[1]

    unroll = 4

    @pl.loop(0, blocks // unroll)
    def _(step):
        ready = [prepare(step * unroll + u) for u in range(unroll)]
        begin = [firsts[0, step * unroll + u] for u in range(unroll)]
        got = [group(begin[u], step * unroll + u, *ready[u]) for u in range(unroll)]
        for u in range(unroll):
            add(begin[u], got[u])
        fit_week[:, 0:weeks] = fit_week[:, 0:weeks] + sum(one[0][8:] for one in got)
        for u in range(unroll):
            block = step * unroll + u

            @pl.loop(0, (firsts[0, block + 1] - begin[u]) // 8)
            def _(turn_at):
                first = begin[u] + (turn_at + 1) * 8
                fit, res, both, hot = prepare(block)
                add(first, group(first, block, fit, res, both, hot))

    positive = signs[...] == 1
    sign = (2 * signs[...] - 1).astype(jnp.float32).astype(jnp.bfloat16)
    left = jnp.concatenate([sign, sign], axis=1)
    four = by_sign[0:suppliers, :].T
    four = four[0:8] + four[8:16]
    rows = [jnp.broadcast_to(four[u : u + 1, :], positive.shape) for u in range(4)]
    supplier[...] = jnp.where(positive, rows[2], rows[3])
    square = jnp.broadcast_to(jnp.sum(jnp.where(positive, rows[0], rows[1]), axis=1, keepdims=True), (columns, 128))
    last = lax.broadcasted_iota(jnp.int32, (columns, 128), 1) == 127
    for u in range(by_week.shape[0]):
        right = jnp.concatenate(split(by_week[u, 0:suppliers, :]), axis=0)
        part = fit_week[0:1, u * 128 : u * 128 + 128]
        part = jnp.dot(left, right, preferred_element_type=jnp.float32) + jnp.broadcast_to(part, (columns, 128))
        if u == by_week.shape[0] - 1:
            part = jnp.where(last, square, part)
        stats[u * columns : (u + 1) * columns, :] = part


def own_sums(firsts, weeks, *sources):
    columns, suppliers = sources[5].shape
    return pl.pallas_call(
        functools.partial(own_sums_kernel, weeks),
        out_shape=[
            jax.ShapeDtypeStruct((columns, suppliers), jnp.float32),
            jax.ShapeDtypeStruct((-(-weeks // 128) * columns, 128), jnp.float32),
        ],
        in_specs=[SMEM] + [ANY] * 6,
        out_specs=[VMEM] * 2,
        scratch_shapes=held_for(sources)
        + [
            pltpu.VMEM((-(-weeks // 128), suppliers + 16, 128), jnp.float32),
            pltpu.VMEM((8, -(-weeks // 128) * 128), jnp.float32),
            pltpu.VMEM((suppliers + 16, 128), jnp.float32),
        ],
        compiler_params=WHOLE,
        cost_estimate=takes(7),
        name="own_sums",
    )(firsts, *sources)


def base_kernel(*refs):
    forward, rhs_out, token = refs[8:11]
    fitted, resid, weight, week, bounds, signs, effects = fetch(refs[:7], refs[11:18], refs[18])
    columns, suppliers = signs.shape
    weeks = effects.shape[1] - suppliers
    sign = (2 * signs[...] - 1).astype(jnp.float32).astype(jnp.bfloat16)
    by_effect = jnp.concatenate(split(effects[...]), axis=0)
    blocks = fitted.shape[0] * 128 // BLOCK

    def one(block):
        row = block * (BLOCK // 128)
        by_supplier = hot_supplier(block, bounds)
        spread = jnp.dot(sign, by_supplier, preferred_element_type=jnp.float32)
        shape = (columns, BLOCK)
        at = pl.ds(pl.multiple_of(block * BLOCK, BLOCK), BLOCK)
        rhs = jnp.broadcast_to(row_of(fitted, row), shape) + spread * jnp.broadcast_to(row_of(resid, row), shape)
        rhs_out[:, at] = rhs
        hot = jnp.concatenate([by_supplier, hot_week(block, week, weeks)], axis=0)
        both = jnp.dot(by_effect, hot, preferred_element_type=jnp.float32)
        forward[:, at] = jnp.broadcast_to(row_of(weight, row), shape) * (both[:columns] + both[columns:])

    unroll = 4

    @pl.loop(0, blocks // unroll)
    def _(step):
        for u in range(unroll):
            one(step * unroll + u)

    token[...] = jnp.zeros_like(token)


def forward_base(sources, before):
    shape = jax.ShapeDtypeStruct((sources[5].shape[0], sources[0].size), jnp.float32)
    return pl.pallas_call(
        base_kernel,
        out_shape=[shape, shape, jax.ShapeDtypeStruct((8, 128), jnp.float32)],
        in_specs=[ANY] * 8,
        out_specs=[VMEM] * 3,
        scratch_shapes=held_for(sources),
        compiler_params=PARAMS,
        cost_estimate=takes(8),
        name="forward_base",
    )(*sources, before)


def near_tables(table, n_ship):
    if n_ship > 16:
        return [lax.all_gather(table, "ship", axis=0, tiled=True)]
    steps = [*range(1, n_ship // 2), *range(n_ship // 2, n_ship, 2)]
    return [table] + [swap(table, "ship", step) for step in steps]


def all_tables(near, n_ship):
    if n_ship > 16:
        return near
    tables = near[: n_ship // 2]
    for table in near[n_ship // 2 :]:
        tables += [table, swap(table, "ship", 1)]
    return tables


def effect_sums_kernel(count, residual, alpha, beta_first, supplier, entry, sums, step_out, inverse):
    columns = alpha.shape[0]
    square = jnp.broadcast_to(residual[0:1, :], (128, 128)).T[0:columns, 0:1]
    beta_next = jnp.sqrt(square / count + EPS)
    step = alpha[...] * beta_first[...] / (alpha[...] * alpha[...] + beta_next * beta_next)
    step_out[...] = step
    inverse[...] = 1.0 / beta_next
    scale = step / (alpha[...] * beta_first[...])
    rows = []
    for line in (supplier[...] * scale, entry[...] * scale):
        total = jnp.sum(line * line, axis=0, keepdims=True)
        rows += [total[:, at : at + 128] for at in range(0, line.shape[1], 128)]
    rows.append(jnp.zeros((sums.shape[0] - len(rows), 128), jnp.float32))
    sums[...] = jnp.concatenate(rows, axis=0)


def effect_sums(count, residual, alpha, beta_first, supplier, entry):
    lines = 1 + entry.shape[1] // 128
    column = jax.ShapeDtypeStruct(alpha.shape, jnp.float32)
    return pl.pallas_call(
        functools.partial(effect_sums_kernel, count),
        out_shape=[jax.ShapeDtypeStruct((lines // 8 * 8 + 8, 128), jnp.float32), column, column],
        in_specs=[VMEM] * 5,
        out_specs=[VMEM] * 3,
        compiler_params=SMALL,
        cost_estimate=takes(1),
        name="effect_sums",
    )(residual, alpha, beta_first, supplier, entry)


def spread_kernel(count, *refs):
    parts, supplier, lane = refs[:-2], refs[-2], refs[-1]
    total = parts[0][...]
    for part in parts[1:]:
        total = total + part[...]
    total = jnp.sqrt(total / count + EPS)
    supplier[...] = total[0:1]
    lane[...] = total[1 : 1 + lane.shape[0]]


def spreads(count, lines, parts):
    return pl.pallas_call(
        functools.partial(spread_kernel, count),
        out_shape=[jax.ShapeDtypeStruct((1, 128), jnp.float32), jax.ShapeDtypeStruct((lines, 128), jnp.float32)],
        in_specs=[VMEM] * len(parts),
        out_specs=[VMEM] * 2,
        compiler_params=SMALL,
        cost_estimate=takes(1),
        name="spreads",
    )(*parts)


def on_device(
    fitted,
    resid,
    row_weight,
    lane_block,
    lane_within,
    week_id,
    supplier_runs,
    signs,
    supplier_scale,
    lane_scale,
    week_scale,
):
    rows = fitted.shape[0]
    columns = signs.shape[0]
    n_ship = lax.axis_size("ship")
    n_boot = lax.axis_size("boot")
    me_ship = lax.axis_index("ship")
    me_boot = lax.axis_index("boot")
    lane_own = lane_scale.shape[0]
    weeks = week_scale.shape[0]
    supplier_own = supplier_scale.shape[0]
    shipments_all = rows * n_ship
    effects_all = supplier_own * n_ship + lane_own * n_ship + weeks
    ratio = effects_all / shipments_all
    share = n_ship // n_boot

    owner = lane_block[:, 0]
    square = (rows // 128, 128)
    fitted, resid, row_weight, week_id = [one.reshape(square) for one in (fitted, resid, row_weight, week_id)]

    planes, bounds, firsts = message(
        lane_own, fitted, resid, row_weight, owner.reshape(square), lane_within.reshape(square), supplier_runs, signs
    )
    got = []
    for turn in range(share):
        pairs = []
        for source in range(n_ship):
            target = (source // n_boot - turn) % share * n_boot
            for b in range(n_boot):
                pairs.append((source * n_boot + b, (target + turned(b, n_boot)) * n_boot + source % n_boot))
        got.append(lax.ppermute(planes, ("ship", "boot"), pairs))

    weeks_up = -(-weeks // 16) * 16
    held = (fitted, resid, row_weight, week_id, bounds, signs)
    supplier_part, early = own_sums(firsts, weeks_up, *held)
    got, early = lax.optimization_barrier((got, early))
    p_supplier = ratio * supplier_scale[None, :] * supplier_part
    supplier_square = jnp.sum(p_supplier * p_supplier, axis=1, keepdims=True)

    me_turn = sum(jnp.where(me_boot == b, turned(b, n_boot), 0) for b in range(n_boot))
    where = jnp.stack([me_ship * lane_own, (me_ship % n_boot) ^ me_turn]).astype(jnp.int32)
    fixed = 3 * square[0] + 8
    others = [one[fixed:] for one in got]
    blocks, step = [], 1
    for at, one in enumerate(got):
        meta = one[fixed - 8 : fixed].reshape(-1).astype(jnp.int32)
        blocks.append(lane_blocks(where, meta, one, square[0], supplier_own, lane_own))
        if step < n_boot:
            lines = step * share * columns
            back = swap(jnp.concatenate([*others, early], axis=0), "ship", step)
            others, early, step = [*others, back[:lines]], early + back[lines:], 2 * step
            if at + 1 < share:
                got[at + 1], early = lax.optimization_barrier((got[at + 1], early))
    early = sum_over(early, "ship", step)
    sums = lane_parts(where, blocks, others, columns, lane_own, supplier_own, n_boot)
    kept, later, sent = sums
    back = swap(sent, "boot", 1)
    pieces = [kept, back[:columns]]
    later = later + back[columns:]
    for step in range(1, n_boot // 2):
        pieces.append(swap(later[(step - 1) * columns : step * columns], "boot", 2 * step))
    entry, table = lane_table(ratio, lane_scale[None, :], supplier_square, pieces)
    near = near_tables(table, n_ship)

    beta_first = jnp.sqrt(early[-columns:, 127] / shipments_all + EPS)
    week_part = jnp.concatenate([early[at : at + columns] for at in range(0, early.shape[0], columns)], axis=1)
    by_beta = (1.0 / beta_first)[:, None]
    p_week = ratio * week_scale[None, :] * week_part[:, :weeks]
    week_square = jnp.sum(p_week * p_week, axis=1, keepdims=True) * by_beta * by_beta
    effects = jnp.concatenate(
        [
            p_supplier * supplier_scale[None, :],
            p_week * week_scale[None, :],
            jnp.zeros((columns, weeks_up - weeks), jnp.float32),
        ],
        axis=1,
    )

    forward, rhs, token = forward_base((*held, effects), near[min(1, len(near) - 1)][:8])
    near[n_ship // 2 :], token = lax.optimization_barrier((near[n_ship // 2 :], token))
    tables = all_tables(near, n_ship)

    quarter = lane_own * columns // LANES_WIDE
    slot = owner if n_ship > 16 else owner ^ me_ship
    index = slot * (quarter + 8) + lane_within % quarter
    lane_part = (lane_within // quarter).reshape(square)
    residual, residual_sum, alpha = forward_lanes(
        effects_all, quarter, index, token, by_beta, week_square, lane_part, row_weight, forward, rhs, tables
    )
    by_both = by_beta / alpha
    v_supplier = p_supplier * by_both
    v_lane = entry * by_both
    v_week = p_week * by_both
    residual_sum = sum_over(residual_sum, "ship")
    effects, step_size, inverse = effect_sums(shipments_all, residual_sum, alpha, beta_first[:, None], p_supplier, entry)
    effects = [effects] + [swap(effects, "boot", step) for step in range(1, n_boot)]
    u_next = residual * inverse
    spread_supplier, spread_lane = spreads(columns * n_boot, lane_own // 128, effects)
    spread_supplier, spread_lane = spread_supplier.reshape(-1), spread_lane.reshape(-1)
    return (v_supplier, v_lane, v_week, u_next, step_size[:, 0], spread_supplier, spread_lane)


def solution(mesh):
    return jax.shard_map(
        on_device,
        mesh=mesh,
        in_specs=(
            P("ship"),
            P("ship"),
            P("ship"),
            P("ship", None),
            P("ship"),
            P("ship"),
            P("ship", None),
            P("boot", "ship"),
            P("ship"),
            P("ship"),
            P(),
        ),
        out_specs=(
            P("boot", "ship"),
            P("boot", "ship"),
            P("boot", None),
            P("boot", "ship"),
            P("boot"),
            P("ship"),
            P("ship"),
        ),
        check_vma=False,
    )
```

time: 556 us -> 136 us (0.24)
  waiting for transfers between devices: 253 us -> 30.7 us
  other arithmetic: 102 us -> 12.6 us
  blocking collectives: 83.1 us -> 0 us
  local copies, waits for them, and re-layouts: 70.7 us -> 4.4 us
  Pallas kernels: 0 us -> 58.9 us
  matrix products: 32.2 us -> 0 us
  starting transfers between devices: 0.26 us -> 27 us
  between operations: 14.2 us -> 1.08 us
    reduce_scatter x1 -> x0, waiting for transfers between devices: 132 us -> none  [on_device(): lane_part = lax.psum_scatter(dense, 'ship', scatter_dimension=1, tiled=True)]
    all_gather x1 -> x0, waiting for transfers between devices: 121 us -> none  [on_device(): lax.all_gather(v_lane * lane_scale[None, :], 'ship', axis=1, tiled=True)]
    scatter-add x1 -> x0, other arithmetic: 91.3 us -> none  [on_device(): dense = jax.ops.segment_sum(weighted.T, lane_index, lane_own * n_ship).T]
    psum x4 -> x0, blocking collectives: 83.1 us -> none  [the longest x1 35.7 us: on_device(): effect_square = lax.psum(own_square, 'ship')]
    gather x2 -> x0, local copies, waits for them, and re-layouts: 62.9 us -> none  [on_device(): forward = forward + table[:, lane_index]]
    pallas_call x0 -> x10, Pallas kernels: none -> 58.9 us  [the longest x1 22.1 us: forward_lanes(): pl.pallas_call(functools.partial(forward_kernel, effects_all, lines), out...]
    dot_general x5 -> x0, matrix products: 32.2 us -> none  [the longest x4 24.8 us: product(): jnp.dot(left, right, precision=lax.Precision.HIGHEST, preferred_element_t...]
    ppermute x0 -> x20, waiting for transfers between devices: none -> 30.7 us  [the longest x18 30.7 us: swap(): return lax.ppermute(value, axis, [(i, i ^ step) for i in range(size)])]
  transfers between devices with their start and end apart: 2 -> 20, of which waited for: 2 -> 10; matrix products, arithmetic and copies ran while one was open for 2% -> 7% of each run, Pallas kernels for 0% -> 24%
where the time goes in v2:
time: 136 us; the launch traced here: 135 us
  Pallas kernels  58.9 us (43%)
  waiting for transfers between devices  30.7 us (23%)
  starting transfers between devices  27 us (20%)
  other arithmetic  12.6 us (9%)
  local copies, waits for them, and re-layouts  4.4 us (3%)
    ppermute x18, waiting for transfers between devices, swap(): return lax.ppermute(value, axis, [(i, i ^ step) for i in range(size)])  30.7 us
    pallas_call x1, Pallas kernels, forward_lanes(): pl.pallas_call(functools.partial(forward_kernel, effects_all, lines), out...  22.1 us
    ppermute x18, starting transfers between devices, swap(): return lax.ppermute(value, axis, [(i, i ^ step) for i in range(size)])  21.3 us
    pallas_call x2, Pallas kernels, lane_blocks(): pl.pallas_call(functools.partial(lane_blocks_kernel, low_n, rows), out_sh...  14.8 us
    pallas_call x1, Pallas kernels, own_sums(): pl.pallas_call(functools.partial(own_sums_kernel, weeks), out_shape=[jax....  9.11 us
    pallas_call x1, Pallas kernels, forward_base(): pl.pallas_call(base_kernel, out_shape=[shape, shape, jax.ShapeDtypeStruct...  8.77 us
    ppermute x2, starting transfers between devices, on_device(): got.append(lax.ppermute(planes, ('ship', 'boot'), pairs))  5.68 us
    unnamed x46, local copies, waits for them, and re-layouts  4.12 us
  transfers between devices with their start and end apart: 20, of which 10 were waited for; matrix products, arithmetic and copies ran while one was open for 7% of the time, Pallas kernels for 24%

profile of v2, /device:TPU:0, one launch (start us, length us, event | category | flops | bytes accessed | tf_op | source)
XLA Modules:
  0.0 134.7 jit_solution(17404214051649864429)
XLA Ops:
  0.6 1.9 %message.1 = (f32[424,128]{1,0:T(8,128)}, s32[144,8]{1,0:T(8,128)}, s32[1,128]{1,0:T(1,128)}) custom-call(f32[128,128]{1,0:T(8,128)} %bitcast.24, f32[128,128]{1,0:T(8,128)} %bitcast.27, f32[128,128]{1,0:T(8,128)} %bitcast.20, s32[128,128]{1,0:T(8,128)} %bitcast.33, s32[128,128]{1,0:T(8,128)} %bitcast.35, s32[1,128]{1,0:T(1,128)} %refs_5_.3, s32[32,128]{1,0:T(8,128)} %refs_5_.5), custom_call_target="tpu_custom_call" | custom-call | bytes 7200000 | tf_op jit(solution)/shard_map/message/pallas_call | solution.py:364
  2.5 4.1 %collective-permute-start.1 = (f32[424,128]{1,0:T(8,128)}, f32[424,128]{1,0:T(8,128)S(1)}, u32[]{:S(2)}, u32[]{:S(2)}) collective-permute-start(f32[424,128]{1,0:T(8,128)} %get-tuple-element.43), channel_id=1, source_target_pairs={{0,16},{1,24},{2,20},{3,28},{4,17},{5,25},{6,21},{7,29},{8,18},{9,... | collective-permute-start | bytes 651272 | tf_op jit(solution)/shard_map/ppermute | solution.py:651
  6.6 1.6 %collective-permute-start = (f32[424,128]{1,0:T(8,128)}, f32[424,128]{1,0:T(8,128)S(1)}, u32[]{:S(2)}, u32[]{:S(2)}) collective-permute-start(f32[424,128]{1,0:T(8,128)} %get-tuple-element.43), channel_id=1, source_target_pairs={{0,0},{1,8},{2,4},{3,12},{4,1},{5,9},{6,5},{7,13},{8,2},{9,10},{10... | collective-permute-start | bytes 651272 | tf_op jit(solution)/shard_map/ppermute | solution.py:651
  9.2 9.1 %own_sums.1 = (f32[32,128]{1,0:T(8,128)}, f32[96,128]{1,0:T(8,128)}) custom-call(s32[1,128]{1,0:T(1,128)} %get-tuple-element.40.firsts, f32[128,128]{1,0:T(8,128)} %bitcast.25, f32[128,128]{1,0:T(8,128)} %bitcast.28, f32[128,128]{1,0:T(8,128)} %bitcast.21, s32[128,128]{1,0:T(8,128)} %bitcast.30, s32[144,8]{1,0:T(8,128)} %get-tuple-element.41.refs_4_, ...), custom_call_target="tpu_custom_call" | custom-call | bytes 25200000 | tf_op jit(solution)/shard_map/own_sums/pallas_call | solution.py:477
  19.9 3.1 %collective-permute-start.2 = (f32[160,128]{1,0:T(8,128)S(1)}, f32[160,128]{1,0:T(8,128)S(1)}, u32[]{:S(2)}, u32[]{:S(2)}) collective-permute-start(f32[160,128]{1,0:T(8,128)S(1)} %pad_maximum_fusion.1), channel_id=1, source_target_pairs={{0,4},{4,0},{8,12},{12,8},{16,20},{20,16},{24,28},{28,24},{1,5},{5... | collective-permute-start | bytes 245768 | tf_op jit(solution)/shard_map/ppermute | solution.py:50
  23.0 7.4 %lane_blocks.2 = (f32[2,1088,128]{2,1,0:T(8,128)S(1)}, f32[8,256]{1,0:T(8,128)S(1)}) custom-call(s32[2]{0:T(128)S(1)} %pad_add_fusion.where, s32[1024]{0:T(1024)S(1)} %convert_bitcast_fusion.1.meta, f32[424,128]{1,0:T(8,128)S(1)} %collective-permute-done.planes), custom_call_target="tpu_custom_call" | custom-call | bytes 28800000 | tf_op jit(solution)/shard_map/lane_blocks/pallas_call | solution.py:132
  31.2 3.4 %collective-permute-start.3 = (f32[224,128]{1,0:T(8,128)S(1)}, f32[224,128]{1,0:T(8,128)S(1)}, u32[]{:S(2)}, u32[]{:S(2)}) collective-permute-start(f32[224,128]{1,0:T(8,128)S(1)} %pad_maximum_fusion), channel_id=1, source_target_pairs={{0,8},{4,12},{8,0},{12,4},{16,24},{20,28},{24,16},{28,20},{1,9},{5... | collective-permute-start | bytes 344072 | tf_op jit(solution)/shard_map/ppermute | solution.py:50
  34.6 7.4 %lane_blocks.3 = (f32[2,1088,128]{2,1,0:T(8,128)S(1)}, f32[8,256]{1,0:T(8,128)S(1)}) custom-call(s32[2]{0:T(128)S(1)} %pad_add_fusion.where, s32[1024]{0:T(1024)S(1)} %convert_bitcast_fusion.meta, f32[424,128]{1,0:T(8,128)S(1)} %collective-permute-done.1.planes), custom_call_target="tpu_custom_call" | custom-call | bytes 28800000 | tf_op jit(solution)/shard_map/lane_blocks/pallas_call | solution.py:132
  43.6 1.8 %collective-permute-done.5 = f32[64,2048]{1,0:T(8,128)S(1)} collective-permute-done((f32[64,2048]{1,0:T(8,128)S(1)}, f32[64,2048]{1,0:T(8,128)S(1)}, u32[]{:S(2)}, u32[]{:S(2)}) %collective-permute-start.5) | collective-permute-done | bytes 524320 | tf_op jit(solution)/shard_map/ppermute | solution.py:50
  45.7 3.4 %collective-permute-done.4 = f32[96,128]{1,0:T(8,128)S(1)} collective-permute-done((f32[96,128]{1,0:T(8,128)S(1)}, f32[96,128]{1,0:T(8,128)S(1)}, u32[]{:S(2)}, u32[]{:S(2)}) %collective-permute-start.4) | collective-permute-done | bytes 49184 | tf_op jit(solution)/shard_map/ppermute | solution.py:50
  49.1 4.7 %collective-permute-done.6.refs_2_ = f32[32,2048]{1,0:T(8,128)S(1)} collective-permute-done((f32[32,2048]{1,0:T(8,128)S(1)}, f32[32,2048]{1,0:T(8,128)S(1)}, u32[]{:S(2)}, u32[]{:S(2)}) %collective-permute-start.6) | collective-permute-done | bytes 262176 | tf_op jit(solution)/shard_map/ppermute | solution.py:50
  55.8 4.3 %collective-permute-start.11 = (f32[520,128]{1,0:T(8,128)S(1)}, f32[520,128]{1,0:T(8,128)S(1)}, u32[]{:S(2)}, u32[]{:S(2)}) collective-permute-start(f32[520,128]{1,0:T(8,128)S(1)} %get-tuple-element.57.refs_2_), channel_id=1, source_target_pairs={{0,12},{4,8},{8,4},{12,0},{16,28},{20,24},{24,20},{28,16},{1,13},{... | collective-permute-start | bytes 798728 | tf_op jit(solution)/shard_map/ppermute | solution.py:50
  60.2 1.7 %collective-permute-done.9.refs_3_ = f32[520,128]{1,0:T(8,128)S(1)} collective-permute-done((f32[520,128]{1,0:T(8,128)S(1)}, f32[520,128]{1,0:T(8,128)S(1)}, u32[]{:S(2)}, u32[]{:S(2)}) %collective-permute-start.9) | collective-permute-done | bytes 266272 | tf_op jit(solution)/shard_map/ppermute | solution.py:50
  61.9 8.8 %forward_base.1 = (f32[32,16384]{1,0:T(8,128)S(1)}, f32[32,16384]{1,0:T(8,128)S(1)}, f32[8,128]{1,0:T(8,128)S(1)}) custom-call(f32[128,128]{1,0:T(8,128)S(1)} %bitcast.26, f32[128,128]{1,0:T(8,128)S(1)} %bitcast.29, f32[128,128]{1,0:T(8,128)S(1)} %bitcast.23, s32[128,128]{1,0:T(8,128)S(1)} %bitcast.31, s32[144,8]{1,0:T(8,128)S(1)} %copy-done.5, ...), custom_call_target="tpu_custom_call" | custom-call | bytes 28800000 | tf_op jit(solution)/shard_map/forward_base/pallas_call | solution.py:530
  73.4 5.2 %collective-permute-done.7.refs_6_ = f32[520,128]{1,0:T(8,128)S(1)} collective-permute-done((f32[520,128]{1,0:T(8,128)S(1)}, f32[520,128]{1,0:T(8,128)S(1)}, u32[]{:S(2)}, u32[]{:S(2)}) %collective-permute-start.7) | collective-permute-done | bytes 266272 | tf_op jit(solution)/shard_map/ppermute | solution.py:50
  78.6 1.7 %collective-permute-start.12 = (f32[520,128]{1,0:T(8,128)S(1)}, f32[520,128]{1,0:T(8,128)S(1)}, u32[]{:S(2)}, u32[]{:S(2)}) collective-permute-start(f32[520,128]{1,0:T(8,128)S(1)} %collective-permute-done.7.refs_6_), channel_id=1, source_target_pairs={{0,4},{4,0},{8,12},{12,8},{16,20},{20,16},{24,28},{28,24},{1,5},{5... | collective-permute-start | bytes 798728 | tf_op jit(solution)/shard_map/ppermute | solution.py:50
  82.1 5.8 %collective-permute-done.12.refs_7_ = f32[520,128]{1,0:T(8,128)S(1)} collective-permute-done((f32[520,128]{1,0:T(8,128)S(1)}, f32[520,128]{1,0:T(8,128)S(1)}, u32[]{:S(2)}, u32[]{:S(2)}) %collective-permute-start.12) | collective-permute-done | bytes 266272 | tf_op jit(solution)/shard_map/ppermute | solution.py:50
  87.9 3.1 %collective-permute-done.13.refs_9_ = f32[520,128]{1,0:T(8,128)S(1)} collective-permute-done((f32[520,128]{1,0:T(8,128)S(1)}, f32[520,128]{1,0:T(8,128)S(1)}, u32[]{:S(2)}, u32[]{:S(2)}) %collective-permute-start.13) | collective-permute-done | bytes 266272 | tf_op jit(solution)/shard_map/ppermute | solution.py:50
  91.7 22.1 %forward_lanes.1 = (f32[32,16384]{1,0:T(8,128)}, f32[8,128]{1,0:T(8,128)}, f32[32,1]{1,0:T(8,128)}) custom-call(s32[16384]{0:T(1024)} %get-tuple-element.78.index, f32[8,128]{1,0:T(8,128)} %copy-done.11, f32[32,1]{1,0:T(8,128)} %get-tuple-element.84.by_beta, f32[32,1]{1,0:T(8,128)} %get-tuple-element.83.week_square, s32[128,128]{1,0:T(8,128)} %get-tuple-element.77.lane_part, ...), custom_call_target="tpu_custom_call" | custom-call | bytes 64800000 | tf_op jit(solution)/shard_map/forward_lanes/pallas_call | solution.py:308
  116.9 1.6 %collective-permute-done.14 = f32[8,128]{1,0:T(8,128)S(1)} collective-permute-done((f32[8,128]{1,0:T(8,128)}, f32[8,128]{1,0:T(8,128)S(1)}, u32[]{:S(2)}, u32[]{:S(2)}) %collective-permute-start.14) | collective-permute-done | bytes 4128 | tf_op jit(solution)/shard_map/ppermute | solution.py:50
  120.9 2.0 %collective-permute-done.15 = f32[8,128]{1,0:T(8,128)S(1)} collective-permute-done((f32[8,128]{1,0:T(8,128)S(1)}, f32[8,128]{1,0:T(8,128)S(1)}, u32[]{:S(2)}, u32[]{:S(2)}) %collective-permute-start.15) | collective-permute-done | bytes 4128 | tf_op jit(solution)/shard_map/ppermute | solution.py:50
  122.9 2.3 %collective-permute-start.16 = (f32[8,128]{1,0:T(8,128)S(1)}, f32[8,128]{1,0:T(8,128)S(1)}, u32[]{:S(2)}, u32[]{:S(2)}) collective-permute-start(f32[8,128]{1,0:T(8,128)S(1)} %add.63), channel_id=1, source_target_pairs={{0,16},{4,20},{8,24},{12,28},{16,0},{20,4},{24,8},{28,12},{1,17},{... | collective-permute-start | bytes 12296 | tf_op jit(solution)/shard_map/ppermute | solution.py:50
  125.8 1.5 %collective-permute-done.16 = f32[8,128]{1,0:T(8,128)S(1)} collective-permute-done((f32[8,128]{1,0:T(8,128)S(1)}, f32[8,128]{1,0:T(8,128)S(1)}, u32[]{:S(2)}, u32[]{:S(2)}) %collective-permute-start.16) | collective-permute-done | bytes 4128 | tf_op jit(solution)/shard_map/ppermute | solution.py:50
  130.3 3.1 %broadcast_multiply_fusion = f32[32,16384]{1,0:T(8,128)} fusion(f32[32,16384]{1,0:T(8,128)} %get-tuple-element.66, f32[32]{0:T(128)S(1)} %reduce.1), kind=kLoop, calls=%fused_computation | loop fusion | flops 524288 | bytes 4194432 | tf_op jit(solution)/shard_map/mul | solution.py:717
  (110 shorter events, 22.7 us)
Async XLA Ops:
  2.5 16.5 %collective-permute-start.1 = (f32[424,128]{1,0:T(8,128)}, f32[424,128]{1,0:T(8,128)S(1)}, u32[]{:S(2)}, u32[]{:S(2)}) collective-permute-start(f32[424,128]{1,0:T(8,128)} %get-tuple-element.43), channel_id=1, source_target_pairs={{0,16},{1,24},{2,20},{3,28},{4,17},{5,25},{6,21},{7,29},{8,18},{9,... | collective-permute-start | bytes 651272 | tf_op jit(solution)/shard_map/ppermute | solution.py:651
  6.6 12.4 %collective-permute-start = (f32[424,128]{1,0:T(8,128)}, f32[424,128]{1,0:T(8,128)S(1)}, u32[]{:S(2)}, u32[]{:S(2)}) collective-permute-start(f32[424,128]{1,0:T(8,128)} %get-tuple-element.43), channel_id=1, source_target_pairs={{0,0},{1,8},{2,4},{3,12},{4,1},{5,9},{6,5},{7,13},{8,2},{9,10},{10... | collective-permute-start | bytes 651272 | tf_op jit(solution)/shard_map/ppermute | solution.py:651
  8.2 35.2 %copy-start.22 = (f32[128]{0:T(128)S(1)}, f32[128]{0:T(128)}, u32[]{:S(2)}) copy-start(f32[128]{0:T(128)} %param.19) | copy-start | bytes 1540
  19.9 10.5 %collective-permute-start.2 = (f32[160,128]{1,0:T(8,128)S(1)}, f32[160,128]{1,0:T(8,128)S(1)}, u32[]{:S(2)}, u32[]{:S(2)}) collective-permute-start(f32[160,128]{1,0:T(8,128)S(1)} %pad_maximum_fusion.1), channel_id=1, source_target_pairs={{0,4},{4,0},{8,12},{12,8},{16,20},{20,16},{24,28},{28,24},{1,5},{5... | collective-permute-start | bytes 245768 | tf_op jit(solution)/shard_map/ppermute | solution.py:50
  31.2 10.8 %collective-permute-start.3 = (f32[224,128]{1,0:T(8,128)S(1)}, f32[224,128]{1,0:T(8,128)S(1)}, u32[]{:S(2)}, u32[]{:S(2)}) collective-permute-start(f32[224,128]{1,0:T(8,128)S(1)} %pad_maximum_fusion), channel_id=1, source_target_pairs={{0,8},{4,12},{8,0},{12,4},{16,24},{20,28},{24,16},{28,20},{1,9},{5... | collective-permute-start | bytes 344072 | tf_op jit(solution)/shard_map/ppermute | solution.py:50
  43.3 37.3 %copy-start.19 = (s32[16384]{0:T(1024)S(1)}, s32[16384]{0:T(1024)}, u32[]{:S(2)}) copy-start(s32[16384]{0:T(1024)} %param.15) | copy-start | bytes 196612
  43.3 2.0 %collective-permute-start.5 = (f32[64,2048]{1,0:T(8,128)S(1)}, f32[64,2048]{1,0:T(8,128)S(1)}, u32[]{:S(2)}, u32[]{:S(2)}) collective-permute-start(f32[64,2048]{1,0:T(8,128)S(1)} %get-tuple-element.55), channel_id=1, source_target_pairs={{0,1},{1,0},{2,3},{3,2},{4,5},{5,4},{6,7},{7,6},{8,9},{9,8},{10,11... | collective-permute-start | bytes 1572872 | tf_op jit(solution)/shard_map/ppermute | solution.py:50
  43.5 5.6 %collective-permute-start.4 = (f32[96,128]{1,0:T(8,128)S(1)}, f32[96,128]{1,0:T(8,128)S(1)}, u32[]{:S(2)}, u32[]{:S(2)}) collective-permute-start(f32[96,128]{1,0:T(8,128)S(1)} %slice_add_fusion.1), channel_id=1, source_target_pairs={{0,16},{4,20},{8,24},{12,28},{16,0},{20,4},{24,8},{28,12},{1,17},{... | collective-permute-start | bytes 147464 | tf_op jit(solution)/shard_map/ppermute | solution.py:50
  45.4 8.4 %collective-permute-start.6 = (f32[32,2048]{1,0:T(8,128)S(1)}, f32[32,2048]{1,0:T(8,128)S(1)}, u32[]{:S(2)}, u32[]{:S(2)}) collective-permute-start(f32[32,2048]{1,0:T(8,128)S(1)} %get-tuple-element.75), channel_id=1, source_target_pairs={{0,2},{1,3},{2,0},{3,1},{4,6},{5,7},{6,4},{7,5},{8,10},{9,11},{10,... | collective-permute-start | bytes 786440 | tf_op jit(solution)/shard_map/ppermute | solution.py:50
  54.1 36.9 %copy-start.6 = (f32[520,128]{1,0:T(8,128)}, f32[520,128]{1,0:T(8,128)S(1)}, u32[]{:S(2)}) copy-start(f32[520,128]{1,0:T(8,128)S(1)} %get-tuple-element.57.refs_2_) | copy-start | bytes 798724
  54.1 7.8 %collective-permute-start.9 = (f32[520,128]{1,0:T(8,128)S(1)}, f32[520,128]{1,0:T(8,128)S(1)}, u32[]{:S(2)}, u32[]{:S(2)}) collective-permute-start(f32[520,128]{1,0:T(8,128)S(1)} %get-tuple-element.57.refs_2_), channel_id=1, source_target_pairs={{0,4},{4,0},{8,12},{12,8},{16,20},{20,16},{24,28},{28,24},{1,5},{5... | collective-permute-start | bytes 798728 | tf_op jit(solution)/shard_map/ppermute | solution.py:50
  54.2 19.2 %collective-permute-start.8 = (f32[520,128]{1,0:T(8,128)S(1)}, f32[520,128]{1,0:T(8,128)S(1)}, u32[]{:S(2)}, u32[]{:S(2)}) collective-permute-start(f32[520,128]{1,0:T(8,128)S(1)} %get-tuple-element.57.refs_2_), channel_id=1, source_target_pairs={{0,24},{4,28},{8,16},{12,20},{16,8},{20,12},{24,0},{28,4},{1,25},{... | collective-permute-start | bytes 798728 | tf_op jit(solution)/shard_map/ppermute | solution.py:50
  54.9 23.7 %collective-permute-start.7 = (f32[520,128]{1,0:T(8,128)S(1)}, f32[520,128]{1,0:T(8,128)S(1)}, u32[]{:S(2)}, u32[]{:S(2)}) collective-permute-start(f32[520,128]{1,0:T(8,128)S(1)} %get-tuple-element.57.refs_2_), channel_id=1, source_target_pairs={{0,16},{4,20},{8,24},{12,28},{16,0},{20,4},{24,8},{28,12},{1,17},{... | collective-permute-start | bytes 798728 | tf_op jit(solution)/shard_map/ppermute | solution.py:50
  55.8 26.2 %collective-permute-start.11 = (f32[520,128]{1,0:T(8,128)S(1)}, f32[520,128]{1,0:T(8,128)S(1)}, u32[]{:S(2)}, u32[]{:S(2)}) collective-permute-start(f32[520,128]{1,0:T(8,128)S(1)} %get-tuple-element.57.refs_2_), channel_id=1, source_target_pairs={{0,12},{4,8},{8,4},{12,0},{16,28},{20,24},{24,20},{28,16},{1,13},{... | collective-permute-start | bytes 798728 | tf_op jit(solution)/shard_map/ppermute | solution.py:50
  60.2 21.9 %collective-permute-start.10 = (f32[520,128]{1,0:T(8,128)S(1)}, f32[520,128]{1,0:T(8,128)S(1)}, u32[]{:S(2)}, u32[]{:S(2)}) collective-permute-start(f32[520,128]{1,0:T(8,128)S(1)} %get-tuple-element.57.refs_2_), channel_id=1, source_target_pairs={{0,8},{4,12},{8,0},{12,4},{16,24},{20,28},{24,16},{28,20},{1,9},{5... | collective-permute-start | bytes 798728 | tf_op jit(solution)/shard_map/ppermute | solution.py:50
  61.8 29.1 %copy-start.12 = (f32[520,128]{1,0:T(8,128)}, f32[520,128]{1,0:T(8,128)S(1)}, u32[]{:S(2)}) copy-start(f32[520,128]{1,0:T(8,128)S(1)} %collective-permute-done.9.refs_3_) | copy-start | bytes 798724
  78.6 9.3 %collective-permute-start.12 = (f32[520,128]{1,0:T(8,128)S(1)}, f32[520,128]{1,0:T(8,128)S(1)}, u32[]{:S(2)}, u32[]{:S(2)}) collective-permute-start(f32[520,128]{1,0:T(8,128)S(1)} %collective-permute-done.7.refs_6_), channel_id=1, source_target_pairs={{0,4},{4,0},{8,12},{12,8},{16,20},{20,16},{24,28},{28,24},{1,5},{5... | collective-permute-start | bytes 798728 | tf_op jit(solution)/shard_map/ppermute | solution.py:50
  80.2 10.7 %collective-permute-start.13 = (f32[520,128]{1,0:T(8,128)S(1)}, f32[520,128]{1,0:T(8,128)S(1)}, u32[]{:S(2)}, u32[]{:S(2)}) collective-permute-start(f32[520,128]{1,0:T(8,128)S(1)} %collective-permute-done.8.refs_8_), channel_id=1, source_target_pairs={{0,4},{4,0},{8,12},{12,8},{16,20},{20,16},{24,28},{28,24},{1,5},{5... | collective-permute-start | bytes 798728 | tf_op jit(solution)/shard_map/ppermute | solution.py:50
  114.7 3.9 %collective-permute-start.14 = (f32[8,128]{1,0:T(8,128)}, f32[8,128]{1,0:T(8,128)S(1)}, u32[]{:S(2)}, u32[]{:S(2)}) collective-permute-start(f32[8,128]{1,0:T(8,128)} %get-tuple-element.67), channel_id=1, source_target_pairs={{0,4},{4,0},{8,12},{12,8},{16,20},{20,16},{24,28},{28,24},{1,5},{5... | collective-permute-start | bytes 12296 | tf_op jit(solution)/shard_map/ppermute | solution.py:50
  119.2 3.6 %collective-permute-start.15 = (f32[8,128]{1,0:T(8,128)S(1)}, f32[8,128]{1,0:T(8,128)S(1)}, u32[]{:S(2)}, u32[]{:S(2)}) collective-permute-start(f32[8,128]{1,0:T(8,128)S(1)} %add.62), channel_id=1, source_target_pairs={{0,8},{4,12},{8,0},{12,4},{16,24},{20,28},{24,16},{28,20},{1,9},{5... | collective-permute-start | bytes 12296 | tf_op jit(solution)/shard_map/ppermute | solution.py:50
  122.9 4.5 %collective-permute-start.16 = (f32[8,128]{1,0:T(8,128)S(1)}, f32[8,128]{1,0:T(8,128)S(1)}, u32[]{:S(2)}, u32[]{:S(2)}) collective-permute-start(f32[8,128]{1,0:T(8,128)S(1)} %add.63), channel_id=1, source_target_pairs={{0,16},{4,20},{8,24},{12,28},{16,0},{20,4},{24,8},{28,12},{1,17},{... | collective-permute-start | bytes 12296 | tf_op jit(solution)/shard_map/ppermute | solution.py:50
  128.3 5.8 %collective-permute-start.19 = (f32[24,128]{1,0:T(8,128)S(1)}, f32[24,128]{1,0:T(8,128)S(1)}, u32[]{:S(2)}, u32[]{:S(2)}) collective-permute-start(f32[24,128]{1,0:T(8,128)S(1)} %get-tuple-element.70.refs_0_), channel_id=1, source_target_pairs={{0,3},{1,2},{2,1},{3,0},{4,7},{5,6},{6,5},{7,4},{8,11},{9,10},{10,... | collective-permute-start | bytes 36872 | tf_op jit(solution)/shard_map/ppermute | solution.py:50
  128.4 5.7 %collective-permute-start.18 = (f32[24,128]{1,0:T(8,128)S(1)}, f32[24,128]{1,0:T(8,128)S(1)}, u32[]{:S(2)}, u32[]{:S(2)}) collective-permute-start(f32[24,128]{1,0:T(8,128)S(1)} %get-tuple-element.70.refs_0_), channel_id=1, source_target_pairs={{0,2},{1,3},{2,0},{3,1},{4,6},{5,7},{6,4},{7,5},{8,10},{9,11},{10,... | collective-permute-start | bytes 36872 | tf_op jit(solution)/shard_map/ppermute | solution.py:50
  129.2 4.9 %collective-permute-start.17 = (f32[24,128]{1,0:T(8,128)S(1)}, f32[24,128]{1,0:T(8,128)S(1)}, u32[]{:S(2)}, u32[]{:S(2)}) collective-permute-start(f32[24,128]{1,0:T(8,128)S(1)} %get-tuple-element.70.refs_0_), channel_id=1, source_target_pairs={{0,1},{1,0},{2,3},{3,2},{4,5},{5,4},{6,7},{7,6},{8,9},{9,8},{10,11... | collective-permute-start | bytes 36872 | tf_op jit(solution)/shard_map/ppermute | solution.py:50
  (19 other events, 241.6 us)

commit v3 on v2

--- a/solution.py
+++ b/solution.py
@@ -14,12 +14,12 @@
 LANES_WIDE = 128
 VMEM = pl.BlockSpec(memory_space=pltpu.VMEM)
 SMEM = pl.BlockSpec(memory_space=pltpu.SMEM)
-ANY = pl.BlockSpec(memory_space=pl.ANY)
+HBM = pl.BlockSpec(memory_space=pltpu.HBM)
 PARAMS = pltpu.CompilerParams(vmem_limit_bytes=40 << 20)
 
 
+WHOLE = pltpu.CompilerParams(vmem_limit_bytes=60 << 20)
 SMALL = pltpu.CompilerParams(vmem_limit_bytes=8 << 20)
-WHOLE = pltpu.CompilerParams(vmem_limit_bytes=60 << 20)
 
 
 def takes(microseconds):
@@ -106,7 +106,7 @@
         for u in range(low_n // 128):
             acc[u, at, :] = acc[u, at, :] + sums[: 8 * SLOTS, u * 128 : (u + 1) * 128]
 
-    unroll = 4
+    unroll = 8
 
     @pl.loop(0, blocks // unroll)
     def _(step):
@@ -116,15 +116,21 @@
         for u in range(unroll):
             add(firsts[u], sums[u])
         acc_fit[...] = acc_fit[...] + sum(one[8 * SLOTS :] for one in sums)
-        for u in range(unroll):
-            block = step * unroll + u
-            more = (meta[FIRSTS + block + 1] - firsts[u]) // SLOTS
-
-            @pl.loop(0, more)
-            def _(turn_at):
-                first = firsts[u] + (turn_at + 1) * SLOTS
-                fit, res, hot = prepare(block)
-                add(first, group(first, block, fit, res, hot))
+        ends = firsts[1:] + [meta[FIRSTS + (step + 1) * unroll]]
+        more = sum((end - first) // SLOTS for first, end in zip(firsts, ends))
+
+        @pl.when(more > 0)
+        def _():
+            @pl.loop(0, unroll)
+            def _(u):
+                block = step * unroll + u
+                begin = meta[FIRSTS + block]
+
+                @pl.loop(0, (meta[FIRSTS + block + 1] - begin) // SLOTS)
+                def _(turn_at):
+                    first = begin + (turn_at + 1) * SLOTS
+                    fit, res, hot = prepare(block)
+                    add(first, group(first, block, fit, res, hot))
 
 
 def lane_blocks(where, meta, planes, rows, suppliers, own):
@@ -232,24 +238,15 @@
     )(scale, own, *parts)
 
 
-def forward_kernel(effects_all, lines, index, before, by_beta, week_square, lane_part, weight, *refs):
-    sources, tables = refs[:2], refs[2:-12]
-    out, squares, alpha_out, table, first, second, total, forward, rhs, value_out, landed, moved = refs[-12:]
-    columns = total.shape[0]
-    groups = weight.shape[0]
+def forward_kernel(effects_all, lines, index, before, by_beta, week_square, lane_part, weight, forward, rhs, *refs):
+    tables, (out, squares, alpha_out, table, first, second, total, landed) = refs[:-8], refs[-8:]
+    columns = out.shape[0]
     copies, at = [], 0
     for place, piece in enumerate(tables):
         here = table.at[pl.ds(at, piece.shape[0])]
         copies.append(pltpu.make_async_copy(piece, here, landed.at[place]))
         at += piece.shape[0]
-    parts = 4
-    wide = groups * 128 // parts
-    loads = []
-    for part in range(parts):
-        here = (slice(None), pl.ds(part * wide, wide))
-        for place, (source, held) in enumerate(zip(sources, (forward, rhs))):
-            loads.append(pltpu.make_async_copy(source.at[here], held.at[here], moved.at[place, part]))
-    for copy in [*copies, *loads]:
+    for copy in copies:
         copy.start()
     for copy in copies:
         copy.wait()
@@ -262,6 +259,7 @@
     alpha_out[...] = alpha
     scale = jnp.broadcast_to(by / alpha, (columns, 128))
     share = jnp.broadcast_to(by * alpha, (columns, 128))
+    groups = weight.shape[0]
     total[...] = jnp.zeros_like(total)
 
     def gather(group, store):
@@ -275,31 +273,22 @@
         for u in range(1, 128 // columns):
             picked = jnp.where(part == u, turned_over[u * columns : (u + 1) * columns], picked)
         at = pl.ds(pl.multiple_of(group * 128, 128), 128)
-        line = jnp.broadcast_to(weight[pl.ds(group, 1), :], (columns, 128))
-        value = (forward[:, at] + picked * line) * scale - share * rhs[:, at]
-        value_out[:, at] = value
+        by = jnp.broadcast_to(weight[pl.ds(group, 1), :], (columns, 128))
+        value = (forward[:, at] + picked * by) * scale - share * rhs[:, at]
+        out[:, at] = value
         total[...] = total[...] + value * value
 
     gather(0, first)
-    stores = []
-    for part in range(parts):
-        for copy in loads[2 * part : 2 * part + 2]:
-            copy.wait()
-
-        @pl.loop(part * groups // 2 // parts, (part + 1) * groups // 2 // parts)
-        def _(step):
-            gather(2 * step + 1, second)
-            finish(2 * step, first)
-            gather(jnp.minimum(2 * step + 2, groups - 1), first)
-            finish(2 * step + 1, second)
-
-        here = (slice(None), pl.ds(part * wide, wide))
-        stores.append(pltpu.make_async_copy(value_out.at[here], out.at[here], moved.at[2, part]))
-        stores[-1].start()
+
+    @pl.loop(0, groups // 2)
+    def _(step):
+        gather(2 * step + 1, second)
+        finish(2 * step, first)
+        gather(jnp.minimum(2 * step + 2, groups - 1), first)
+        finish(2 * step + 1, second)
+
     across = jnp.broadcast_to(jnp.sum(total[...], axis=1, keepdims=True), (columns, 128))
     squares[...] = jnp.concatenate([across] * (128 // columns), axis=0).T[0:8]
-    for copy in stores:
-        copy.wait()
 
 
 def forward_lanes(effects_all, lines, index, before, by_beta, week_square, lane_part, weight, forward, rhs, tables):
@@ -312,18 +301,16 @@
             jax.ShapeDtypeStruct((8, 128), jnp.float32),
             jax.ShapeDtypeStruct((columns, 1), jnp.float32),
         ],
-        in_specs=[SMEM] + [VMEM] * 5 + [ANY] * (2 + len(tables)),
-        out_specs=[ANY] + [VMEM] * 2,
+        in_specs=[SMEM] + [VMEM] * 7 + [HBM] * len(tables),
+        out_specs=[VMEM] * 3,
         scratch_shapes=[
             pltpu.VMEM((height, LANES_WIDE), jnp.float32),
             pltpu.VMEM((128, LANES_WIDE), jnp.float32),
             pltpu.VMEM((128, LANES_WIDE), jnp.float32),
             pltpu.VMEM((columns, 128), jnp.float32),
-            *[pltpu.VMEM((columns, rows), jnp.float32)] * 3,
             pltpu.SemaphoreType.DMA((len(tables),)),
-            pltpu.SemaphoreType.DMA((3, 4)),
-        ],
-        compiler_params=WHOLE,
+        ],
+        compiler_params=PARAMS,
         cost_estimate=takes(18),
         name="forward_lanes",
     )(index, before, by_beta, week_square, lane_part, weight, forward, rhs, *tables)
@@ -368,7 +355,7 @@
             jax.ShapeDtypeStruct((suppliers + 16, 8), jnp.int32),
             jax.ShapeDtypeStruct((1, suppliers), jnp.int32),
         ],
-        in_specs=[ANY] * 7,
+        in_specs=[HBM] * 7,
         out_specs=[VMEM] * 3,
         scratch_shapes=held_for(sources),
         compiler_params=WHOLE,
@@ -435,7 +422,7 @@
             by_week[u, at, wide] = by_week[u, at, wide] + part
         by_sign[at, 0:16] = by_sign[at, 0:16] + got[1]
 
-    unroll = 4
+    unroll = 8
 
     @pl.loop(0, blocks // unroll)
     def _(step):
@@ -445,14 +432,21 @@
         for u in range(unroll):
             add(begin[u], got[u])
         fit_week[:, 0:weeks] = fit_week[:, 0:weeks] + sum(one[0][8:] for one in got)
-        for u in range(unroll):
-            block = step * unroll + u
-
-            @pl.loop(0, (firsts[0, block + 1] - begin[u]) // 8)
-            def _(turn_at):
-                first = begin[u] + (turn_at + 1) * 8
-                fit, res, both, hot = prepare(block)
-                add(first, group(first, block, fit, res, both, hot))
+        ends = begin[1:] + [firsts[0, (step + 1) * unroll]]
+        more = sum((end - first) // 8 for first, end in zip(begin, ends))
+
+        @pl.when(more > 0)
+        def _():
+            @pl.loop(0, unroll)
+            def _(u):
+                block = step * unroll + u
+                start = firsts[0, block]
+
+                @pl.loop(0, (firsts[0, block + 1] - start) // 8)
+                def _(turn_at):
+                    first = start + (turn_at + 1) * 8
+                    fit, res, both, hot = prepare(block)
+                    add(first, group(first, block, fit, res, both, hot))
 
     positive = signs[...] == 1
     sign = (2 * signs[...] - 1).astype(jnp.float32).astype(jnp.bfloat16)
@@ -480,7 +474,7 @@
             jax.ShapeDtypeStruct((columns, suppliers), jnp.float32),
             jax.ShapeDtypeStruct((-(-weeks // 128) * columns, 128), jnp.float32),
         ],
-        in_specs=[SMEM] + [ANY] * 6,
+        in_specs=[SMEM] + [HBM] * 6,
         out_specs=[VMEM] * 2,
         scratch_shapes=held_for(sources)
         + [
@@ -515,7 +509,7 @@
         both = jnp.dot(by_effect, hot, preferred_element_type=jnp.float32)
         forward[:, at] = jnp.broadcast_to(row_of(weight, row), shape) * (both[:columns] + both[columns:])
 
-    unroll = 4
+    unroll = 8
 
     @pl.loop(0, blocks // unroll)
     def _(step):
@@ -530,7 +524,7 @@
     return pl.pallas_call(
         base_kernel,
         out_shape=[shape, shape, jax.ShapeDtypeStruct((8, 128), jnp.float32)],
-        in_specs=[ANY] * 8,
+        in_specs=[HBM] * 8,
         out_specs=[VMEM] * 3,
         scratch_shapes=held_for(sources),
         compiler_params=PARAMS,
@@ -560,7 +554,8 @@
     square = jnp.broadcast_to(residual[0:1, :], (128, 128)).T[0:columns, 0:1]
     beta_next = jnp.sqrt(square / count + EPS)
     step = alpha[...] * beta_first[...] / (alpha[...] * alpha[...] + beta_next * beta_next)
-    step_out[...] = step
+    across = jnp.concatenate([jnp.broadcast_to(step, (columns, 128))] * (128 // columns), axis=0)
+    step_out[...] = across.T[0:1, 0:columns]
     inverse[...] = 1.0 / beta_next
     scale = step / (alpha[...] * beta_first[...])
     rows = []
@@ -576,7 +571,11 @@
     column = jax.ShapeDtypeStruct(alpha.shape, jnp.float32)
     return pl.pallas_call(
         functools.partial(effect_sums_kernel, count),
-        out_shape=[jax.ShapeDtypeStruct((lines // 8 * 8 + 8, 128), jnp.float32), column, column],
+        out_shape=[
+            jax.ShapeDtypeStruct((lines // 8 * 8 + 8, 128), jnp.float32),
+            jax.ShapeDtypeStruct((1, alpha.shape[0]), jnp.float32),
+            column,
+        ],
         in_specs=[VMEM] * 5,
         out_specs=[VMEM] * 3,
         compiler_params=SMALL,
@@ -697,7 +696,6 @@
     )
 
     forward, rhs, token = forward_base((*held, effects), near[min(1, len(near) - 1)][:8])
-    near[n_ship // 2 :], token = lax.optimization_barrier((near[n_ship // 2 :], token))
     tables = all_tables(near, n_ship)
 
     quarter = lane_own * columns // LANES_WIDE
@@ -717,7 +715,7 @@
     u_next = residual * inverse
     spread_supplier, spread_lane = spreads(columns * n_boot, lane_own // 128, effects)
     spread_supplier, spread_lane = spread_supplier.reshape(-1), spread_lane.reshape(-1)
-    return (v_supplier, v_lane, v_week, u_next, step_size[:, 0], spread_supplier, spread_lane)
+    return (v_supplier, v_lane, v_week, u_next, step_size.reshape(-1), spread_supplier, spread_lane)
 
 
 def solution(mesh):

time: 136 us -> 114 us (0.84)
  Pallas kernels: 58.9 us -> 46.3 us
  other arithmetic: 12.6 us -> 7.75 us
  local copies, waits for them, and re-layouts: 4.4 us -> 0.34 us
    pallas_call x2, Pallas kernels: 14.8 us -> 10.3 us  [lane_blocks(): pl.pallas_call(functools.partial(lane_blocks_kernel, low_n, rows), out_sh...]
    pallas_call x1, Pallas kernels: 22.1 us -> 18 us  [forward_lanes(): pl.pallas_call(functools.partial(forward_kernel, effects_all, lines), out...]
    unnamed x46 -> x22, local copies, waits for them, and re-layouts: 4.12 us -> 0.06 us
    pallas_call x1, Pallas kernels: 8.77 us -> 6.43 us  [forward_base(): pl.pallas_call(base_kernel, out_shape=[shape, shape, jax.ShapeDtypeStruct...]
    pallas_call x1, Pallas kernels: 9.11 us -> 6.91 us  [own_sums(): pl.pallas_call(functools.partial(own_sums_kernel, weeks), out_shape=[jax....]
    mul x1, other arithmetic: 3.12 us -> 1.53 us  [on_device(): u_next = residual * inverse]
  transfers between devices with their start and end apart: 20 -> 20, of which waited for: 10 -> 10; matrix products, arithmetic and copies ran while one was open for 7% -> 5% of each run, Pallas kernels for 24% -> 21%
where the time goes in v3:
time: 114 us
  Pallas kernels  46.3 us (41%)
  waiting for transfers between devices  31.4 us (28%)
  starting transfers between devices  26.9 us (24%)
  other arithmetic  7.75 us (7%)
    ppermute x18, waiting for transfers between devices, swap(): return lax.ppermute(value, axis, [(i, i ^ step) for i in range(size)])  30.6 us
    ppermute x18, starting transfers between devices, swap(): return lax.ppermute(value, axis, [(i, i ^ step) for i in range(size)])  21.3 us
    pallas_call x1, Pallas kernels, forward_lanes(): pl.pallas_call(functools.partial(forward_kernel, effects_all, lines), out...  18 us
    pallas_call x2, Pallas kernels, lane_blocks(): pl.pallas_call(functools.partial(lane_blocks_kernel, low_n, rows), out_sh...  10.3 us
    pallas_call x1, Pallas kernels, own_sums(): pl.pallas_call(functools.partial(own_sums_kernel, weeks), out_shape=[jax....  6.91 us
    pallas_call x1, Pallas kernels, forward_base(): pl.pallas_call(base_kernel, out_shape=[shape, shape, jax.ShapeDtypeStruct...  6.43 us
    ppermute x2, starting transfers between devices, on_device(): got.append(lax.ppermute(planes, ('ship', 'boot'), pairs))  5.68 us
  transfers between devices with their start and end apart: 20, of which 10 were waited for; matrix products, arithmetic and copies ran while one was open for 5% of the time, Pallas kernels for 21%

profile of v3, /device:TPU:0, one launch (start us, length us, event | category | flops | bytes accessed | tf_op | source)
XLA Modules:
  0.0 113.8 jit_solution(8892260404039707513)
XLA Ops:
  0.6 1.9 %message.1 = (f32[424,128]{1,0:T(8,128)}, s32[144,8]{1,0:T(8,128)}, s32[1,128]{1,0:T(1,128)}) custom-call(f32[128,128]{1,0:T(8,128)} %bitcast.25, f32[128,128]{1,0:T(8,128)} %bitcast.28, f32[128,128]{1,0:T(8,128)} %bitcast.21, s32[128,128]{1,0:T(8,128)} %bitcast.34, s32[128,128]{1,0:T(8,128)} %bitcast.36, s32[1,128]{1,0:T(1,128)} %refs_5_.3, s32[32,128]{1,0:T(8,128)} %refs_5_.5), custom_call_target="tpu_custom_call" | custom-call | bytes 7200000 | tf_op jit(solution)/shard_map/message/pallas_call | solution.py:351
  2.5 4.1 %collective-permute-start.1 = (f32[424,128]{1,0:T(8,128)}, f32[424,128]{1,0:T(8,128)S(1)}, u32[]{:S(2)}, u32[]{:S(2)}) collective-permute-start(f32[424,128]{1,0:T(8,128)} %get-tuple-element.40), channel_id=1, source_target_pairs={{0,16},{1,24},{2,20},{3,28},{4,17},{5,25},{6,21},{7,29},{8,18},{9,... | collective-permute-start | bytes 651272 | tf_op jit(solution)/shard_map/ppermute | solution.py:650
  6.6 1.6 %collective-permute-start = (f32[424,128]{1,0:T(8,128)}, f32[424,128]{1,0:T(8,128)S(1)}, u32[]{:S(2)}, u32[]{:S(2)}) collective-permute-start(f32[424,128]{1,0:T(8,128)} %get-tuple-element.40), channel_id=1, source_target_pairs={{0,0},{1,8},{2,4},{3,12},{4,1},{5,9},{6,5},{7,13},{8,2},{9,10},{10... | collective-permute-start | bytes 651272 | tf_op jit(solution)/shard_map/ppermute | solution.py:650
  9.2 6.9 %own_sums.1 = (f32[32,128]{1,0:T(8,128)}, f32[96,128]{1,0:T(8,128)}) custom-call(s32[1,128]{1,0:T(1,128)} %get-tuple-element.37.firsts, f32[128,128]{1,0:T(8,128)} %bitcast.26, f32[128,128]{1,0:T(8,128)} %bitcast.29, f32[128,128]{1,0:T(8,128)} %bitcast.22, s32[128,128]{1,0:T(8,128)} %bitcast.31, s32[144,8]{1,0:T(8,128)} %get-tuple-element.38.refs_4_, ...), custom_call_target="tpu_custom_call" | custom-call | bytes 25200000 | tf_op jit(solution)/shard_map/own_sums/pallas_call | solution.py:471
  18.4 3.3 %collective-permute-start.2 = (f32[160,128]{1,0:T(8,128)S(1)}, f32[160,128]{1,0:T(8,128)S(1)}, u32[]{:S(2)}, u32[]{:S(2)}) collective-permute-start(f32[160,128]{1,0:T(8,128)S(1)} %pad_maximum_fusion.1), channel_id=1, source_target_pairs={{0,4},{4,0},{8,12},{12,8},{16,20},{20,16},{24,28},{28,24},{1,5},{5... | collective-permute-start | bytes 245768 | tf_op jit(solution)/shard_map/ppermute | solution.py:50
  21.7 5.2 %lane_blocks.2 = (f32[2,1088,128]{2,1,0:T(8,128)S(1)}, f32[8,256]{1,0:T(8,128)S(1)}) custom-call(s32[2]{0:T(128)S(1)} %pad_add_fusion.where, s32[1024]{0:T(1024)S(1)} %convert_bitcast_fusion.1.meta, f32[424,128]{1,0:T(8,128)S(1)} %collective-permute-done.planes), custom_call_target="tpu_custom_call" | custom-call | bytes 28800000 | tf_op jit(solution)/shard_map/lane_blocks/pallas_call | solution.py:138
  27.7 2.5 %collective-permute-start.3 = (f32[224,128]{1,0:T(8,128)S(1)}, f32[224,128]{1,0:T(8,128)S(1)}, u32[]{:S(2)}, u32[]{:S(2)}) collective-permute-start(f32[224,128]{1,0:T(8,128)S(1)} %pad_maximum_fusion), channel_id=1, source_target_pairs={{0,8},{4,12},{8,0},{12,4},{16,24},{20,28},{24,16},{28,20},{1,9},{5... | collective-permute-start | bytes 344072 | tf_op jit(solution)/shard_map/ppermute | solution.py:50
  30.2 5.1 %lane_blocks.3 = (f32[2,1088,128]{2,1,0:T(8,128)S(1)}, f32[8,256]{1,0:T(8,128)S(1)}) custom-call(s32[2]{0:T(128)S(1)} %pad_add_fusion.where, s32[1024]{0:T(1024)S(1)} %convert_bitcast_fusion.meta, f32[424,128]{1,0:T(8,128)S(1)} %collective-permute-done.1.planes), custom_call_target="tpu_custom_call" | custom-call | bytes 28800000 | tf_op jit(solution)/shard_map/lane_blocks/pallas_call | solution.py:138
  36.9 1.7 %collective-permute-done.5 = f32[64,2048]{1,0:T(8,128)S(1)} collective-permute-done((f32[64,2048]{1,0:T(8,128)S(1)}, f32[64,2048]{1,0:T(8,128)S(1)}, u32[]{:S(2)}, u32[]{:S(2)}) %collective-permute-start.5) | collective-permute-done | bytes 524320 | tf_op jit(solution)/shard_map/ppermute | solution.py:50
  38.8 1.8 %collective-permute-start.4 = (f32[96,128]{1,0:T(8,128)S(1)}, f32[96,128]{1,0:T(8,128)S(1)}, u32[]{:S(2)}, u32[]{:S(2)}) collective-permute-start(f32[96,128]{1,0:T(8,128)S(1)} %slice_add_fusion.1), channel_id=1, source_target_pairs={{0,16},{4,20},{8,24},{12,28},{16,0},{20,4},{24,8},{28,12},{1,17},{... | collective-permute-start | bytes 147464 | tf_op jit(solution)/shard_map/ppermute | solution.py:50
  40.7 3.3 %collective-permute-done.4 = f32[96,128]{1,0:T(8,128)S(1)} collective-permute-done((f32[96,128]{1,0:T(8,128)S(1)}, f32[96,128]{1,0:T(8,128)S(1)}, u32[]{:S(2)}, u32[]{:S(2)}) %collective-permute-start.4) | collective-permute-done | bytes 49184 | tf_op jit(solution)/shard_map/ppermute | solution.py:50
  44.0 3.0 %collective-permute-done.6.refs_2_ = f32[32,2048]{1,0:T(8,128)S(1)} collective-permute-done((f32[32,2048]{1,0:T(8,128)S(1)}, f32[32,2048]{1,0:T(8,128)S(1)}, u32[]{:S(2)}, u32[]{:S(2)}) %collective-permute-start.6) | collective-permute-done | bytes 262176 | tf_op jit(solution)/shard_map/ppermute | solution.py:50
  47.4 1.5 %collective-permute-start.10 = (f32[520,128]{1,0:T(8,128)S(1)}, f32[520,128]{1,0:T(8,128)S(1)}, u32[]{:S(2)}, u32[]{:S(2)}) collective-permute-start(f32[520,128]{1,0:T(8,128)S(1)} %get-tuple-element.54.refs_0_), channel_id=1, source_target_pairs={{0,16},{4,20},{8,24},{12,28},{16,0},{20,4},{24,8},{28,12},{1,17},{... | collective-permute-start | bytes 798728 | tf_op jit(solution)/shard_map/ppermute | solution.py:50
  49.1 2.4 %collective-permute-start.9 = (f32[520,128]{1,0:T(8,128)S(1)}, f32[520,128]{1,0:T(8,128)S(1)}, u32[]{:S(2)}, u32[]{:S(2)}) collective-permute-start(f32[520,128]{1,0:T(8,128)S(1)} %get-tuple-element.54.refs_0_), channel_id=1, source_target_pairs={{0,12},{4,8},{8,4},{12,0},{16,28},{20,24},{24,20},{28,16},{1,13},{... | collective-permute-start | bytes 798728 | tf_op jit(solution)/shard_map/ppermute | solution.py:50
  52.1 1.4 %collective-permute-start.7 = (f32[520,128]{1,0:T(8,128)S(1)}, f32[520,128]{1,0:T(8,128)S(1)}, u32[]{:S(2)}, u32[]{:S(2)}) collective-permute-start(f32[520,128]{1,0:T(8,128)S(1)} %get-tuple-element.54.refs_0_), channel_id=1, source_target_pairs={{0,4},{4,0},{8,12},{12,8},{16,20},{20,16},{24,28},{28,24},{1,5},{5... | collective-permute-start | bytes 798728 | tf_op jit(solution)/shard_map/ppermute | solution.py:50
  53.5 5.2 %collective-permute-done.12.refs_6_ = f32[520,128]{1,0:T(8,128)S(1)} collective-permute-done((f32[520,128]{1,0:T(8,128)S(1)}, f32[520,128]{1,0:T(8,128)S(1)}, u32[]{:S(2)}, u32[]{:S(2)}) %collective-permute-start.12) | collective-permute-done | bytes 266272 | tf_op jit(solution)/shard_map/ppermute | solution.py:50
  58.7 13.0 %collective-permute-done.10.refs_4_ = f32[520,128]{1,0:T(8,128)S(1)} collective-permute-done((f32[520,128]{1,0:T(8,128)S(1)}, f32[520,128]{1,0:T(8,128)S(1)}, u32[]{:S(2)}, u32[]{:S(2)}) %collective-permute-start.10) | collective-permute-done | bytes 266272 | tf_op jit(solution)/shard_map/ppermute | solution.py:50
  72.2 6.4 %forward_base.1 = (f32[32,16384]{1,0:T(8,128)S(1)}, f32[32,16384]{1,0:T(8,128)S(1)}, f32[8,128]{1,0:T(8,128)S(1)}) custom-call(f32[128,128]{1,0:T(8,128)S(1)} %bitcast.27, f32[128,128]{1,0:T(8,128)S(1)} %bitcast.30, f32[128,128]{1,0:T(8,128)S(1)} %bitcast.23, s32[128,128]{1,0:T(8,128)S(1)} %bitcast.32, s32[144,8]{1,0:T(8,128)S(1)} %copy-done.3, ...), custom_call_target="tpu_custom_call" | custom-call | bytes 28800000 | tf_op jit(solution)/shard_map/forward_base/pallas_call | solution.py:524
  78.6 18.0 %forward_lanes.1 = (f32[32,16384]{1,0:T(8,128)S(1)}, f32[8,128]{1,0:T(8,128)S(1)}, f32[32,1]{1,0:T(8,128)S(1)}) custom-call(s32[16384]{0:T(1024)S(1)} %get-tuple-element.72.index, f32[8,128]{1,0:T(8,128)S(1)} %get-tuple-element.55.before, f32[32,1]{1,0:T(8,128)S(1)} %get-tuple-element.78.by_beta, f32[32,1]{1,0:T(8,128)S(1)} %get-tuple-element.77.week_square, ...), custom_call_target="tpu_custom_call" | custom-call | bytes 64800000 | tf_op jit(solution)/shard_map/forward_lanes/pallas_call | solution.py:297
  96.8 1.8 %collective-permute-start.14 = (f32[8,128]{1,0:T(8,128)S(1)}, f32[8,128]{1,0:T(8,128)S(1)}, u32[]{:S(2)}, u32[]{:S(2)}) collective-permute-start(f32[8,128]{1,0:T(8,128)S(1)} %get-tuple-element.61), channel_id=1, source_target_pairs={{0,4},{4,0},{8,12},{12,8},{16,20},{20,16},{24,28},{28,24},{1,5},{5... | collective-permute-start | bytes 12296 | tf_op jit(solution)/shard_map/ppermute | solution.py:50
  100.5 1.7 %collective-permute-start.15 = (f32[8,128]{1,0:T(8,128)S(1)}, f32[8,128]{1,0:T(8,128)S(1)}, u32[]{:S(2)}, u32[]{:S(2)}) collective-permute-start(f32[8,128]{1,0:T(8,128)S(1)} %add.62), channel_id=1, source_target_pairs={{0,8},{4,12},{8,0},{12,4},{16,24},{20,28},{24,16},{28,20},{1,9},{5... | collective-permute-start | bytes 12296 | tf_op jit(solution)/shard_map/ppermute | solution.py:50
  104.1 2.0 %collective-permute-start.16 = (f32[8,128]{1,0:T(8,128)S(1)}, f32[8,128]{1,0:T(8,128)S(1)}, u32[]{:S(2)}, u32[]{:S(2)}) collective-permute-start(f32[8,128]{1,0:T(8,128)S(1)} %add.63), channel_id=1, source_target_pairs={{0,16},{4,20},{8,24},{12,28},{16,0},{20,4},{24,8},{28,12},{1,17},{... | collective-permute-start | bytes 12296 | tf_op jit(solution)/shard_map/ppermute | solution.py:50
  106.8 1.8 %collective-permute-done.16 = f32[8,128]{1,0:T(8,128)S(1)} collective-permute-done((f32[8,128]{1,0:T(8,128)S(1)}, f32[8,128]{1,0:T(8,128)S(1)}, u32[]{:S(2)}, u32[]{:S(2)}) %collective-permute-start.16) | collective-permute-done | bytes 4128 | tf_op jit(solution)/shard_map/ppermute | solution.py:50
  111.4 1.5 %broadcast_multiply_fusion = f32[32,16384]{1,0:T(8,128)} fusion(f32[32,16384]{1,0:T(8,128)S(1)} %get-tuple-element.60, f32[32]{0:T(128)S(1)} %reduce.1), kind=kLoop, calls=%fused_computation | loop fusion | flops 524288 | bytes 4194432 | tf_op jit(solution)/shard_map/mul | solution.py:715
  (85 shorter events, 15.6 us)
Async XLA Ops:
  2.5 15.0 %collective-permute-start.1 = (f32[424,128]{1,0:T(8,128)}, f32[424,128]{1,0:T(8,128)S(1)}, u32[]{:S(2)}, u32[]{:S(2)}) collective-permute-start(f32[424,128]{1,0:T(8,128)} %get-tuple-element.40), channel_id=1, source_target_pairs={{0,16},{1,24},{2,20},{3,28},{4,17},{5,25},{6,21},{7,29},{8,18},{9,... | collective-permute-start | bytes 651272 | tf_op jit(solution)/shard_map/ppermute | solution.py:650
  6.6 10.9 %collective-permute-start = (f32[424,128]{1,0:T(8,128)}, f32[424,128]{1,0:T(8,128)S(1)}, u32[]{:S(2)}, u32[]{:S(2)}) collective-permute-start(f32[424,128]{1,0:T(8,128)} %get-tuple-element.40), channel_id=1, source_target_pairs={{0,0},{1,8},{2,4},{3,12},{4,1},{5,9},{6,5},{7,13},{8,2},{9,10},{10... | collective-permute-start | bytes 651272 | tf_op jit(solution)/shard_map/ppermute | solution.py:650
  18.4 8.5 %collective-permute-start.2 = (f32[160,128]{1,0:T(8,128)S(1)}, f32[160,128]{1,0:T(8,128)S(1)}, u32[]{:S(2)}, u32[]{:S(2)}) collective-permute-start(f32[160,128]{1,0:T(8,128)S(1)} %pad_maximum_fusion.1), channel_id=1, source_target_pairs={{0,4},{4,0},{8,12},{12,8},{16,20},{20,16},{24,28},{28,24},{1,5},{5... | collective-permute-start | bytes 245768 | tf_op jit(solution)/shard_map/ppermute | solution.py:50
  27.7 7.6 %collective-permute-start.3 = (f32[224,128]{1,0:T(8,128)S(1)}, f32[224,128]{1,0:T(8,128)S(1)}, u32[]{:S(2)}, u32[]{:S(2)}) collective-permute-start(f32[224,128]{1,0:T(8,128)S(1)} %pad_maximum_fusion), channel_id=1, source_target_pairs={{0,8},{4,12},{8,0},{12,4},{16,24},{20,28},{24,16},{28,20},{1,9},{5... | collective-permute-start | bytes 344072 | tf_op jit(solution)/shard_map/ppermute | solution.py:50
  36.6 35.6 %copy-start = (f32[16384]{0:T(1024)S(1)}, f32[16384]{0:T(1024)}, u32[]{:S(2)}) copy-start(f32[16384]{0:T(1024)} %param.13) | copy-start | bytes 196612
  36.6 35.5 %copy-start.1 = (f32[16384]{0:T(1024)S(1)}, f32[16384]{0:T(1024)}, u32[]{:S(2)}) copy-start(f32[16384]{0:T(1024)} %param.11) | copy-start | bytes 196612
  36.6 35.5 %copy-start.2 = (f32[16384]{0:T(1024)S(1)}, f32[16384]{0:T(1024)}, u32[]{:S(2)}) copy-start(f32[16384]{0:T(1024)} %param.12) | copy-start | bytes 196612
  36.6 35.5 %copy-start.3 = (s32[144,8]{1,0:T(8,128)S(1)}, s32[144,8]{1,0:T(8,128)}, u32[]{:S(2)}) copy-start(s32[144,8]{1,0:T(8,128)} %get-tuple-element.38.refs_4_) | copy-start | bytes 13828
  36.6 2.0 %collective-permute-start.5 = (f32[64,2048]{1,0:T(8,128)S(1)}, f32[64,2048]{1,0:T(8,128)S(1)}, u32[]{:S(2)}, u32[]{:S(2)}) collective-permute-start(f32[64,2048]{1,0:T(8,128)S(1)} %get-tuple-element.52), channel_id=1, source_target_pairs={{0,1},{1,0},{2,3},{3,2},{4,5},{5,4},{6,7},{7,6},{8,9},{9,8},{10,11... | collective-permute-start | bytes 1572872 | tf_op jit(solution)/shard_map/ppermute | solution.py:50
  38.7 8.4 %collective-permute-start.6 = (f32[32,2048]{1,0:T(8,128)S(1)}, f32[32,2048]{1,0:T(8,128)S(1)}, u32[]{:S(2)}, u32[]{:S(2)}) collective-permute-start(f32[32,2048]{1,0:T(8,128)S(1)} %get-tuple-element.69), channel_id=1, source_target_pairs={{0,2},{1,3},{2,0},{3,1},{4,6},{5,7},{6,4},{7,5},{8,10},{9,11},{10,... | collective-permute-start | bytes 786440 | tf_op jit(solution)/shard_map/ppermute | solution.py:50
  38.8 5.3 %collective-permute-start.4 = (f32[96,128]{1,0:T(8,128)S(1)}, f32[96,128]{1,0:T(8,128)S(1)}, u32[]{:S(2)}, u32[]{:S(2)}) collective-permute-start(f32[96,128]{1,0:T(8,128)S(1)} %slice_add_fusion.1), channel_id=1, source_target_pairs={{0,16},{4,20},{8,24},{12,28},{16,0},{20,4},{24,8},{28,12},{1,17},{... | collective-permute-start | bytes 147464 | tf_op jit(solution)/shard_map/ppermute | solution.py:50
  47.4 11.3 %collective-permute-start.12 = (f32[520,128]{1,0:T(8,128)S(1)}, f32[520,128]{1,0:T(8,128)S(1)}, u32[]{:S(2)}, u32[]{:S(2)}) collective-permute-start(f32[520,128]{1,0:T(8,128)S(1)} %get-tuple-element.54.refs_0_), channel_id=1, source_target_pairs={{0,24},{4,28},{8,16},{12,20},{16,8},{20,12},{24,0},{28,4},{1,25},{... | collective-permute-start | bytes 798728 | tf_op jit(solution)/shard_map/ppermute | solution.py:50
  47.4 24.3 %collective-permute-start.10 = (f32[520,128]{1,0:T(8,128)S(1)}, f32[520,128]{1,0:T(8,128)S(1)}, u32[]{:S(2)}, u32[]{:S(2)}) collective-permute-start(f32[520,128]{1,0:T(8,128)S(1)} %get-tuple-element.54.refs_0_), channel_id=1, source_target_pairs={{0,16},{4,20},{8,24},{12,28},{16,0},{20,4},{24,8},{28,12},{1,17},{... | collective-permute-start | bytes 798728 | tf_op jit(solution)/shard_map/ppermute | solution.py:50
  49.1 29.5 %collective-permute-start.9 = (f32[520,128]{1,0:T(8,128)S(1)}, f32[520,128]{1,0:T(8,128)S(1)}, u32[]{:S(2)}, u32[]{:S(2)}) collective-permute-start(f32[520,128]{1,0:T(8,128)S(1)} %get-tuple-element.54.refs_0_), channel_id=1, source_target_pairs={{0,12},{4,8},{8,4},{12,0},{16,28},{20,24},{24,20},{28,16},{1,13},{... | collective-permute-start | bytes 798728 | tf_op jit(solution)/shard_map/ppermute | solution.py:50
  51.5 27.1 %collective-permute-start.8 = (f32[520,128]{1,0:T(8,128)S(1)}, f32[520,128]{1,0:T(8,128)S(1)}, u32[]{:S(2)}, u32[]{:S(2)}) collective-permute-start(f32[520,128]{1,0:T(8,128)S(1)} %get-tuple-element.54.refs_0_), channel_id=1, source_target_pairs={{0,8},{4,12},{8,0},{12,4},{16,24},{20,28},{24,16},{28,20},{1,9},{5... | collective-permute-start | bytes 798728 | tf_op jit(solution)/shard_map/ppermute | solution.py:50
  52.1 20.0 %collective-permute-start.7 = (f32[520,128]{1,0:T(8,128)S(1)}, f32[520,128]{1,0:T(8,128)S(1)}, u32[]{:S(2)}, u32[]{:S(2)}) collective-permute-start(f32[520,128]{1,0:T(8,128)S(1)} %get-tuple-element.54.refs_0_), channel_id=1, source_target_pairs={{0,4},{4,0},{8,12},{12,8},{16,20},{20,16},{24,28},{28,24},{1,5},{5... | collective-permute-start | bytes 798728 | tf_op jit(solution)/shard_map/ppermute | solution.py:50
  58.7 20.0 %collective-permute-start.13 = (f32[520,128]{1,0:T(8,128)S(1)}, f32[520,128]{1,0:T(8,128)S(1)}, u32[]{:S(2)}, u32[]{:S(2)}) collective-permute-start(f32[520,128]{1,0:T(8,128)S(1)} %collective-permute-done.12.refs_6_), channel_id=1, source_target_pairs={{0,4},{4,0},{8,12},{12,8},{16,20},{20,16},{24,28},{28,24},{1,5},{5... | collective-permute-start | bytes 798728 | tf_op jit(solution)/shard_map/ppermute | solution.py:50
  71.7 6.9 %collective-permute-start.11 = (f32[520,128]{1,0:T(8,128)S(1)}, f32[520,128]{1,0:T(8,128)S(1)}, u32[]{:S(2)}, u32[]{:S(2)}) collective-permute-start(f32[520,128]{1,0:T(8,128)S(1)} %collective-permute-done.10.refs_4_), channel_id=1, source_target_pairs={{0,4},{4,0},{8,12},{12,8},{16,20},{20,16},{24,28},{28,24},{1,5},{5... | collective-permute-start | bytes 798728 | tf_op jit(solution)/shard_map/ppermute | solution.py:50
  96.8 3.7 %collective-permute-start.14 = (f32[8,128]{1,0:T(8,128)S(1)}, f32[8,128]{1,0:T(8,128)S(1)}, u32[]{:S(2)}, u32[]{:S(2)}) collective-permute-start(f32[8,128]{1,0:T(8,128)S(1)} %get-tuple-element.61), channel_id=1, source_target_pairs={{0,4},{4,0},{8,12},{12,8},{16,20},{20,16},{24,28},{28,24},{1,5},{5... | collective-permute-start | bytes 12296 | tf_op jit(solution)/shard_map/ppermute | solution.py:50
  100.5 3.6 %collective-permute-start.15 = (f32[8,128]{1,0:T(8,128)S(1)}, f32[8,128]{1,0:T(8,128)S(1)}, u32[]{:S(2)}, u32[]{:S(2)}) collective-permute-start(f32[8,128]{1,0:T(8,128)S(1)} %add.62), channel_id=1, source_target_pairs={{0,8},{4,12},{8,0},{12,4},{16,24},{20,28},{24,16},{28,20},{1,9},{5... | collective-permute-start | bytes 12296 | tf_op jit(solution)/shard_map/ppermute | solution.py:50
  104.1 4.5 %collective-permute-start.16 = (f32[8,128]{1,0:T(8,128)S(1)}, f32[8,128]{1,0:T(8,128)S(1)}, u32[]{:S(2)}, u32[]{:S(2)}) collective-permute-start(f32[8,128]{1,0:T(8,128)S(1)} %add.63), channel_id=1, source_target_pairs={{0,16},{4,20},{8,24},{12,28},{16,0},{20,4},{24,8},{28,12},{1,17},{... | collective-permute-start | bytes 12296 | tf_op jit(solution)/shard_map/ppermute | solution.py:50
  109.4 3.5 %collective-permute-start.19 = (f32[24,128]{1,0:T(8,128)S(1)}, f32[24,128]{1,0:T(8,128)S(1)}, u32[]{:S(2)}, u32[]{:S(2)}) collective-permute-start(f32[24,128]{1,0:T(8,128)S(1)} %get-tuple-element.64.refs_0_), channel_id=1, source_target_pairs={{0,3},{1,2},{2,1},{3,0},{4,7},{5,6},{6,5},{7,4},{8,11},{9,10},{10,... | collective-permute-start | bytes 36872 | tf_op jit(solution)/shard_map/ppermute | solution.py:50
  109.4 3.8 %collective-permute-start.18 = (f32[24,128]{1,0:T(8,128)S(1)}, f32[24,128]{1,0:T(8,128)S(1)}, u32[]{:S(2)}, u32[]{:S(2)}) collective-permute-start(f32[24,128]{1,0:T(8,128)S(1)} %get-tuple-element.64.refs_0_), channel_id=1, source_target_pairs={{0,2},{1,3},{2,0},{3,1},{4,6},{5,7},{6,4},{7,5},{8,10},{9,11},{10,... | collective-permute-start | bytes 36872 | tf_op jit(solution)/shard_map/ppermute | solution.py:50
  110.2 2.9 %collective-permute-start.17 = (f32[24,128]{1,0:T(8,128)S(1)}, f32[24,128]{1,0:T(8,128)S(1)}, u32[]{:S(2)}, u32[]{:S(2)}) collective-permute-start(f32[24,128]{1,0:T(8,128)S(1)} %get-tuple-element.64.refs_0_), channel_id=1, source_target_pairs={{0,1},{1,0},{2,3},{3,2},{4,5},{5,4},{6,7},{7,6},{8,9},{9,8},{10,11... | collective-permute-start | bytes 36872 | tf_op jit(solution)/shard_map/ppermute | solution.py:50
  (7 other events, 165.8 us)

commit v4 on v3

--- a/solution.py
+++ b/solution.py
@@ -106,7 +106,7 @@
         for u in range(low_n // 128):
             acc[u, at, :] = acc[u, at, :] + sums[: 8 * SLOTS, u * 128 : (u + 1) * 128]
 
-    unroll = 8
+    unroll = 32
 
     @pl.loop(0, blocks // unroll)
     def _(step):
@@ -202,8 +202,10 @@
     )(where, *[acc for acc, _ in blocks], *[fit for _, fit in blocks], *got)
 
 
-def table_kernel(ratio, scale, own, *refs):
-    parts, entries, table = refs[:-2], refs[-2], refs[-1]
+def table_kernel(ratio, scale, supplier, supplier_scale, *refs):
+    parts, entries, table, supplier_out = refs[:-3], *refs[-3:]
+    own = ratio * jnp.broadcast_to(supplier_scale[...], supplier.shape) * supplier[...]
+    supplier_out[...] = own
     total = parts[0][...]
     for part in parts[1:]:
         total = total + part[...]
@@ -211,7 +213,7 @@
     entry = ratio * by * total
     entries[...] = entry
     columns = total.shape[0]
-    square = jnp.sum(entry * entry, axis=1, keepdims=True) + own[...]
+    square = jnp.sum(entry * entry, axis=1, keepdims=True) + jnp.sum(own * own, axis=1, keepdims=True)
     wide = jnp.broadcast_to(square, (columns, 128))
     scaled = by * entry
     quarter = table.shape[0] - 8
@@ -221,7 +223,7 @@
     table[quarter:, :] = jnp.concatenate([wide] * (128 // columns), axis=0).T[0:8]
 
 
-def lane_table(ratio, scale, own, parts):
+def lane_table(ratio, scale, supplier, supplier_scale, parts):
     columns, lanes = parts[0].shape
     quarter = lanes * columns // LANES_WIDE
     return pl.pallas_call(
@@ -229,13 +231,14 @@
         out_shape=[
             jax.ShapeDtypeStruct((columns, lanes), jnp.float32),
             jax.ShapeDtypeStruct((quarter + 8, LANES_WIDE), jnp.float32),
-        ],
-        in_specs=[VMEM] * (2 + len(parts)),
-        out_specs=[VMEM] * 2,
+            jax.ShapeDtypeStruct(supplier.shape, jnp.float32),
+        ],
+        in_specs=[VMEM] * (3 + len(parts)),
+        out_specs=[VMEM] * 3,
         compiler_params=SMALL,
         cost_estimate=takes(1),
         name="lane_table",
-    )(scale, own, *parts)
+    )(scale, supplier, supplier_scale, *parts)
 
 
 def forward_kernel(effects_all, lines, index, before, by_beta, week_square, lane_part, weight, forward, rhs, *refs):
@@ -422,7 +425,7 @@
             by_week[u, at, wide] = by_week[u, at, wide] + part
         by_sign[at, 0:16] = by_sign[at, 0:16] + got[1]
 
-    unroll = 8
+    unroll = 32
 
     @pl.loop(0, blocks // unroll)
     def _(step):
@@ -509,7 +512,7 @@
         both = jnp.dot(by_effect, hot, preferred_element_type=jnp.float32)
         forward[:, at] = jnp.broadcast_to(row_of(weight, row), shape) * (both[:columns] + both[columns:])
 
-    unroll = 8
+    unroll = 32
 
     @pl.loop(0, blocks // unroll)
     def _(step):
@@ -653,8 +656,6 @@
     held = (fitted, resid, row_weight, week_id, bounds, signs)
     supplier_part, early = own_sums(firsts, weeks_up, *held)
     got, early = lax.optimization_barrier((got, early))
-    p_supplier = ratio * supplier_scale[None, :] * supplier_part
-    supplier_square = jnp.sum(p_supplier * p_supplier, axis=1, keepdims=True)
 
     me_turn = sum(jnp.where(me_boot == b, turned(b, n_boot), 0) for b in range(n_boot))
     where = jnp.stack([me_ship * lane_own, (me_ship % n_boot) ^ me_turn]).astype(jnp.int32)
@@ -678,7 +679,9 @@
     later = later + back[columns:]
     for step in range(1, n_boot // 2):
         pieces.append(swap(later[(step - 1) * columns : step * columns], "boot", 2 * step))
-    entry, table = lane_table(ratio, lane_scale[None, :], supplier_square, pieces)
+    entry, table, p_supplier = lane_table(
+        ratio, lane_scale[None, :], supplier_part, supplier_scale[None, :], pieces
+    )
     near = near_tables(table, n_ship)
 
     beta_first = jnp.sqrt(early[-columns:, 127] / shipments_all + EPS)

time: 114 us -> 113 us (level); the launches traced: 114 us -> 111 us
  waiting for transfers between devices: 31.4 us -> 37.7 us
  Pallas kernels: 46.3 us -> 42.1 us
  starting transfers between devices: 26.9 us -> 24.3 us
  other arithmetic: 7.75 us -> 6.11 us
    ppermute x18, waiting for transfers between devices: 30.6 us -> 34.5 us  [swap(): return lax.ppermute(value, axis, [(i, i ^ step) for i in range(size)])]
    ppermute x18, starting transfers between devices: 21.3 us -> 18.7 us  [swap(): return lax.ppermute(value, axis, [(i, i ^ step) for i in range(size)])]
    ppermute x2, waiting for transfers between devices: 0.71 us -> 3.18 us  [on_device(): got.append(lax.ppermute(planes, ('ship', 'boot'), pairs))]
    pallas_call x1, Pallas kernels: 6.43 us -> 4.64 us  [forward_base(): pl.pallas_call(base_kernel, out_shape=[shape, shape, jax.ShapeDtypeStruct...]
    pallas_call x2, Pallas kernels: 10.3 us -> 8.71 us  [lane_blocks(): pl.pallas_call(functools.partial(lane_blocks_kernel, low_n, rows), out_sh...]
  transfers between devices with their start and end apart: 20 -> 20, of which waited for: 10 -> 11; matrix products, arithmetic and copies ran while one was open for 5% -> 4% of each run, Pallas kernels for 21% -> 17%
where the time goes in v4:
time: 113 us; the launch traced here: 111 us
  Pallas kernels  42.1 us (37%)
  waiting for transfers between devices  37.7 us (33%)
  starting transfers between devices  24.3 us (22%)
  other arithmetic  6.11 us (5%)
    ppermute x18, waiting for transfers between devices, swap(): return lax.ppermute(value, axis, [(i, i ^ step) for i in range(size)])  34.5 us
    ppermute x18, starting transfers between devices, swap(): return lax.ppermute(value, axis, [(i, i ^ step) for i in range(size)])  18.7 us
    pallas_call x1, Pallas kernels, forward_lanes(): pl.pallas_call(functools.partial(forward_kernel, effects_all, lines), out...  18 us
    pallas_call x2, Pallas kernels, lane_blocks(): pl.pallas_call(functools.partial(lane_blocks_kernel, low_n, rows), out_sh...  8.71 us
    pallas_call x1, Pallas kernels, own_sums(): pl.pallas_call(functools.partial(own_sums_kernel, weeks), out_shape=[jax....  6.08 us
    ppermute x2, starting transfers between devices, on_device(): got.append(lax.ppermute(planes, ('ship', 'boot'), pairs))  5.68 us
    pallas_call x1, Pallas kernels, forward_base(): pl.pallas_call(base_kernel, out_shape=[shape, shape, jax.ShapeDtypeStruct...  4.64 us
    ppermute x2, waiting for transfers between devices, on_device(): got.append(lax.ppermute(planes, ('ship', 'boot'), pairs))  3.18 us
  transfers between devices with their start and end apart: 20, of which 11 were waited for; matrix products, arithmetic and copies ran while one was open for 4% of the time, Pallas kernels for 17%

profile of v4, /device:TPU:0, one launch (start us, length us, event | category | flops | bytes accessed | tf_op | source)
XLA Modules:
  0.0 111.5 jit_solution(6822931661868063956)
XLA Ops:
  0.6 1.9 %message.1 = (f32[424,128]{1,0:T(8,128)}, s32[144,8]{1,0:T(8,128)}, s32[1,128]{1,0:T(1,128)}) custom-call(f32[128,128]{1,0:T(8,128)} %bitcast.25, f32[128,128]{1,0:T(8,128)} %bitcast.28, f32[128,128]{1,0:T(8,128)} %bitcast.21, s32[128,128]{1,0:T(8,128)} %bitcast.35, s32[128,128]{1,0:T(8,128)} %bitcast.37, s32[1,128]{1,0:T(1,128)} %refs_5_.3, s32[32,128]{1,0:T(8,128)} %refs_5_.5), custom_call_target="tpu_custom_call" | custom-call | bytes 7200000 | tf_op jit(solution)/shard_map/message/pallas_call | solution.py:354
  2.5 4.1 %collective-permute-start.1 = (f32[424,128]{1,0:T(8,128)}, f32[424,128]{1,0:T(8,128)S(1)}, u32[]{:S(2)}, u32[]{:S(2)}) collective-permute-start(f32[424,128]{1,0:T(8,128)} %get-tuple-element.41), channel_id=1, source_target_pairs={{0,16},{1,24},{2,20},{3,28},{4,17},{5,25},{6,21},{7,29},{8,18},{9,... | collective-permute-start | bytes 651272 | tf_op jit(solution)/shard_map/ppermute | solution.py:653
  6.6 1.6 %collective-permute-start = (f32[424,128]{1,0:T(8,128)}, f32[424,128]{1,0:T(8,128)S(1)}, u32[]{:S(2)}, u32[]{:S(2)}) collective-permute-start(f32[424,128]{1,0:T(8,128)} %get-tuple-element.41), channel_id=1, source_target_pairs={{0,0},{1,8},{2,4},{3,12},{4,1},{5,9},{6,5},{7,13},{8,2},{9,10},{10... | collective-permute-start | bytes 651272 | tf_op jit(solution)/shard_map/ppermute | solution.py:653
  8.2 6.1 %own_sums.1 = (f32[32,128]{1,0:T(8,128)}, f32[96,128]{1,0:T(8,128)}) custom-call(s32[1,128]{1,0:T(1,128)} %get-tuple-element.38.firsts, f32[128,128]{1,0:T(8,128)} %bitcast.26, f32[128,128]{1,0:T(8,128)} %bitcast.29, f32[128,128]{1,0:T(8,128)} %bitcast.22, s32[128,128]{1,0:T(8,128)} %bitcast.31, s32[144,8]{1,0:T(8,128)} %get-tuple-element.39.refs_4_, ...), custom_call_target="tpu_custom_call" | custom-call | bytes 25200000 | tf_op jit(solution)/shard_map/own_sums/pallas_call | solution.py:474
  14.4 3.2 %collective-permute-done.1.planes = f32[424,128]{1,0:T(8,128)S(1)} collective-permute-done((f32[424,128]{1,0:T(8,128)}, f32[424,128]{1,0:T(8,128)S(1)}, u32[]{:S(2)}, u32[]{:S(2)}) %collective-permute-start.1) | collective-permute-done | bytes 217120 | tf_op jit(solution)/shard_map/ppermute | solution.py:653
  18.4 3.3 %collective-permute-start.2 = (f32[160,128]{1,0:T(8,128)S(1)}, f32[160,128]{1,0:T(8,128)S(1)}, u32[]{:S(2)}, u32[]{:S(2)}) collective-permute-start(f32[160,128]{1,0:T(8,128)S(1)} %pad_maximum_fusion.1), channel_id=1, source_target_pairs={{0,4},{4,0},{8,12},{12,8},{16,20},{20,16},{24,28},{28,24},{1,5},{5... | collective-permute-start | bytes 245768 | tf_op jit(solution)/shard_map/ppermute | solution.py:50
  21.7 4.3 %lane_blocks.2 = (f32[2,1088,128]{2,1,0:T(8,128)S(1)}, f32[8,256]{1,0:T(8,128)S(1)}) custom-call(s32[2]{0:T(128)S(1)} %pad_add_fusion.where, s32[1024]{0:T(1024)S(1)} %convert_bitcast_fusion.1.meta, f32[424,128]{1,0:T(8,128)S(1)} %collective-permute-done.planes), custom_call_target="tpu_custom_call" | custom-call | bytes 28800000 | tf_op jit(solution)/shard_map/lane_blocks/pallas_call | solution.py:138
  28.1 4.4 %lane_blocks.3 = (f32[2,1088,128]{2,1,0:T(8,128)S(1)}, f32[8,256]{1,0:T(8,128)S(1)}) custom-call(s32[2]{0:T(128)S(1)} %pad_add_fusion.where, s32[1024]{0:T(1024)S(1)} %convert_bitcast_fusion.meta, f32[424,128]{1,0:T(8,128)S(1)} %collective-permute-done.1.planes), custom_call_target="tpu_custom_call" | custom-call | bytes 28800000 | tf_op jit(solution)/shard_map/lane_blocks/pallas_call | solution.py:138
  34.2 1.6 %collective-permute-done.4 = f32[64,2048]{1,0:T(8,128)S(1)} collective-permute-done((f32[64,2048]{1,0:T(8,128)S(1)}, f32[64,2048]{1,0:T(8,128)S(1)}, u32[]{:S(2)}, u32[]{:S(2)}) %collective-permute-start.4) | collective-permute-done | bytes 524320 | tf_op jit(solution)/shard_map/ppermute | solution.py:50
  35.9 1.5 %collective-permute-start.5 = (f32[32,2048]{1,0:T(8,128)S(1)}, f32[32,2048]{1,0:T(8,128)S(1)}, u32[]{:S(2)}, u32[]{:S(2)}) collective-permute-start(f32[32,2048]{1,0:T(8,128)S(1)} %get-tuple-element.69), channel_id=1, source_target_pairs={{0,2},{1,3},{2,0},{3,1},{4,6},{5,7},{6,4},{7,5},{8,10},{9,11},{10,... | collective-permute-start | bytes 786440 | tf_op jit(solution)/shard_map/ppermute | solution.py:50
  37.4 2.8 %collective-permute-done.6 = f32[96,128]{1,0:T(8,128)S(1)} collective-permute-done((f32[96,128]{1,0:T(8,128)S(1)}, f32[96,128]{1,0:T(8,128)S(1)}, u32[]{:S(2)}, u32[]{:S(2)}) %collective-permute-start.6) | collective-permute-done | bytes 49184 | tf_op jit(solution)/shard_map/ppermute | solution.py:50
  40.2 4.0 %collective-permute-done.5.refs_2_ = f32[32,2048]{1,0:T(8,128)S(1)} collective-permute-done((f32[32,2048]{1,0:T(8,128)S(1)}, f32[32,2048]{1,0:T(8,128)S(1)}, u32[]{:S(2)}, u32[]{:S(2)}) %collective-permute-start.5) | collective-permute-done | bytes 262176 | tf_op jit(solution)/shard_map/ppermute | solution.py:50
  44.5 1.7 %collective-permute-start.12 = (f32[520,128]{1,0:T(8,128)S(1)}, f32[520,128]{1,0:T(8,128)S(1)}, u32[]{:S(2)}, u32[]{:S(2)}) collective-permute-start(f32[520,128]{1,0:T(8,128)S(1)} %get-tuple-element.56.refs_0_), channel_id=1, source_target_pairs={{0,24},{4,28},{8,16},{12,20},{16,8},{20,12},{24,0},{28,4},{1,25},{... | collective-permute-start | bytes 798728 | tf_op jit(solution)/shard_map/ppermute | solution.py:50
  47.2 1.8 %collective-permute-start.9 = (f32[520,128]{1,0:T(8,128)S(1)}, f32[520,128]{1,0:T(8,128)S(1)}, u32[]{:S(2)}, u32[]{:S(2)}) collective-permute-start(f32[520,128]{1,0:T(8,128)S(1)} %get-tuple-element.56.refs_0_), channel_id=1, source_target_pairs={{0,12},{4,8},{8,4},{12,0},{16,28},{20,24},{24,20},{28,16},{1,13},{... | collective-permute-start | bytes 798728 | tf_op jit(solution)/shard_map/ppermute | solution.py:50
  50.8 5.0 %collective-permute-done.12.refs_6_ = f32[520,128]{1,0:T(8,128)S(1)} collective-permute-done((f32[520,128]{1,0:T(8,128)S(1)}, f32[520,128]{1,0:T(8,128)S(1)}, u32[]{:S(2)}, u32[]{:S(2)}) %collective-permute-start.12) | collective-permute-done | bytes 266272 | tf_op jit(solution)/shard_map/ppermute | solution.py:50
  56.0 13.7 %collective-permute-done.10.refs_4_ = f32[520,128]{1,0:T(8,128)S(1)} collective-permute-done((f32[520,128]{1,0:T(8,128)S(1)}, f32[520,128]{1,0:T(8,128)S(1)}, u32[]{:S(2)}, u32[]{:S(2)}) %collective-permute-start.10) | collective-permute-done | bytes 266272 | tf_op jit(solution)/shard_map/ppermute | solution.py:50
  69.9 4.6 %forward_base.1 = (f32[32,16384]{1,0:T(8,128)S(1)}, f32[32,16384]{1,0:T(8,128)S(1)}, f32[8,128]{1,0:T(8,128)S(1)}) custom-call(f32[128,128]{1,0:T(8,128)S(1)} %bitcast.27, f32[128,128]{1,0:T(8,128)S(1)} %bitcast.30, f32[128,128]{1,0:T(8,128)S(1)} %bitcast.23, s32[128,128]{1,0:T(8,128)S(1)} %bitcast.32, s32[144,8]{1,0:T(8,128)S(1)} %copy-done.3, ...), custom_call_target="tpu_custom_call" | custom-call | bytes 28800000 | tf_op jit(solution)/shard_map/forward_base/pallas_call | solution.py:527
  74.6 1.8 %collective-permute-done.11.refs_5_ = f32[520,128]{1,0:T(8,128)S(1)} collective-permute-done((f32[520,128]{1,0:T(8,128)S(1)}, f32[520,128]{1,0:T(8,128)S(1)}, u32[]{:S(2)}, u32[]{:S(2)}) %collective-permute-start.11) | collective-permute-done | bytes 266272 | tf_op jit(solution)/shard_map/ppermute | solution.py:50
  76.4 18.0 %forward_lanes.1 = (f32[32,16384]{1,0:T(8,128)S(1)}, f32[8,128]{1,0:T(8,128)S(1)}, f32[32,1]{1,0:T(8,128)S(1)}) custom-call(s32[16384]{0:T(1024)S(1)} %get-tuple-element.72.index, f32[8,128]{1,0:T(8,128)S(1)} %get-tuple-element.57.before, f32[32,1]{1,0:T(8,128)S(1)} %get-tuple-element.78.by_beta, f32[32,1]{1,0:T(8,128)S(1)} %get-tuple-element.77.week_square, ...), custom_call_target="tpu_custom_call" | custom-call | bytes 64800000 | tf_op jit(solution)/shard_map/forward_lanes/pallas_call | solution.py:300
  95.7 2.5 %collective-permute-done.14 = f32[8,128]{1,0:T(8,128)S(1)} collective-permute-done((f32[8,128]{1,0:T(8,128)S(1)}, f32[8,128]{1,0:T(8,128)S(1)}, u32[]{:S(2)}, u32[]{:S(2)}) %collective-permute-start.14) | collective-permute-done | bytes 4128 | tf_op jit(solution)/shard_map/ppermute | solution.py:50
  98.3 1.9 %collective-permute-start.15 = (f32[8,128]{1,0:T(8,128)S(1)}, f32[8,128]{1,0:T(8,128)S(1)}, u32[]{:S(2)}, u32[]{:S(2)}) collective-permute-start(f32[8,128]{1,0:T(8,128)S(1)} %add.62), channel_id=1, source_target_pairs={{0,8},{4,12},{8,0},{12,4},{16,24},{20,28},{24,16},{28,20},{1,9},{5... | collective-permute-start | bytes 12296 | tf_op jit(solution)/shard_map/ppermute | solution.py:50
  101.9 2.1 %collective-permute-start.16 = (f32[8,128]{1,0:T(8,128)S(1)}, f32[8,128]{1,0:T(8,128)S(1)}, u32[]{:S(2)}, u32[]{:S(2)}) collective-permute-start(f32[8,128]{1,0:T(8,128)S(1)} %add.63), channel_id=1, source_target_pairs={{0,16},{4,20},{8,24},{12,28},{16,0},{20,4},{24,8},{28,12},{1,17},{... | collective-permute-start | bytes 12296 | tf_op jit(solution)/shard_map/ppermute | solution.py:50
  104.6 1.7 %collective-permute-done.16 = f32[8,128]{1,0:T(8,128)S(1)} collective-permute-done((f32[8,128]{1,0:T(8,128)S(1)}, f32[8,128]{1,0:T(8,128)S(1)}, u32[]{:S(2)}, u32[]{:S(2)}) %collective-permute-start.16) | collective-permute-done | bytes 4128 | tf_op jit(solution)/shard_map/ppermute | solution.py:50
  109.1 1.5 %broadcast_multiply_fusion = f32[32,16384]{1,0:T(8,128)} fusion(f32[32,16384]{1,0:T(8,128)S(1)} %get-tuple-element.62, f32[32]{0:T(128)S(1)} %reduce.1), kind=kLoop, calls=%fused_computation | loop fusion | flops 524288 | bytes 4194432 | tf_op jit(solution)/shard_map/mul | solution.py:718
  (84 shorter events, 15.4 us)
Async XLA Ops:
  2.5 15.0 %collective-permute-start.1 = (f32[424,128]{1,0:T(8,128)}, f32[424,128]{1,0:T(8,128)S(1)}, u32[]{:S(2)}, u32[]{:S(2)}) collective-permute-start(f32[424,128]{1,0:T(8,128)} %get-tuple-element.41), channel_id=1, source_target_pairs={{0,16},{1,24},{2,20},{3,28},{4,17},{5,25},{6,21},{7,29},{8,18},{9,... | collective-permute-start | bytes 651272 | tf_op jit(solution)/shard_map/ppermute | solution.py:653
  6.6 10.9 %collective-permute-start = (f32[424,128]{1,0:T(8,128)}, f32[424,128]{1,0:T(8,128)S(1)}, u32[]{:S(2)}, u32[]{:S(2)}) collective-permute-start(f32[424,128]{1,0:T(8,128)} %get-tuple-element.41), channel_id=1, source_target_pairs={{0,0},{1,8},{2,4},{3,12},{4,1},{5,9},{6,5},{7,13},{8,2},{9,10},{10... | collective-permute-start | bytes 651272 | tf_op jit(solution)/shard_map/ppermute | solution.py:653
  18.4 7.7 %collective-permute-start.2 = (f32[160,128]{1,0:T(8,128)S(1)}, f32[160,128]{1,0:T(8,128)S(1)}, u32[]{:S(2)}, u32[]{:S(2)}) collective-permute-start(f32[160,128]{1,0:T(8,128)S(1)} %pad_maximum_fusion.1), channel_id=1, source_target_pairs={{0,4},{4,0},{8,12},{12,8},{16,20},{20,16},{24,28},{28,24},{1,5},{5... | collective-permute-start | bytes 245768 | tf_op jit(solution)/shard_map/ppermute | solution.py:50
  26.9 5.6 %collective-permute-start.3 = (f32[224,128]{1,0:T(8,128)S(1)}, f32[224,128]{1,0:T(8,128)S(1)}, u32[]{:S(2)}, u32[]{:S(2)}) collective-permute-start(f32[224,128]{1,0:T(8,128)S(1)} %pad_maximum_fusion), channel_id=1, source_target_pairs={{0,8},{4,12},{8,0},{12,4},{16,24},{20,28},{24,16},{28,20},{1,9},{5... | collective-permute-start | bytes 344072 | tf_op jit(solution)/shard_map/ppermute | solution.py:50
  33.7 36.1 %copy-start = (f32[16384]{0:T(1024)S(1)}, f32[16384]{0:T(1024)}, u32[]{:S(2)}) copy-start(f32[16384]{0:T(1024)} %param.13) | copy-start | bytes 196612
  33.8 36.1 %copy-start.1 = (f32[16384]{0:T(1024)S(1)}, f32[16384]{0:T(1024)}, u32[]{:S(2)}) copy-start(f32[16384]{0:T(1024)} %param.11) | copy-start | bytes 196612
  33.8 36.1 %copy-start.2 = (f32[16384]{0:T(1024)S(1)}, f32[16384]{0:T(1024)}, u32[]{:S(2)}) copy-start(f32[16384]{0:T(1024)} %param.12) | copy-start | bytes 196612
  33.8 36.1 %copy-start.3 = (s32[144,8]{1,0:T(8,128)S(1)}, s32[144,8]{1,0:T(8,128)}, u32[]{:S(2)}) copy-start(s32[144,8]{1,0:T(8,128)} %get-tuple-element.39.refs_4_) | copy-start | bytes 13828
  33.8 2.0 %collective-permute-start.4 = (f32[64,2048]{1,0:T(8,128)S(1)}, f32[64,2048]{1,0:T(8,128)S(1)}, u32[]{:S(2)}, u32[]{:S(2)}) collective-permute-start(f32[64,2048]{1,0:T(8,128)S(1)} %get-tuple-element.53), channel_id=1, source_target_pairs={{0,1},{1,0},{2,3},{3,2},{4,5},{5,4},{6,7},{7,6},{8,9},{9,8},{10,11... | collective-permute-start | bytes 1572872 | tf_op jit(solution)/shard_map/ppermute | solution.py:50
  34.1 6.1 %collective-permute-start.6 = (f32[96,128]{1,0:T(8,128)S(1)}, f32[96,128]{1,0:T(8,128)S(1)}, u32[]{:S(2)}, u32[]{:S(2)}) collective-permute-start(f32[96,128]{1,0:T(8,128)S(1)} %slice_add_fusion.1), channel_id=1, source_target_pairs={{0,16},{4,20},{8,24},{12,28},{16,0},{20,4},{24,8},{28,12},{1,17},{... | collective-permute-start | bytes 147464 | tf_op jit(solution)/shard_map/ppermute | solution.py:50
  35.9 8.4 %collective-permute-start.5 = (f32[32,2048]{1,0:T(8,128)S(1)}, f32[32,2048]{1,0:T(8,128)S(1)}, u32[]{:S(2)}, u32[]{:S(2)}) collective-permute-start(f32[32,2048]{1,0:T(8,128)S(1)} %get-tuple-element.69), channel_id=1, source_target_pairs={{0,2},{1,3},{2,0},{3,1},{4,6},{5,7},{6,4},{7,5},{8,10},{9,11},{10,... | collective-permute-start | bytes 786440 | tf_op jit(solution)/shard_map/ppermute | solution.py:50
  44.5 11.3 %collective-permute-start.12 = (f32[520,128]{1,0:T(8,128)S(1)}, f32[520,128]{1,0:T(8,128)S(1)}, u32[]{:S(2)}, u32[]{:S(2)}) collective-permute-start(f32[520,128]{1,0:T(8,128)S(1)} %get-tuple-element.56.refs_0_), channel_id=1, source_target_pairs={{0,24},{4,28},{8,16},{12,20},{16,8},{20,12},{24,0},{28,4},{1,25},{... | collective-permute-start | bytes 798728 | tf_op jit(solution)/shard_map/ppermute | solution.py:50
  46.2 23.5 %collective-permute-start.10 = (f32[520,128]{1,0:T(8,128)S(1)}, f32[520,128]{1,0:T(8,128)S(1)}, u32[]{:S(2)}, u32[]{:S(2)}) collective-permute-start(f32[520,128]{1,0:T(8,128)S(1)} %get-tuple-element.56.refs_0_), channel_id=1, source_target_pairs={{0,16},{4,20},{8,24},{12,28},{16,0},{20,4},{24,8},{28,12},{1,17},{... | collective-permute-start | bytes 798728 | tf_op jit(solution)/shard_map/ppermute | solution.py:50
  47.2 27.3 %collective-permute-start.9 = (f32[520,128]{1,0:T(8,128)S(1)}, f32[520,128]{1,0:T(8,128)S(1)}, u32[]{:S(2)}, u32[]{:S(2)}) collective-permute-start(f32[520,128]{1,0:T(8,128)S(1)} %get-tuple-element.56.refs_0_), channel_id=1, source_target_pairs={{0,12},{4,8},{8,4},{12,0},{16,28},{20,24},{24,20},{28,16},{1,13},{... | collective-permute-start | bytes 798728 | tf_op jit(solution)/shard_map/ppermute | solution.py:50
  49.0 25.6 %collective-permute-start.8 = (f32[520,128]{1,0:T(8,128)S(1)}, f32[520,128]{1,0:T(8,128)S(1)}, u32[]{:S(2)}, u32[]{:S(2)}) collective-permute-start(f32[520,128]{1,0:T(8,128)S(1)} %get-tuple-element.56.refs_0_), channel_id=1, source_target_pairs={{0,8},{4,12},{8,0},{12,4},{16,24},{20,28},{24,16},{28,20},{1,9},{5... | collective-permute-start | bytes 798728 | tf_op jit(solution)/shard_map/ppermute | solution.py:50
  49.4 20.4 %collective-permute-start.7 = (f32[520,128]{1,0:T(8,128)S(1)}, f32[520,128]{1,0:T(8,128)S(1)}, u32[]{:S(2)}, u32[]{:S(2)}) collective-permute-start(f32[520,128]{1,0:T(8,128)S(1)} %get-tuple-element.56.refs_0_), channel_id=1, source_target_pairs={{0,4},{4,0},{8,12},{12,8},{16,20},{20,16},{24,28},{28,24},{1,5},{5... | collective-permute-start | bytes 798728 | tf_op jit(solution)/shard_map/ppermute | solution.py:50
  55.8 18.7 %collective-permute-start.13 = (f32[520,128]{1,0:T(8,128)S(1)}, f32[520,128]{1,0:T(8,128)S(1)}, u32[]{:S(2)}, u32[]{:S(2)}) collective-permute-start(f32[520,128]{1,0:T(8,128)S(1)} %collective-permute-done.12.refs_6_), channel_id=1, source_target_pairs={{0,4},{4,0},{8,12},{12,8},{16,20},{20,16},{24,28},{28,24},{1,5},{5... | collective-permute-start | bytes 798728 | tf_op jit(solution)/shard_map/ppermute | solution.py:50
  69.7 6.7 %collective-permute-start.11 = (f32[520,128]{1,0:T(8,128)S(1)}, f32[520,128]{1,0:T(8,128)S(1)}, u32[]{:S(2)}, u32[]{:S(2)}) collective-permute-start(f32[520,128]{1,0:T(8,128)S(1)} %collective-permute-done.10.refs_4_), channel_id=1, source_target_pairs={{0,4},{4,0},{8,12},{12,8},{16,20},{20,16},{24,28},{28,24},{1,5},{5... | collective-permute-start | bytes 798728 | tf_op jit(solution)/shard_map/ppermute | solution.py:50
  94.6 3.7 %collective-permute-start.14 = (f32[8,128]{1,0:T(8,128)S(1)}, f32[8,128]{1,0:T(8,128)S(1)}, u32[]{:S(2)}, u32[]{:S(2)}) collective-permute-start(f32[8,128]{1,0:T(8,128)S(1)} %get-tuple-element.63), channel_id=1, source_target_pairs={{0,4},{4,0},{8,12},{12,8},{16,20},{20,16},{24,28},{28,24},{1,5},{5... | collective-permute-start | bytes 12296 | tf_op jit(solution)/shard_map/ppermute | solution.py:50
  98.3 3.6 %collective-permute-start.15 = (f32[8,128]{1,0:T(8,128)S(1)}, f32[8,128]{1,0:T(8,128)S(1)}, u32[]{:S(2)}, u32[]{:S(2)}) collective-permute-start(f32[8,128]{1,0:T(8,128)S(1)} %add.62), channel_id=1, source_target_pairs={{0,8},{4,12},{8,0},{12,4},{16,24},{20,28},{24,16},{28,20},{1,9},{5... | collective-permute-start | bytes 12296 | tf_op jit(solution)/shard_map/ppermute | solution.py:50
  101.9 4.5 %collective-permute-start.16 = (f32[8,128]{1,0:T(8,128)S(1)}, f32[8,128]{1,0:T(8,128)S(1)}, u32[]{:S(2)}, u32[]{:S(2)}) collective-permute-start(f32[8,128]{1,0:T(8,128)S(1)} %add.63), channel_id=1, source_target_pairs={{0,16},{4,20},{8,24},{12,28},{16,0},{20,4},{24,8},{28,12},{1,17},{... | collective-permute-start | bytes 12296 | tf_op jit(solution)/shard_map/ppermute | solution.py:50
  107.1 3.5 %collective-permute-start.19 = (f32[24,128]{1,0:T(8,128)S(1)}, f32[24,128]{1,0:T(8,128)S(1)}, u32[]{:S(2)}, u32[]{:S(2)}) collective-permute-start(f32[24,128]{1,0:T(8,128)S(1)} %get-tuple-element.66.refs_0_), channel_id=1, source_target_pairs={{0,3},{1,2},{2,1},{3,0},{4,7},{5,6},{6,5},{7,4},{8,11},{9,10},{10,... | collective-permute-start | bytes 36872 | tf_op jit(solution)/shard_map/ppermute | solution.py:50
  107.1 3.7 %collective-permute-start.18 = (f32[24,128]{1,0:T(8,128)S(1)}, f32[24,128]{1,0:T(8,128)S(1)}, u32[]{:S(2)}, u32[]{:S(2)}) collective-permute-start(f32[24,128]{1,0:T(8,128)S(1)} %get-tuple-element.66.refs_0_), channel_id=1, source_target_pairs={{0,2},{1,3},{2,0},{3,1},{4,6},{5,7},{6,4},{7,5},{8,10},{9,11},{10,... | collective-permute-start | bytes 36872 | tf_op jit(solution)/shard_map/ppermute | solution.py:50
  108.3 2.6 %collective-permute-start.17 = (f32[24,128]{1,0:T(8,128)S(1)}, f32[24,128]{1,0:T(8,128)S(1)}, u32[]{:S(2)}, u32[]{:S(2)}) collective-permute-start(f32[24,128]{1,0:T(8,128)S(1)} %get-tuple-element.66.refs_0_), channel_id=1, source_target_pairs={{0,1},{1,0},{2,3},{3,2},{4,5},{5,4},{6,7},{7,6},{8,9},{9,8},{10,11... | collective-permute-start | bytes 36872 | tf_op jit(solution)/shard_map/ppermute | solution.py:50
  (8 other events, 169.2 us)

commit v5 on v4

--- a/solution.py
+++ b/solution.py
@@ -270,7 +270,7 @@
             store[u : u + 1, :] = table[pl.ds(index[group * 128 + u], 1), :]
 
     def finish(group, store):
-        turned_over = store[...].T
+        turned_over = store
         part = jnp.broadcast_to(lane_part[pl.ds(group, 1), :], (columns, 128))
         picked = turned_over[0:columns]
         for u in range(1, 128 // columns):
@@ -283,12 +283,11 @@
 
     gather(0, first)
 
-    @pl.loop(0, groups // 2)
-    def _(step):
-        gather(2 * step + 1, second)
-        finish(2 * step, first)
-        gather(jnp.minimum(2 * step + 2, groups - 1), first)
-        finish(2 * step + 1, second)
+    @pl.loop(0, groups)
+    def _(group):
+        turned_over = first[...].T
+        gather(jnp.minimum(group + 1, groups - 1), first)
+        finish(group, turned_over)
 
     across = jnp.broadcast_to(jnp.sum(total[...], axis=1, keepdims=True), (columns, 128))
     squares[...] = jnp.concatenate([across] * (128 // columns), axis=0).T[0:8]

time: 113 us -> 113 us (level); the launches traced: 111 us -> 113 us
  waiting for transfers between devices: 37.7 us -> 39.4 us
  starting transfers between devices: 24.3 us -> 22.7 us
  Pallas kernels: 42.1 us -> 43.4 us
    pallas_call x2, Pallas kernels: 8.71 us -> 10.9 us  [lane_blocks(): pl.pallas_call(functools.partial(lane_blocks_kernel, low_n, rows), out_sh...]
    ppermute x18, waiting for transfers between devices: 34.5 us -> 36.2 us  [swap(): return lax.ppermute(value, axis, [(i, i ^ step) for i in range(size)])]
    ppermute x18, starting transfers between devices: 18.7 us -> 17 us  [swap(): return lax.ppermute(value, axis, [(i, i ^ step) for i in range(size)])]
  transfers between devices with their start and end apart: 20 -> 20, of which waited for: 11 -> 11; matrix products, arithmetic and copies ran while one was open for 4% -> 4% of each run, Pallas kernels for 17% -> 19%
where the time goes in v5:
time: 113 us
  Pallas kernels  43.4 us (38%)
  waiting for transfers between devices  39.4 us (35%)
  starting transfers between devices  22.7 us (20%)
  other arithmetic  6.11 us (5%)
    ppermute x18, waiting for transfers between devices, swap(): return lax.ppermute(value, axis, [(i, i ^ step) for i in range(size)])  36.2 us
    pallas_call x1, Pallas kernels, forward_lanes(): pl.pallas_call(functools.partial(forward_kernel, effects_all, lines), out...  17.1 us
    ppermute x18, starting transfers between devices, swap(): return lax.ppermute(value, axis, [(i, i ^ step) for i in range(size)])  17 us
    pallas_call x2, Pallas kernels, lane_blocks(): pl.pallas_call(functools.partial(lane_blocks_kernel, low_n, rows), out_sh...  10.9 us
    pallas_call x1, Pallas kernels, own_sums(): pl.pallas_call(functools.partial(own_sums_kernel, weeks), out_shape=[jax....  6.08 us
    ppermute x2, starting transfers between devices, on_device(): got.append(lax.ppermute(planes, ('ship', 'boot'), pairs))  5.68 us
    pallas_call x1, Pallas kernels, forward_base(): pl.pallas_call(base_kernel, out_shape=[shape, shape, jax.ShapeDtypeStruct...  4.65 us
    ppermute x2, waiting for transfers between devices, on_device(): got.append(lax.ppermute(planes, ('ship', 'boot'), pairs))  3.18 us
  transfers between devices with their start and end apart: 20, of which 11 were waited for; matrix products, arithmetic and copies ran while one was open for 4% of the time, Pallas kernels for 19%

profile of v5, /device:TPU:0, one launch (start us, length us, event | category | flops | bytes accessed | tf_op | source)
XLA Modules:
  0.0 112.9 jit_solution(5844691385835500519)
XLA Ops:
  0.6 1.9 %message.1 = (f32[424,128]{1,0:T(8,128)}, s32[144,8]{1,0:T(8,128)}, s32[1,128]{1,0:T(1,128)}) custom-call(f32[128,128]{1,0:T(8,128)} %bitcast.25, f32[128,128]{1,0:T(8,128)} %bitcast.28, f32[128,128]{1,0:T(8,128)} %bitcast.21, s32[128,128]{1,0:T(8,128)} %bitcast.35, s32[128,128]{1,0:T(8,128)} %bitcast.37, s32[1,128]{1,0:T(1,128)} %refs_5_.3, s32[32,128]{1,0:T(8,128)} %refs_5_.5), custom_call_target="tpu_custom_call" | custom-call | bytes 7200000 | tf_op jit(solution)/shard_map/message/pallas_call | solution.py:353
  2.5 4.1 %collective-permute-start.1 = (f32[424,128]{1,0:T(8,128)}, f32[424,128]{1,0:T(8,128)S(1)}, u32[]{:S(2)}, u32[]{:S(2)}) collective-permute-start(f32[424,128]{1,0:T(8,128)} %get-tuple-element.41), channel_id=1, source_target_pairs={{0,16},{1,24},{2,20},{3,28},{4,17},{5,25},{6,21},{7,29},{8,18},{9,... | collective-permute-start | bytes 651272 | tf_op jit(solution)/shard_map/ppermute | solution.py:652
  6.6 1.6 %collective-permute-start = (f32[424,128]{1,0:T(8,128)}, f32[424,128]{1,0:T(8,128)S(1)}, u32[]{:S(2)}, u32[]{:S(2)}) collective-permute-start(f32[424,128]{1,0:T(8,128)} %get-tuple-element.41), channel_id=1, source_target_pairs={{0,0},{1,8},{2,4},{3,12},{4,1},{5,9},{6,5},{7,13},{8,2},{9,10},{10... | collective-permute-start | bytes 651272 | tf_op jit(solution)/shard_map/ppermute | solution.py:652
  8.2 6.1 %own_sums.1 = (f32[32,128]{1,0:T(8,128)}, f32[96,128]{1,0:T(8,128)}) custom-call(s32[1,128]{1,0:T(1,128)} %get-tuple-element.38.firsts, f32[128,128]{1,0:T(8,128)} %bitcast.26, f32[128,128]{1,0:T(8,128)} %bitcast.29, f32[128,128]{1,0:T(8,128)} %bitcast.22, s32[128,128]{1,0:T(8,128)} %bitcast.31, s32[144,8]{1,0:T(8,128)} %get-tuple-element.39.refs_4_, ...), custom_call_target="tpu_custom_call" | custom-call | bytes 25200000 | tf_op jit(solution)/shard_map/own_sums/pallas_call | solution.py:473
  14.4 3.2 %collective-permute-done.1.planes = f32[424,128]{1,0:T(8,128)S(1)} collective-permute-done((f32[424,128]{1,0:T(8,128)}, f32[424,128]{1,0:T(8,128)S(1)}, u32[]{:S(2)}, u32[]{:S(2)}) %collective-permute-start.1) | collective-permute-done | bytes 217120 | tf_op jit(solution)/shard_map/ppermute | solution.py:652
  18.4 3.3 %collective-permute-start.2 = (f32[160,128]{1,0:T(8,128)S(1)}, f32[160,128]{1,0:T(8,128)S(1)}, u32[]{:S(2)}, u32[]{:S(2)}) collective-permute-start(f32[160,128]{1,0:T(8,128)S(1)} %pad_maximum_fusion.1), channel_id=1, source_target_pairs={{0,4},{4,0},{8,12},{12,8},{16,20},{20,16},{24,28},{28,24},{1,5},{5... | collective-permute-start | bytes 245768 | tf_op jit(solution)/shard_map/ppermute | solution.py:50
  21.7 5.4 %lane_blocks.2 = (f32[2,1088,128]{2,1,0:T(8,128)S(1)}, f32[8,256]{1,0:T(8,128)S(1)}) custom-call(s32[2]{0:T(128)S(1)} %pad_add_fusion.where, s32[1024]{0:T(1024)S(1)} %convert_bitcast_fusion.1.meta, f32[424,128]{1,0:T(8,128)S(1)} %collective-permute-done.planes), custom_call_target="tpu_custom_call" | custom-call | bytes 28800000 | tf_op jit(solution)/shard_map/lane_blocks/pallas_call | solution.py:138
  29.2 5.6 %lane_blocks.3 = (f32[2,1088,128]{2,1,0:T(8,128)S(1)}, f32[8,256]{1,0:T(8,128)S(1)}) custom-call(s32[2]{0:T(128)S(1)} %pad_add_fusion.where, s32[1024]{0:T(1024)S(1)} %convert_bitcast_fusion.meta, f32[424,128]{1,0:T(8,128)S(1)} %collective-permute-done.1.planes), custom_call_target="tpu_custom_call" | custom-call | bytes 28800000 | tf_op jit(solution)/shard_map/lane_blocks/pallas_call | solution.py:138
  36.5 1.6 %collective-permute-done.4 = f32[64,2048]{1,0:T(8,128)S(1)} collective-permute-done((f32[64,2048]{1,0:T(8,128)S(1)}, f32[64,2048]{1,0:T(8,128)S(1)}, u32[]{:S(2)}, u32[]{:S(2)}) %collective-permute-start.4) | collective-permute-done | bytes 524320 | tf_op jit(solution)/shard_map/ppermute | solution.py:50
  38.3 4.2 %collective-permute-done.6 = f32[96,128]{1,0:T(8,128)S(1)} collective-permute-done((f32[96,128]{1,0:T(8,128)S(1)}, f32[96,128]{1,0:T(8,128)S(1)}, u32[]{:S(2)}, u32[]{:S(2)}) %collective-permute-start.6) | collective-permute-done | bytes 49184 | tf_op jit(solution)/shard_map/ppermute | solution.py:50
  42.5 4.0 %collective-permute-done.5.refs_2_ = f32[32,2048]{1,0:T(8,128)S(1)} collective-permute-done((f32[32,2048]{1,0:T(8,128)S(1)}, f32[32,2048]{1,0:T(8,128)S(1)}, u32[]{:S(2)}, u32[]{:S(2)}) %collective-permute-start.5) | collective-permute-done | bytes 262176 | tf_op jit(solution)/shard_map/ppermute | solution.py:50
  46.8 1.7 %collective-permute-start.12 = (f32[520,128]{1,0:T(8,128)S(1)}, f32[520,128]{1,0:T(8,128)S(1)}, u32[]{:S(2)}, u32[]{:S(2)}) collective-permute-start(f32[520,128]{1,0:T(8,128)S(1)} %get-tuple-element.56.refs_0_), channel_id=1, source_target_pairs={{0,24},{4,28},{8,16},{12,20},{16,8},{20,12},{24,0},{28,4},{1,25},{... | collective-permute-start | bytes 798728 | tf_op jit(solution)/shard_map/ppermute | solution.py:50
  49.4 1.6 %collective-permute-start.9 = (f32[520,128]{1,0:T(8,128)S(1)}, f32[520,128]{1,0:T(8,128)S(1)}, u32[]{:S(2)}, u32[]{:S(2)}) collective-permute-start(f32[520,128]{1,0:T(8,128)S(1)} %get-tuple-element.56.refs_0_), channel_id=1, source_target_pairs={{0,12},{4,8},{8,4},{12,0},{16,28},{20,24},{24,20},{28,16},{1,13},{... | collective-permute-start | bytes 798728 | tf_op jit(solution)/shard_map/ppermute | solution.py:50
  51.6 1.4 %collective-permute-start.7 = (f32[520,128]{1,0:T(8,128)S(1)}, f32[520,128]{1,0:T(8,128)S(1)}, u32[]{:S(2)}, u32[]{:S(2)}) collective-permute-start(f32[520,128]{1,0:T(8,128)S(1)} %get-tuple-element.56.refs_0_), channel_id=1, source_target_pairs={{0,4},{4,0},{8,12},{12,8},{16,20},{20,16},{24,28},{28,24},{1,5},{5... | collective-permute-start | bytes 798728 | tf_op jit(solution)/shard_map/ppermute | solution.py:50
  53.0 5.0 %collective-permute-done.12.refs_6_ = f32[520,128]{1,0:T(8,128)S(1)} collective-permute-done((f32[520,128]{1,0:T(8,128)S(1)}, f32[520,128]{1,0:T(8,128)S(1)}, u32[]{:S(2)}, u32[]{:S(2)}) %collective-permute-start.12) | collective-permute-done | bytes 266272 | tf_op jit(solution)/shard_map/ppermute | solution.py:50
  58.1 13.9 %collective-permute-done.10.refs_4_ = f32[520,128]{1,0:T(8,128)S(1)} collective-permute-done((f32[520,128]{1,0:T(8,128)S(1)}, f32[520,128]{1,0:T(8,128)S(1)}, u32[]{:S(2)}, u32[]{:S(2)}) %collective-permute-start.10) | collective-permute-done | bytes 266272 | tf_op jit(solution)/shard_map/ppermute | solution.py:50
  72.0 4.6 %forward_base.1 = (f32[32,16384]{1,0:T(8,128)S(1)}, f32[32,16384]{1,0:T(8,128)S(1)}, f32[8,128]{1,0:T(8,128)S(1)}) custom-call(f32[128,128]{1,0:T(8,128)S(1)} %bitcast.27, f32[128,128]{1,0:T(8,128)S(1)} %bitcast.30, f32[128,128]{1,0:T(8,128)S(1)} %bitcast.23, s32[128,128]{1,0:T(8,128)S(1)} %bitcast.32, s32[144,8]{1,0:T(8,128)S(1)} %copy-done.3, ...), custom_call_target="tpu_custom_call" | custom-call | bytes 28800000 | tf_op jit(solution)/shard_map/forward_base/pallas_call | solution.py:526
  76.7 1.9 %collective-permute-done.11.refs_5_ = f32[520,128]{1,0:T(8,128)S(1)} collective-permute-done((f32[520,128]{1,0:T(8,128)S(1)}, f32[520,128]{1,0:T(8,128)S(1)}, u32[]{:S(2)}, u32[]{:S(2)}) %collective-permute-start.11) | collective-permute-done | bytes 266272 | tf_op jit(solution)/shard_map/ppermute | solution.py:50
  78.6 17.1 %forward_lanes.1 = (f32[32,16384]{1,0:T(8,128)S(1)}, f32[8,128]{1,0:T(8,128)S(1)}, f32[32,1]{1,0:T(8,128)S(1)}) custom-call(s32[16384]{0:T(1024)S(1)} %get-tuple-element.72.index, f32[8,128]{1,0:T(8,128)S(1)} %get-tuple-element.57.before, f32[32,1]{1,0:T(8,128)S(1)} %get-tuple-element.78.by_beta, f32[32,1]{1,0:T(8,128)S(1)} %get-tuple-element.77.week_square, ...), custom_call_target="tpu_custom_call" | custom-call | bytes 64800000 | tf_op jit(solution)/shard_map/forward_lanes/pallas_call | solution.py:299
  97.0 2.5 %collective-permute-done.14 = f32[8,128]{1,0:T(8,128)S(1)} collective-permute-done((f32[8,128]{1,0:T(8,128)S(1)}, f32[8,128]{1,0:T(8,128)S(1)}, u32[]{:S(2)}, u32[]{:S(2)}) %collective-permute-start.14) | collective-permute-done | bytes 4128 | tf_op jit(solution)/shard_map/ppermute | solution.py:50
  99.6 1.9 %collective-permute-start.15 = (f32[8,128]{1,0:T(8,128)S(1)}, f32[8,128]{1,0:T(8,128)S(1)}, u32[]{:S(2)}, u32[]{:S(2)}) collective-permute-start(f32[8,128]{1,0:T(8,128)S(1)} %add.62), channel_id=1, source_target_pairs={{0,8},{4,12},{8,0},{12,4},{16,24},{20,28},{24,16},{28,20},{1,9},{5... | collective-permute-start | bytes 12296 | tf_op jit(solution)/shard_map/ppermute | solution.py:50
  103.2 2.1 %collective-permute-start.16 = (f32[8,128]{1,0:T(8,128)S(1)}, f32[8,128]{1,0:T(8,128)S(1)}, u32[]{:S(2)}, u32[]{:S(2)}) collective-permute-start(f32[8,128]{1,0:T(8,128)S(1)} %add.63), channel_id=1, source_target_pairs={{0,16},{4,20},{8,24},{12,28},{16,0},{20,4},{24,8},{28,12},{1,17},{... | collective-permute-start | bytes 12296 | tf_op jit(solution)/shard_map/ppermute | solution.py:50
  105.9 1.7 %collective-permute-done.16 = f32[8,128]{1,0:T(8,128)S(1)} collective-permute-done((f32[8,128]{1,0:T(8,128)S(1)}, f32[8,128]{1,0:T(8,128)S(1)}, u32[]{:S(2)}, u32[]{:S(2)}) %collective-permute-start.16) | collective-permute-done | bytes 4128 | tf_op jit(solution)/shard_map/ppermute | solution.py:50
  110.4 1.5 %broadcast_multiply_fusion = f32[32,16384]{1,0:T(8,128)} fusion(f32[32,16384]{1,0:T(8,128)S(1)} %get-tuple-element.62, f32[32]{0:T(128)S(1)} %reduce.1), kind=kLoop, calls=%fused_computation | loop fusion | flops 524288 | bytes 4194432 | tf_op jit(solution)/shard_map/mul | solution.py:717
  (84 shorter events, 14.1 us)
Async XLA Ops:
  2.5 15.0 %collective-permute-start.1 = (f32[424,128]{1,0:T(8,128)}, f32[424,128]{1,0:T(8,128)S(1)}, u32[]{:S(2)}, u32[]{:S(2)}) collective-permute-start(f32[424,128]{1,0:T(8,128)} %get-tuple-element.41), channel_id=1, source_target_pairs={{0,16},{1,24},{2,20},{3,28},{4,17},{5,25},{6,21},{7,29},{8,18},{9,... | collective-permute-start | bytes 651272 | tf_op jit(solution)/shard_map/ppermute | solution.py:652
  6.6 10.9 %collective-permute-start = (f32[424,128]{1,0:T(8,128)}, f32[424,128]{1,0:T(8,128)S(1)}, u32[]{:S(2)}, u32[]{:S(2)}) collective-permute-start(f32[424,128]{1,0:T(8,128)} %get-tuple-element.41), channel_id=1, source_target_pairs={{0,0},{1,8},{2,4},{3,12},{4,1},{5,9},{6,5},{7,13},{8,2},{9,10},{10... | collective-permute-start | bytes 651272 | tf_op jit(solution)/shard_map/ppermute | solution.py:652
  18.4 8.7 %collective-permute-start.2 = (f32[160,128]{1,0:T(8,128)S(1)}, f32[160,128]{1,0:T(8,128)S(1)}, u32[]{:S(2)}, u32[]{:S(2)}) collective-permute-start(f32[160,128]{1,0:T(8,128)S(1)} %pad_maximum_fusion.1), channel_id=1, source_target_pairs={{0,4},{4,0},{8,12},{12,8},{16,20},{20,16},{24,28},{28,24},{1,5},{5... | collective-permute-start | bytes 245768 | tf_op jit(solution)/shard_map/ppermute | solution.py:50
  27.9 6.8 %collective-permute-start.3 = (f32[224,128]{1,0:T(8,128)S(1)}, f32[224,128]{1,0:T(8,128)S(1)}, u32[]{:S(2)}, u32[]{:S(2)}) collective-permute-start(f32[224,128]{1,0:T(8,128)S(1)} %pad_maximum_fusion), channel_id=1, source_target_pairs={{0,8},{4,12},{8,0},{12,4},{16,24},{20,28},{24,16},{28,20},{1,9},{5... | collective-permute-start | bytes 344072 | tf_op jit(solution)/shard_map/ppermute | solution.py:50
  36.0 36.0 %copy-start = (f32[16384]{0:T(1024)S(1)}, f32[16384]{0:T(1024)}, u32[]{:S(2)}) copy-start(f32[16384]{0:T(1024)} %param.13) | copy-start | bytes 196612
  36.0 36.0 %copy-start.1 = (f32[16384]{0:T(1024)S(1)}, f32[16384]{0:T(1024)}, u32[]{:S(2)}) copy-start(f32[16384]{0:T(1024)} %param.11) | copy-start | bytes 196612
  36.0 36.0 %copy-start.2 = (f32[16384]{0:T(1024)S(1)}, f32[16384]{0:T(1024)}, u32[]{:S(2)}) copy-start(f32[16384]{0:T(1024)} %param.12) | copy-start | bytes 196612
  36.0 36.0 %copy-start.3 = (s32[144,8]{1,0:T(8,128)S(1)}, s32[144,8]{1,0:T(8,128)}, u32[]{:S(2)}) copy-start(s32[144,8]{1,0:T(8,128)} %get-tuple-element.39.refs_4_) | copy-start | bytes 13828
  36.1 2.0 %collective-permute-start.4 = (f32[64,2048]{1,0:T(8,128)S(1)}, f32[64,2048]{1,0:T(8,128)S(1)}, u32[]{:S(2)}, u32[]{:S(2)}) collective-permute-start(f32[64,2048]{1,0:T(8,128)S(1)} %get-tuple-element.53), channel_id=1, source_target_pairs={{0,1},{1,0},{2,3},{3,2},{4,5},{5,4},{6,7},{7,6},{8,9},{9,8},{10,11... | collective-permute-start | bytes 1572872 | tf_op jit(solution)/shard_map/ppermute | solution.py:50
  36.3 6.1 %collective-permute-start.6 = (f32[96,128]{1,0:T(8,128)S(1)}, f32[96,128]{1,0:T(8,128)S(1)}, u32[]{:S(2)}, u32[]{:S(2)}) collective-permute-start(f32[96,128]{1,0:T(8,128)S(1)} %slice_add_fusion.1), channel_id=1, source_target_pairs={{0,16},{4,20},{8,24},{12,28},{16,0},{20,4},{24,8},{28,12},{1,17},{... | collective-permute-start | bytes 147464 | tf_op jit(solution)/shard_map/ppermute | solution.py:50
  38.1 8.4 %collective-permute-start.5 = (f32[32,2048]{1,0:T(8,128)S(1)}, f32[32,2048]{1,0:T(8,128)S(1)}, u32[]{:S(2)}, u32[]{:S(2)}) collective-permute-start(f32[32,2048]{1,0:T(8,128)S(1)} %get-tuple-element.69), channel_id=1, source_target_pairs={{0,2},{1,3},{2,0},{3,1},{4,6},{5,7},{6,4},{7,5},{8,10},{9,11},{10,... | collective-permute-start | bytes 786440 | tf_op jit(solution)/shard_map/ppermute | solution.py:50
  46.8 11.3 %collective-permute-start.12 = (f32[520,128]{1,0:T(8,128)S(1)}, f32[520,128]{1,0:T(8,128)S(1)}, u32[]{:S(2)}, u32[]{:S(2)}) collective-permute-start(f32[520,128]{1,0:T(8,128)S(1)} %get-tuple-element.56.refs_0_), channel_id=1, source_target_pairs={{0,24},{4,28},{8,16},{12,20},{16,8},{20,12},{24,0},{28,4},{1,25},{... | collective-permute-start | bytes 798728 | tf_op jit(solution)/shard_map/ppermute | solution.py:50
  48.4 23.5 %collective-permute-start.10 = (f32[520,128]{1,0:T(8,128)S(1)}, f32[520,128]{1,0:T(8,128)S(1)}, u32[]{:S(2)}, u32[]{:S(2)}) collective-permute-start(f32[520,128]{1,0:T(8,128)S(1)} %get-tuple-element.56.refs_0_), channel_id=1, source_target_pairs={{0,16},{4,20},{8,24},{12,28},{16,0},{20,4},{24,8},{28,12},{1,17},{... | collective-permute-start | bytes 798728 | tf_op jit(solution)/shard_map/ppermute | solution.py:50
  49.4 27.3 %collective-permute-start.9 = (f32[520,128]{1,0:T(8,128)S(1)}, f32[520,128]{1,0:T(8,128)S(1)}, u32[]{:S(2)}, u32[]{:S(2)}) collective-permute-start(f32[520,128]{1,0:T(8,128)S(1)} %get-tuple-element.56.refs_0_), channel_id=1, source_target_pairs={{0,12},{4,8},{8,4},{12,0},{16,28},{20,24},{24,20},{28,16},{1,13},{... | collective-permute-start | bytes 798728 | tf_op jit(solution)/shard_map/ppermute | solution.py:50
  51.0 25.7 %collective-permute-start.8 = (f32[520,128]{1,0:T(8,128)S(1)}, f32[520,128]{1,0:T(8,128)S(1)}, u32[]{:S(2)}, u32[]{:S(2)}) collective-permute-start(f32[520,128]{1,0:T(8,128)S(1)} %get-tuple-element.56.refs_0_), channel_id=1, source_target_pairs={{0,8},{4,12},{8,0},{12,4},{16,24},{20,28},{24,16},{28,20},{1,9},{5... | collective-permute-start | bytes 798728 | tf_op jit(solution)/shard_map/ppermute | solution.py:50
  51.6 20.3 %collective-permute-start.7 = (f32[520,128]{1,0:T(8,128)S(1)}, f32[520,128]{1,0:T(8,128)S(1)}, u32[]{:S(2)}, u32[]{:S(2)}) collective-permute-start(f32[520,128]{1,0:T(8,128)S(1)} %get-tuple-element.56.refs_0_), channel_id=1, source_target_pairs={{0,4},{4,0},{8,12},{12,8},{16,20},{20,16},{24,28},{28,24},{1,5},{5... | collective-permute-start | bytes 798728 | tf_op jit(solution)/shard_map/ppermute | solution.py:50
  58.0 18.7 %collective-permute-start.13 = (f32[520,128]{1,0:T(8,128)S(1)}, f32[520,128]{1,0:T(8,128)S(1)}, u32[]{:S(2)}, u32[]{:S(2)}) collective-permute-start(f32[520,128]{1,0:T(8,128)S(1)} %collective-permute-done.12.refs_6_), channel_id=1, source_target_pairs={{0,4},{4,0},{8,12},{12,8},{16,20},{20,16},{24,28},{28,24},{1,5},{5... | collective-permute-start | bytes 798728 | tf_op jit(solution)/shard_map/ppermute | solution.py:50
  71.9 6.7 %collective-permute-start.11 = (f32[520,128]{1,0:T(8,128)S(1)}, f32[520,128]{1,0:T(8,128)S(1)}, u32[]{:S(2)}, u32[]{:S(2)}) collective-permute-start(f32[520,128]{1,0:T(8,128)S(1)} %collective-permute-done.10.refs_4_), channel_id=1, source_target_pairs={{0,4},{4,0},{8,12},{12,8},{16,20},{20,16},{24,28},{28,24},{1,5},{5... | collective-permute-start | bytes 798728 | tf_op jit(solution)/shard_map/ppermute | solution.py:50
  95.9 3.7 %collective-permute-start.14 = (f32[8,128]{1,0:T(8,128)S(1)}, f32[8,128]{1,0:T(8,128)S(1)}, u32[]{:S(2)}, u32[]{:S(2)}) collective-permute-start(f32[8,128]{1,0:T(8,128)S(1)} %get-tuple-element.63), channel_id=1, source_target_pairs={{0,4},{4,0},{8,12},{12,8},{16,20},{20,16},{24,28},{28,24},{1,5},{5... | collective-permute-start | bytes 12296 | tf_op jit(solution)/shard_map/ppermute | solution.py:50
  99.6 3.6 %collective-permute-start.15 = (f32[8,128]{1,0:T(8,128)S(1)}, f32[8,128]{1,0:T(8,128)S(1)}, u32[]{:S(2)}, u32[]{:S(2)}) collective-permute-start(f32[8,128]{1,0:T(8,128)S(1)} %add.62), channel_id=1, source_target_pairs={{0,8},{4,12},{8,0},{12,4},{16,24},{20,28},{24,16},{28,20},{1,9},{5... | collective-permute-start | bytes 12296 | tf_op jit(solution)/shard_map/ppermute | solution.py:50
  103.2 4.5 %collective-permute-start.16 = (f32[8,128]{1,0:T(8,128)S(1)}, f32[8,128]{1,0:T(8,128)S(1)}, u32[]{:S(2)}, u32[]{:S(2)}) collective-permute-start(f32[8,128]{1,0:T(8,128)S(1)} %add.63), channel_id=1, source_target_pairs={{0,16},{4,20},{8,24},{12,28},{16,0},{20,4},{24,8},{28,12},{1,17},{... | collective-permute-start | bytes 12296 | tf_op jit(solution)/shard_map/ppermute | solution.py:50
  108.4 3.5 %collective-permute-start.19 = (f32[24,128]{1,0:T(8,128)S(1)}, f32[24,128]{1,0:T(8,128)S(1)}, u32[]{:S(2)}, u32[]{:S(2)}) collective-permute-start(f32[24,128]{1,0:T(8,128)S(1)} %get-tuple-element.66.refs_0_), channel_id=1, source_target_pairs={{0,3},{1,2},{2,1},{3,0},{4,7},{5,6},{6,5},{7,4},{8,11},{9,10},{10,... | collective-permute-start | bytes 36872 | tf_op jit(solution)/shard_map/ppermute | solution.py:50
  108.4 3.8 %collective-permute-start.18 = (f32[24,128]{1,0:T(8,128)S(1)}, f32[24,128]{1,0:T(8,128)S(1)}, u32[]{:S(2)}, u32[]{:S(2)}) collective-permute-start(f32[24,128]{1,0:T(8,128)S(1)} %get-tuple-element.66.refs_0_), channel_id=1, source_target_pairs={{0,2},{1,3},{2,0},{3,1},{4,6},{5,7},{6,4},{7,5},{8,10},{9,11},{10,... | collective-permute-start | bytes 36872 | tf_op jit(solution)/shard_map/ppermute | solution.py:50
  109.4 2.9 %collective-permute-start.17 = (f32[24,128]{1,0:T(8,128)S(1)}, f32[24,128]{1,0:T(8,128)S(1)}, u32[]{:S(2)}, u32[]{:S(2)}) collective-permute-start(f32[24,128]{1,0:T(8,128)S(1)} %get-tuple-element.66.refs_0_), channel_id=1, source_target_pairs={{0,1},{1,0},{2,3},{3,2},{4,5},{5,4},{6,7},{7,6},{8,9},{9,8},{10,11... | collective-permute-start | bytes 36872 | tf_op jit(solution)/shard_map/ppermute | solution.py:50
  (8 other events, 172.2 us)

commit v6 on v5

--- a/solution.py
+++ b/solution.py
@@ -285,9 +285,8 @@
 
     @pl.loop(0, groups)
     def _(group):
-        turned_over = first[...].T
+        finish(group, first[...].T)
         gather(jnp.minimum(group + 1, groups - 1), first)
-        finish(group, turned_over)
 
     across = jnp.broadcast_to(jnp.sum(total[...], axis=1, keepdims=True), (columns, 128))
     squares[...] = jnp.concatenate([across] * (128 // columns), axis=0).T[0:8]

time: 113 us -> 113 us (level); the launches traced: 113 us -> 112 us
  waiting for transfers between devices: 39.4 us -> 37.6 us
  starting transfers between devices: 22.7 us -> 24.4 us
    ppermute x18, waiting for transfers between devices: 36.2 us -> 34.5 us  [swap(): return lax.ppermute(value, axis, [(i, i ^ step) for i in range(size)])]
    ppermute x18, starting transfers between devices: 17 us -> 18.7 us  [swap(): return lax.ppermute(value, axis, [(i, i ^ step) for i in range(size)])]
  transfers between devices with their start and end apart: 20 -> 20, of which waited for: 11 -> 11; matrix products, arithmetic and copies ran while one was open for 4% -> 4% of each run, Pallas kernels for 19% -> 18%
where the time goes in v6:
time: 113 us; the launch traced here: 112 us
  Pallas kernels  42.3 us (37%)
  waiting for transfers between devices  37.6 us (33%)
  starting transfers between devices  24.4 us (22%)
  other arithmetic  6.11 us (5%)
    ppermute x18, waiting for transfers between devices, swap(): return lax.ppermute(value, axis, [(i, i ^ step) for i in range(size)])  34.5 us
    ppermute x18, starting transfers between devices, swap(): return lax.ppermute(value, axis, [(i, i ^ step) for i in range(size)])  18.7 us
    pallas_call x1, Pallas kernels, forward_lanes(): pl.pallas_call(functools.partial(forward_kernel, effects_all, lines), out...  17 us
    pallas_call x2, Pallas kernels, lane_blocks(): pl.pallas_call(functools.partial(lane_blocks_kernel, low_n, rows), out_sh...  9.91 us
    pallas_call x1, Pallas kernels, own_sums(): pl.pallas_call(functools.partial(own_sums_kernel, weeks), out_shape=[jax....  6.08 us
    ppermute x2, starting transfers between devices, on_device(): got.append(lax.ppermute(planes, ('ship', 'boot'), pairs))  5.68 us
    pallas_call x1, Pallas kernels, forward_base(): pl.pallas_call(base_kernel, out_shape=[shape, shape, jax.ShapeDtypeStruct...  4.64 us
    ppermute x2, waiting for transfers between devices, on_device(): got.append(lax.ppermute(planes, ('ship', 'boot'), pairs))  3.18 us
  transfers between devices with their start and end apart: 20, of which 11 were waited for; matrix products, arithmetic and copies ran while one was open for 4% of the time, Pallas kernels for 18%

profile of v6, /device:TPU:0, one launch (start us, length us, event | category | flops | bytes accessed | tf_op | source)
XLA Modules:
  0.0 111.7 jit_solution(13283474837555156004)
XLA Ops:
  0.6 1.9 %message.1 = (f32[424,128]{1,0:T(8,128)}, s32[144,8]{1,0:T(8,128)}, s32[1,128]{1,0:T(1,128)}) custom-call(f32[128,128]{1,0:T(8,128)} %bitcast.25, f32[128,128]{1,0:T(8,128)} %bitcast.28, f32[128,128]{1,0:T(8,128)} %bitcast.21, s32[128,128]{1,0:T(8,128)} %bitcast.35, s32[128,128]{1,0:T(8,128)} %bitcast.37, s32[1,128]{1,0:T(1,128)} %refs_5_.3, s32[32,128]{1,0:T(8,128)} %refs_5_.5), custom_call_target="tpu_custom_call" | custom-call | bytes 7200000 | tf_op jit(solution)/shard_map/message/pallas_call | solution.py:352
  2.5 4.1 %collective-permute-start.1 = (f32[424,128]{1,0:T(8,128)}, f32[424,128]{1,0:T(8,128)S(1)}, u32[]{:S(2)}, u32[]{:S(2)}) collective-permute-start(f32[424,128]{1,0:T(8,128)} %get-tuple-element.41), channel_id=1, source_target_pairs={{0,16},{1,24},{2,20},{3,28},{4,17},{5,25},{6,21},{7,29},{8,18},{9,... | collective-permute-start | bytes 651272 | tf_op jit(solution)/shard_map/ppermute | solution.py:651
  6.6 1.6 %collective-permute-start = (f32[424,128]{1,0:T(8,128)}, f32[424,128]{1,0:T(8,128)S(1)}, u32[]{:S(2)}, u32[]{:S(2)}) collective-permute-start(f32[424,128]{1,0:T(8,128)} %get-tuple-element.41), channel_id=1, source_target_pairs={{0,0},{1,8},{2,4},{3,12},{4,1},{5,9},{6,5},{7,13},{8,2},{9,10},{10... | collective-permute-start | bytes 651272 | tf_op jit(solution)/shard_map/ppermute | solution.py:651
  8.2 6.1 %own_sums.1 = (f32[32,128]{1,0:T(8,128)}, f32[96,128]{1,0:T(8,128)}) custom-call(s32[1,128]{1,0:T(1,128)} %get-tuple-element.38.firsts, f32[128,128]{1,0:T(8,128)} %bitcast.26, f32[128,128]{1,0:T(8,128)} %bitcast.29, f32[128,128]{1,0:T(8,128)} %bitcast.22, s32[128,128]{1,0:T(8,128)} %bitcast.31, s32[144,8]{1,0:T(8,128)} %get-tuple-element.39.refs_4_, ...), custom_call_target="tpu_custom_call" | custom-call | bytes 25200000 | tf_op jit(solution)/shard_map/own_sums/pallas_call | solution.py:472
  14.4 3.2 %collective-permute-done.1.planes = f32[424,128]{1,0:T(8,128)S(1)} collective-permute-done((f32[424,128]{1,0:T(8,128)}, f32[424,128]{1,0:T(8,128)S(1)}, u32[]{:S(2)}, u32[]{:S(2)}) %collective-permute-start.1) | collective-permute-done | bytes 217120 | tf_op jit(solution)/shard_map/ppermute | solution.py:651
  18.4 3.3 %collective-permute-start.2 = (f32[160,128]{1,0:T(8,128)S(1)}, f32[160,128]{1,0:T(8,128)S(1)}, u32[]{:S(2)}, u32[]{:S(2)}) collective-permute-start(f32[160,128]{1,0:T(8,128)S(1)} %pad_maximum_fusion.1), channel_id=1, source_target_pairs={{0,4},{4,0},{8,12},{12,8},{16,20},{20,16},{24,28},{28,24},{1,5},{5... | collective-permute-start | bytes 245768 | tf_op jit(solution)/shard_map/ppermute | solution.py:50
  21.7 5.6 %lane_blocks.2 = (f32[2,1088,128]{2,1,0:T(8,128)S(1)}, f32[8,256]{1,0:T(8,128)S(1)}) custom-call(s32[2]{0:T(128)S(1)} %pad_add_fusion.where, s32[1024]{0:T(1024)S(1)} %convert_bitcast_fusion.1.meta, f32[424,128]{1,0:T(8,128)S(1)} %collective-permute-done.planes), custom_call_target="tpu_custom_call" | custom-call | bytes 28800000 | tf_op jit(solution)/shard_map/lane_blocks/pallas_call | solution.py:138
  29.4 4.3 %lane_blocks.3 = (f32[2,1088,128]{2,1,0:T(8,128)S(1)}, f32[8,256]{1,0:T(8,128)S(1)}) custom-call(s32[2]{0:T(128)S(1)} %pad_add_fusion.where, s32[1024]{0:T(1024)S(1)} %convert_bitcast_fusion.meta, f32[424,128]{1,0:T(8,128)S(1)} %collective-permute-done.1.planes), custom_call_target="tpu_custom_call" | custom-call | bytes 28800000 | tf_op jit(solution)/shard_map/lane_blocks/pallas_call | solution.py:138
  35.4 1.6 %collective-permute-done.4 = f32[64,2048]{1,0:T(8,128)S(1)} collective-permute-done((f32[64,2048]{1,0:T(8,128)S(1)}, f32[64,2048]{1,0:T(8,128)S(1)}, u32[]{:S(2)}, u32[]{:S(2)}) %collective-permute-start.4) | collective-permute-done | bytes 524320 | tf_op jit(solution)/shard_map/ppermute | solution.py:50
  37.1 1.5 %collective-permute-start.5 = (f32[32,2048]{1,0:T(8,128)S(1)}, f32[32,2048]{1,0:T(8,128)S(1)}, u32[]{:S(2)}, u32[]{:S(2)}) collective-permute-start(f32[32,2048]{1,0:T(8,128)S(1)} %get-tuple-element.69), channel_id=1, source_target_pairs={{0,2},{1,3},{2,0},{3,1},{4,6},{5,7},{6,4},{7,5},{8,10},{9,11},{10,... | collective-permute-start | bytes 786440 | tf_op jit(solution)/shard_map/ppermute | solution.py:50
  38.6 2.8 %collective-permute-done.6 = f32[96,128]{1,0:T(8,128)S(1)} collective-permute-done((f32[96,128]{1,0:T(8,128)S(1)}, f32[96,128]{1,0:T(8,128)S(1)}, u32[]{:S(2)}, u32[]{:S(2)}) %collective-permute-start.6) | collective-permute-done | bytes 49184 | tf_op jit(solution)/shard_map/ppermute | solution.py:50
  41.4 4.0 %collective-permute-done.5.refs_2_ = f32[32,2048]{1,0:T(8,128)S(1)} collective-permute-done((f32[32,2048]{1,0:T(8,128)S(1)}, f32[32,2048]{1,0:T(8,128)S(1)}, u32[]{:S(2)}, u32[]{:S(2)}) %collective-permute-start.5) | collective-permute-done | bytes 262176 | tf_op jit(solution)/shard_map/ppermute | solution.py:50
  45.7 1.7 %collective-permute-start.12 = (f32[520,128]{1,0:T(8,128)S(1)}, f32[520,128]{1,0:T(8,128)S(1)}, u32[]{:S(2)}, u32[]{:S(2)}) collective-permute-start(f32[520,128]{1,0:T(8,128)S(1)} %get-tuple-element.56.refs_0_), channel_id=1, source_target_pairs={{0,24},{4,28},{8,16},{12,20},{16,8},{20,12},{24,0},{28,4},{1,25},{... | collective-permute-start | bytes 798728 | tf_op jit(solution)/shard_map/ppermute | solution.py:50
  48.4 1.8 %collective-permute-start.9 = (f32[520,128]{1,0:T(8,128)S(1)}, f32[520,128]{1,0:T(8,128)S(1)}, u32[]{:S(2)}, u32[]{:S(2)}) collective-permute-start(f32[520,128]{1,0:T(8,128)S(1)} %get-tuple-element.56.refs_0_), channel_id=1, source_target_pairs={{0,12},{4,8},{8,4},{12,0},{16,28},{20,24},{24,20},{28,16},{1,13},{... | collective-permute-start | bytes 798728 | tf_op jit(solution)/shard_map/ppermute | solution.py:50
  52.0 5.0 %collective-permute-done.12.refs_6_ = f32[520,128]{1,0:T(8,128)S(1)} collective-permute-done((f32[520,128]{1,0:T(8,128)S(1)}, f32[520,128]{1,0:T(8,128)S(1)}, u32[]{:S(2)}, u32[]{:S(2)}) %collective-permute-start.12) | collective-permute-done | bytes 266272 | tf_op jit(solution)/shard_map/ppermute | solution.py:50
  57.2 13.7 %collective-permute-done.10.refs_4_ = f32[520,128]{1,0:T(8,128)S(1)} collective-permute-done((f32[520,128]{1,0:T(8,128)S(1)}, f32[520,128]{1,0:T(8,128)S(1)}, u32[]{:S(2)}, u32[]{:S(2)}) %collective-permute-start.10) | collective-permute-done | bytes 266272 | tf_op jit(solution)/shard_map/ppermute | solution.py:50
  71.1 4.6 %forward_base.1 = (f32[32,16384]{1,0:T(8,128)S(1)}, f32[32,16384]{1,0:T(8,128)S(1)}, f32[8,128]{1,0:T(8,128)S(1)}) custom-call(f32[128,128]{1,0:T(8,128)S(1)} %bitcast.27, f32[128,128]{1,0:T(8,128)S(1)} %bitcast.30, f32[128,128]{1,0:T(8,128)S(1)} %bitcast.23, s32[128,128]{1,0:T(8,128)S(1)} %bitcast.32, s32[144,8]{1,0:T(8,128)S(1)} %copy-done.3, ...), custom_call_target="tpu_custom_call" | custom-call | bytes 28800000 | tf_op jit(solution)/shard_map/forward_base/pallas_call | solution.py:525
  75.8 1.8 %collective-permute-done.11.refs_5_ = f32[520,128]{1,0:T(8,128)S(1)} collective-permute-done((f32[520,128]{1,0:T(8,128)S(1)}, f32[520,128]{1,0:T(8,128)S(1)}, u32[]{:S(2)}, u32[]{:S(2)}) %collective-permute-start.11) | collective-permute-done | bytes 266272 | tf_op jit(solution)/shard_map/ppermute | solution.py:50
  77.6 17.0 %forward_lanes.1 = (f32[32,16384]{1,0:T(8,128)S(1)}, f32[8,128]{1,0:T(8,128)S(1)}, f32[32,1]{1,0:T(8,128)S(1)}) custom-call(s32[16384]{0:T(1024)S(1)} %get-tuple-element.72.index, f32[8,128]{1,0:T(8,128)S(1)} %get-tuple-element.57.before, f32[32,1]{1,0:T(8,128)S(1)} %get-tuple-element.78.by_beta, f32[32,1]{1,0:T(8,128)S(1)} %get-tuple-element.77.week_square, ...), custom_call_target="tpu_custom_call" | custom-call | bytes 64800000 | tf_op jit(solution)/shard_map/forward_lanes/pallas_call | solution.py:298
  96.0 2.5 %collective-permute-done.14 = f32[8,128]{1,0:T(8,128)S(1)} collective-permute-done((f32[8,128]{1,0:T(8,128)S(1)}, f32[8,128]{1,0:T(8,128)S(1)}, u32[]{:S(2)}, u32[]{:S(2)}) %collective-permute-start.14) | collective-permute-done | bytes 4128 | tf_op jit(solution)/shard_map/ppermute | solution.py:50
  98.5 1.9 %collective-permute-start.15 = (f32[8,128]{1,0:T(8,128)S(1)}, f32[8,128]{1,0:T(8,128)S(1)}, u32[]{:S(2)}, u32[]{:S(2)}) collective-permute-start(f32[8,128]{1,0:T(8,128)S(1)} %add.62), channel_id=1, source_target_pairs={{0,8},{4,12},{8,0},{12,4},{16,24},{20,28},{24,16},{28,20},{1,9},{5... | collective-permute-start | bytes 12296 | tf_op jit(solution)/shard_map/ppermute | solution.py:50
  102.1 2.1 %collective-permute-start.16 = (f32[8,128]{1,0:T(8,128)S(1)}, f32[8,128]{1,0:T(8,128)S(1)}, u32[]{:S(2)}, u32[]{:S(2)}) collective-permute-start(f32[8,128]{1,0:T(8,128)S(1)} %add.63), channel_id=1, source_target_pairs={{0,16},{4,20},{8,24},{12,28},{16,0},{20,4},{24,8},{28,12},{1,17},{... | collective-permute-start | bytes 12296 | tf_op jit(solution)/shard_map/ppermute | solution.py:50
  104.9 1.7 %collective-permute-done.16 = f32[8,128]{1,0:T(8,128)S(1)} collective-permute-done((f32[8,128]{1,0:T(8,128)S(1)}, f32[8,128]{1,0:T(8,128)S(1)}, u32[]{:S(2)}, u32[]{:S(2)}) %collective-permute-start.16) | collective-permute-done | bytes 4128 | tf_op jit(solution)/shard_map/ppermute | solution.py:50
  109.3 1.5 %broadcast_multiply_fusion = f32[32,16384]{1,0:T(8,128)} fusion(f32[32,16384]{1,0:T(8,128)S(1)} %get-tuple-element.62, f32[32]{0:T(128)S(1)} %reduce.1), kind=kLoop, calls=%fused_computation | loop fusion | flops 524288 | bytes 4194432 | tf_op jit(solution)/shard_map/mul | solution.py:716
  (84 shorter events, 15.4 us)
Async XLA Ops:
  2.5 15.0 %collective-permute-start.1 = (f32[424,128]{1,0:T(8,128)}, f32[424,128]{1,0:T(8,128)S(1)}, u32[]{:S(2)}, u32[]{:S(2)}) collective-permute-start(f32[424,128]{1,0:T(8,128)} %get-tuple-element.41), channel_id=1, source_target_pairs={{0,16},{1,24},{2,20},{3,28},{4,17},{5,25},{6,21},{7,29},{8,18},{9,... | collective-permute-start | bytes 651272 | tf_op jit(solution)/shard_map/ppermute | solution.py:651
  6.6 10.9 %collective-permute-start = (f32[424,128]{1,0:T(8,128)}, f32[424,128]{1,0:T(8,128)S(1)}, u32[]{:S(2)}, u32[]{:S(2)}) collective-permute-start(f32[424,128]{1,0:T(8,128)} %get-tuple-element.41), channel_id=1, source_target_pairs={{0,0},{1,8},{2,4},{3,12},{4,1},{5,9},{6,5},{7,13},{8,2},{9,10},{10... | collective-permute-start | bytes 651272 | tf_op jit(solution)/shard_map/ppermute | solution.py:651
  18.4 8.9 %collective-permute-start.2 = (f32[160,128]{1,0:T(8,128)S(1)}, f32[160,128]{1,0:T(8,128)S(1)}, u32[]{:S(2)}, u32[]{:S(2)}) collective-permute-start(f32[160,128]{1,0:T(8,128)S(1)} %pad_maximum_fusion.1), channel_id=1, source_target_pairs={{0,4},{4,0},{8,12},{12,8},{16,20},{20,16},{24,28},{28,24},{1,5},{5... | collective-permute-start | bytes 245768 | tf_op jit(solution)/shard_map/ppermute | solution.py:50
  28.1 5.6 %collective-permute-start.3 = (f32[224,128]{1,0:T(8,128)S(1)}, f32[224,128]{1,0:T(8,128)S(1)}, u32[]{:S(2)}, u32[]{:S(2)}) collective-permute-start(f32[224,128]{1,0:T(8,128)S(1)} %pad_maximum_fusion), channel_id=1, source_target_pairs={{0,8},{4,12},{8,0},{12,4},{16,24},{20,28},{24,16},{28,20},{1,9},{5... | collective-permute-start | bytes 344072 | tf_op jit(solution)/shard_map/ppermute | solution.py:50
  34.9 36.1 %copy-start = (f32[16384]{0:T(1024)S(1)}, f32[16384]{0:T(1024)}, u32[]{:S(2)}) copy-start(f32[16384]{0:T(1024)} %param.13) | copy-start | bytes 196612
  35.0 36.1 %copy-start.1 = (f32[16384]{0:T(1024)S(1)}, f32[16384]{0:T(1024)}, u32[]{:S(2)}) copy-start(f32[16384]{0:T(1024)} %param.11) | copy-start | bytes 196612
  35.0 36.1 %copy-start.2 = (f32[16384]{0:T(1024)S(1)}, f32[16384]{0:T(1024)}, u32[]{:S(2)}) copy-start(f32[16384]{0:T(1024)} %param.12) | copy-start | bytes 196612
  35.0 36.1 %copy-start.3 = (s32[144,8]{1,0:T(8,128)S(1)}, s32[144,8]{1,0:T(8,128)}, u32[]{:S(2)}) copy-start(s32[144,8]{1,0:T(8,128)} %get-tuple-element.39.refs_4_) | copy-start | bytes 13828
  35.0 2.0 %collective-permute-start.4 = (f32[64,2048]{1,0:T(8,128)S(1)}, f32[64,2048]{1,0:T(8,128)S(1)}, u32[]{:S(2)}, u32[]{:S(2)}) collective-permute-start(f32[64,2048]{1,0:T(8,128)S(1)} %get-tuple-element.53), channel_id=1, source_target_pairs={{0,1},{1,0},{2,3},{3,2},{4,5},{5,4},{6,7},{7,6},{8,9},{9,8},{10,11... | collective-permute-start | bytes 1572872 | tf_op jit(solution)/shard_map/ppermute | solution.py:50
  35.3 6.1 %collective-permute-start.6 = (f32[96,128]{1,0:T(8,128)S(1)}, f32[96,128]{1,0:T(8,128)S(1)}, u32[]{:S(2)}, u32[]{:S(2)}) collective-permute-start(f32[96,128]{1,0:T(8,128)S(1)} %slice_add_fusion.1), channel_id=1, source_target_pairs={{0,16},{4,20},{8,24},{12,28},{16,0},{20,4},{24,8},{28,12},{1,17},{... | collective-permute-start | bytes 147464 | tf_op jit(solution)/shard_map/ppermute | solution.py:50
  37.1 8.4 %collective-permute-start.5 = (f32[32,2048]{1,0:T(8,128)S(1)}, f32[32,2048]{1,0:T(8,128)S(1)}, u32[]{:S(2)}, u32[]{:S(2)}) collective-permute-start(f32[32,2048]{1,0:T(8,128)S(1)} %get-tuple-element.69), channel_id=1, source_target_pairs={{0,2},{1,3},{2,0},{3,1},{4,6},{5,7},{6,4},{7,5},{8,10},{9,11},{10,... | collective-permute-start | bytes 786440 | tf_op jit(solution)/shard_map/ppermute | solution.py:50
  45.7 11.3 %collective-permute-start.12 = (f32[520,128]{1,0:T(8,128)S(1)}, f32[520,128]{1,0:T(8,128)S(1)}, u32[]{:S(2)}, u32[]{:S(2)}) collective-permute-start(f32[520,128]{1,0:T(8,128)S(1)} %get-tuple-element.56.refs_0_), channel_id=1, source_target_pairs={{0,24},{4,28},{8,16},{12,20},{16,8},{20,12},{24,0},{28,4},{1,25},{... | collective-permute-start | bytes 798728 | tf_op jit(solution)/shard_map/ppermute | solution.py:50
  47.4 23.5 %collective-permute-start.10 = (f32[520,128]{1,0:T(8,128)S(1)}, f32[520,128]{1,0:T(8,128)S(1)}, u32[]{:S(2)}, u32[]{:S(2)}) collective-permute-start(f32[520,128]{1,0:T(8,128)S(1)} %get-tuple-element.56.refs_0_), channel_id=1, source_target_pairs={{0,16},{4,20},{8,24},{12,28},{16,0},{20,4},{24,8},{28,12},{1,17},{... | collective-permute-start | bytes 798728 | tf_op jit(solution)/shard_map/ppermute | solution.py:50
  48.4 27.4 %collective-permute-start.9 = (f32[520,128]{1,0:T(8,128)S(1)}, f32[520,128]{1,0:T(8,128)S(1)}, u32[]{:S(2)}, u32[]{:S(2)}) collective-permute-start(f32[520,128]{1,0:T(8,128)S(1)} %get-tuple-element.56.refs_0_), channel_id=1, source_target_pairs={{0,12},{4,8},{8,4},{12,0},{16,28},{20,24},{24,20},{28,16},{1,13},{... | collective-permute-start | bytes 798728 | tf_op jit(solution)/shard_map/ppermute | solution.py:50
  50.2 25.6 %collective-permute-start.8 = (f32[520,128]{1,0:T(8,128)S(1)}, f32[520,128]{1,0:T(8,128)S(1)}, u32[]{:S(2)}, u32[]{:S(2)}) collective-permute-start(f32[520,128]{1,0:T(8,128)S(1)} %get-tuple-element.56.refs_0_), channel_id=1, source_target_pairs={{0,8},{4,12},{8,0},{12,4},{16,24},{20,28},{24,16},{28,20},{1,9},{5... | collective-permute-start | bytes 798728 | tf_op jit(solution)/shard_map/ppermute | solution.py:50
  50.6 20.4 %collective-permute-start.7 = (f32[520,128]{1,0:T(8,128)S(1)}, f32[520,128]{1,0:T(8,128)S(1)}, u32[]{:S(2)}, u32[]{:S(2)}) collective-permute-start(f32[520,128]{1,0:T(8,128)S(1)} %get-tuple-element.56.refs_0_), channel_id=1, source_target_pairs={{0,4},{4,0},{8,12},{12,8},{16,20},{20,16},{24,28},{28,24},{1,5},{5... | collective-permute-start | bytes 798728 | tf_op jit(solution)/shard_map/ppermute | solution.py:50
  57.0 18.8 %collective-permute-start.13 = (f32[520,128]{1,0:T(8,128)S(1)}, f32[520,128]{1,0:T(8,128)S(1)}, u32[]{:S(2)}, u32[]{:S(2)}) collective-permute-start(f32[520,128]{1,0:T(8,128)S(1)} %collective-permute-done.12.refs_6_), channel_id=1, source_target_pairs={{0,4},{4,0},{8,12},{12,8},{16,20},{20,16},{24,28},{28,24},{1,5},{5... | collective-permute-start | bytes 798728 | tf_op jit(solution)/shard_map/ppermute | solution.py:50
  70.9 6.7 %collective-permute-start.11 = (f32[520,128]{1,0:T(8,128)S(1)}, f32[520,128]{1,0:T(8,128)S(1)}, u32[]{:S(2)}, u32[]{:S(2)}) collective-permute-start(f32[520,128]{1,0:T(8,128)S(1)} %collective-permute-done.10.refs_4_), channel_id=1, source_target_pairs={{0,4},{4,0},{8,12},{12,8},{16,20},{20,16},{24,28},{28,24},{1,5},{5... | collective-permute-start | bytes 798728 | tf_op jit(solution)/shard_map/ppermute | solution.py:50
  94.8 3.7 %collective-permute-start.14 = (f32[8,128]{1,0:T(8,128)S(1)}, f32[8,128]{1,0:T(8,128)S(1)}, u32[]{:S(2)}, u32[]{:S(2)}) collective-permute-start(f32[8,128]{1,0:T(8,128)S(1)} %get-tuple-element.63), channel_id=1, source_target_pairs={{0,4},{4,0},{8,12},{12,8},{16,20},{20,16},{24,28},{28,24},{1,5},{5... | collective-permute-start | bytes 12296 | tf_op jit(solution)/shard_map/ppermute | solution.py:50
  98.5 3.6 %collective-permute-start.15 = (f32[8,128]{1,0:T(8,128)S(1)}, f32[8,128]{1,0:T(8,128)S(1)}, u32[]{:S(2)}, u32[]{:S(2)}) collective-permute-start(f32[8,128]{1,0:T(8,128)S(1)} %add.62), channel_id=1, source_target_pairs={{0,8},{4,12},{8,0},{12,4},{16,24},{20,28},{24,16},{28,20},{1,9},{5... | collective-permute-start | bytes 12296 | tf_op jit(solution)/shard_map/ppermute | solution.py:50
  102.1 4.5 %collective-permute-start.16 = (f32[8,128]{1,0:T(8,128)S(1)}, f32[8,128]{1,0:T(8,128)S(1)}, u32[]{:S(2)}, u32[]{:S(2)}) collective-permute-start(f32[8,128]{1,0:T(8,128)S(1)} %add.63), channel_id=1, source_target_pairs={{0,16},{4,20},{8,24},{12,28},{16,0},{20,4},{24,8},{28,12},{1,17},{... | collective-permute-start | bytes 12296 | tf_op jit(solution)/shard_map/ppermute | solution.py:50
  107.4 3.5 %collective-permute-start.19 = (f32[24,128]{1,0:T(8,128)S(1)}, f32[24,128]{1,0:T(8,128)S(1)}, u32[]{:S(2)}, u32[]{:S(2)}) collective-permute-start(f32[24,128]{1,0:T(8,128)S(1)} %get-tuple-element.66.refs_0_), channel_id=1, source_target_pairs={{0,3},{1,2},{2,1},{3,0},{4,7},{5,6},{6,5},{7,4},{8,11},{9,10},{10,... | collective-permute-start | bytes 36872 | tf_op jit(solution)/shard_map/ppermute | solution.py:50
  107.4 3.7 %collective-permute-start.18 = (f32[24,128]{1,0:T(8,128)S(1)}, f32[24,128]{1,0:T(8,128)S(1)}, u32[]{:S(2)}, u32[]{:S(2)}) collective-permute-start(f32[24,128]{1,0:T(8,128)S(1)} %get-tuple-element.66.refs_0_), channel_id=1, source_target_pairs={{0,2},{1,3},{2,0},{3,1},{4,6},{5,7},{6,4},{7,5},{8,10},{9,11},{10,... | collective-permute-start | bytes 36872 | tf_op jit(solution)/shard_map/ppermute | solution.py:50
  108.6 2.5 %collective-permute-start.17 = (f32[24,128]{1,0:T(8,128)S(1)}, f32[24,128]{1,0:T(8,128)S(1)}, u32[]{:S(2)}, u32[]{:S(2)}) collective-permute-start(f32[24,128]{1,0:T(8,128)S(1)} %get-tuple-element.66.refs_0_), channel_id=1, source_target_pairs={{0,1},{1,0},{2,3},{3,2},{4,5},{5,4},{6,7},{7,6},{8,9},{9,8},{10,11... | collective-permute-start | bytes 36872 | tf_op jit(solution)/shard_map/ppermute | solution.py:50
  (8 other events, 171.7 us)
